TPU v7x, 256 devices: a whole 4x4x8 slice. The times are simulated.
256 devices in a mesh: grp: 8 (over y, core), dev: 32 (over z, x).
Axes of the slice: x: 4, y: 4, z: 8, core: 2. Of those that a mesh axis runs over, the one named last changes fastest.
Arguments:
- segments: float32 [9, 524288], P(None, ('grp', 'dev')), may hold values from -6 to 6
- pair_blocks: int32 [8192, 2], P(('grp', 'dev')), may hold values from -1 to 511, as said below
- block_cells: int32 [4096], P(('grp', 'dev')), may hold values from 0 to 255, as said below
- mobility: float32 [524288], P(('grp', 'dev')), may hold values from 0.5 to 3
- cell_centers: float32 [3, 256], replicated, may hold values from -2 to 2
Outputs:
- forces: float32 [3, 524288], P(None, ('grp', 'dev'))
- displacement: float32 [3, 524288], P(None, ('grp', 'dev'))
Inputs may be any that keep to these rules, and one draw needn't show every extreme that they name: `pair_blocks`: A device's 32 slots list its valid pairs first, each of two different group-local blocks, and then rows of -1 in both columns; every device has one valid pair or more, and in each group one device's slots are all valid. `block_cells`: block k lies in a cell of its own group: from (k // 512) * 32 to (k // 512 + 1) * 32 - 1.
All inputs are finite; a program needn't handle non-finite values.
Results may differ from a plain program's by a relative error of at most 0.0003.
Values sent between devices are 32-bit elements; how exact they have to be, the bound alone decides.
No kernel may reach another device: no remote copies, remote signals or barrier semaphores. Data moves between devices by JAX's collectives and lax.ppermute only.
A program may use at most 128 MiB of HBM per device.

v0:
```python
import jax
import jax.numpy as jnp
from jax import lax
from jax.sharding import PartitionSpec as P

NEAR_CORE = 0.25
FAR_CORE = 1.0
STEP_LIMIT = 0.5


def pair_weights(first, second, core):
    offset = first[0:3, :, None] - second[0:3, None, :]
    dist_sq = jnp.sum(offset * offset, axis=0) + core
    high = lax.Precision.HIGHEST
    burgers = jnp.dot(first[6:9].T, second[6:9], precision=high)
    lines = jnp.dot(first[3:6].T, second[3:6], precision=high)
    cross_one = jnp.dot(first[6:9].T, second[3:6], precision=high)
    cross_two = jnp.dot(first[3:6].T, second[6:9], precision=high)
    coupling = burgers * lines + 0.5 * cross_one * cross_two
    return (coupling / (dist_sq * jnp.sqrt(dist_sq)), offset)


def pair_forces(first, second):
    weights, offset = pair_weights(first, second, NEAR_CORE)
    pulled = weights[None] * offset
    return (jnp.sum(pulled, axis=2), -jnp.sum(pulled, axis=1))


def self_force(block):
    return pair_forces(block, block)[0]


def add_pair(buffer, blocks, pair_row):
    first = pair_row[0]
    second = pair_row[1]
    usable = (first >= 0).astype(buffer.dtype)
    first_c = jnp.maximum(first, 0)
    second_c = jnp.maximum(second, 0)
    zero = jnp.zeros((), jnp.int32)
    length = blocks.shape[2]
    seg_one = lax.dynamic_slice(blocks, (zero, first_c, zero), (9, 1, length))[:, 0, :]
    seg_two = lax.dynamic_slice(blocks, (zero, second_c, zero), (9, 1, length))[:, 0, :]
    force_one, force_two = pair_forces(seg_one, seg_two)
    old_one = lax.dynamic_slice(buffer, (zero, first_c, zero), (3, 1, length))
    buffer = lax.dynamic_update_slice(
        buffer, old_one + usable * force_one[:, None, :], (zero, first_c, zero)
    )
    old_two = lax.dynamic_slice(buffer, (zero, second_c, zero), (3, 1, length))
    buffer = lax.dynamic_update_slice(
        buffer, old_two + usable * force_two[:, None, :], (zero, second_c, zero)
    )
    return buffer


def block_outer(block):
    return (block[6:9, None, :] * block[3:6][None, :, :]).reshape(9, block.shape[1])


def cell_moments(segs, cells, cell_count):
    block_count = cells.shape[0]
    outer = (segs[6:9, None, :] * segs[3:6][None, :, :]).reshape(
        9, block_count, segs.shape[1] // block_count
    )
    per_block = jnp.sum(outer, axis=2)
    onehot = (cells[:, None] == lax.iota(jnp.int32, cell_count)[None, :]).astype(segs.dtype)
    return jnp.dot(per_block, onehot, precision=lax.Precision.HIGHEST)


def far_force(block, cell, moments, centers):
    coupling = jnp.dot(block_outer(block).T, moments, precision=lax.Precision.HIGHEST)
    offset = block[0:3, :, None] - centers[:, None, :]
    dist_sq = jnp.sum(offset * offset, axis=0) + FAR_CORE
    keep = (lax.iota(jnp.int32, centers.shape[1]) != cell).astype(block.dtype)
    weights = coupling * keep[None, :] / (dist_sq * jnp.sqrt(dist_sq))
    return jnp.sum(weights[None] * offset, axis=2)


def body(segments, pair_blocks, block_cells, mobility, cell_centers):
    block_count = block_cells.shape[0]
    seg_count = segments.shape[1]
    block_len = seg_count // block_count
    dev_count = lax.axis_size("dev")
    gathered = lax.all_gather(segments, "dev", axis=1, tiled=True)
    blocks = gathered.reshape(9, dev_count * block_count, block_len)
    buffer = jnp.zeros((3, dev_count * block_count, block_len), jnp.float32)
    my_valid = jnp.sum((pair_blocks[:, 0] >= 0).astype(jnp.int32))

    def listed_step(turn, carry):
        pair_row = lax.dynamic_slice(pair_blocks, (turn, jnp.zeros((), jnp.int32)), (1, 2))[0]
        return add_pair(carry, blocks, pair_row)

    buffer = lax.fori_loop(jnp.zeros((), jnp.int32), my_valid, listed_step, buffer)
    near = lax.psum_scatter(
        buffer.reshape(3, dev_count * seg_count), "dev", scatter_dimension=1, tiled=True
    )
    by_block = jnp.moveaxis(segments.reshape(9, block_count, block_len), 1, 0)
    own = jnp.moveaxis(lax.map(self_force, by_block), 0, 1).reshape(3, seg_count)
    cell_count = cell_centers.shape[1]
    local_moments = cell_moments(segments, block_cells, cell_count)
    moments = lax.psum(local_moments, ("grp", "dev"))

    def far_one(item):
        return far_force(item[0], item[1], moments, cell_centers)

    far = jnp.moveaxis(lax.map(far_one, (by_block, block_cells)), 0, 1).reshape(3, seg_count)
    forces = near + own + far
    velocity = mobility[None, :] * forces
    local_fastest = jnp.max(jnp.sqrt(jnp.sum(velocity * velocity, axis=0)))
    fastest = lax.pmax(local_fastest, ("grp", "dev"))
    return (forces, STEP_LIMIT / (fastest + 1e-06) * velocity)


def solution(mesh):
    in_specs = (
        P(None, ("grp", "dev")),
        P(("grp", "dev"), None),
        P(("grp", "dev")),
        P(("grp", "dev")),
        P(),
    )
    out_specs = (P(None, ("grp", "dev")), P(None, ("grp", "dev")))
    return jax.shard_map(body, mesh=mesh, in_specs=in_specs, out_specs=out_specs, check_vma=False)
```

profile of v0, /device:TPU:1, one launch (start us, length us, event | category | flops | bytes accessed | tf_op | source)
XLA Modules:
  0.0 806.1 jit_solution(4079883501339572306)
XLA Ops:
  7.2 0.7 all-gather.2.cloned.1.call-update
  8.0 0.9 copy.37
  9.0 26.0 %while.31 = (s32[]{:T(128)}, f32[16,3,128]{2,1,0:T(4,128)S(1)}, f32[16,9,128]{2,1,0:T(8,128)S(1)}, s32[]{:T(128)}, s32[]{:T(128)}, /*index=5*/s32[]{}, s32[]{}) while((s32[]{:T(128)}, f32[16,3,128]{2,1,0:T(4,128)S(1)}, f32[16,9,128]{2,1,0:T(8,128)S(1)}, s32[]{:T(128)}, s32[]{:T(128)}, /*index=5*/s32[]{}, s32[]{}) %tuple.78), condition=%wide.region_10.11_spmd, body=%wide.region_7.10_spmd.sunk | while | flops 2752132 | bytes 683653 | solution.py:97
  35.4 82.0 %psum.7 = f32[9,256]{1,0:T(8,128)S(1)} all-reduce(f32[9,256]{1,0:T(8,128)S(1)} %fusion.30), channel_id=1, replica_groups=mesh['grp'=8,'dev'=32] {'grp','dev'}, use_global_device_ids=true, to_apply=%region_12.13 | all-reduce | flops 2304 | bytes 18432 | tf_op jit(solution)/shard_map/psum | solution.py:100
  118.0 3.0 copy.36
  121.2 3.4 copy.28
  124.7 9.0 %while.30 = (s32[]{:T(128)}, f32[3,512,128]{2,0,1:T(4,128)S(1)}, s32[]{:T(128)}, s32[32,2]{0,1:T(2,128)S(1)}, f32[9,512,128]{2,0,1:T(8,128)}, /*index=5*/s32[]{:...) while((s32[]{:T(128)}, f32[3,512,128]{2,0,1:T(4,128)S(1)}, s32[]{:T(128)}, ...), condition=%wide.region_5.0_spmd, body=%wide.region_1.0_spmd.sunk | while | flops 2802827 | bytes 705825 | solution.py:92
  128.0 0.7 fusion.71
  128.8 1.0 convolution_multiply_fusion.12
  129.8 1.0 fusion.70
  130.9 1.0 convolution_multiply_fusion.11
  131.9 1.0 fusion.73
  133.8 16.1 %copy.34 = f32[3,65536]{0,1:T(8,128)} copy(f32[3,65536]{1,0:T(4,128)S(1)} %bitcast.132) | data formatting | bytes 1572864
  150.5 32.1 %while.32 = (s32[]{:T(128)}, f32[16,3,128]{2,1,0:T(4,128)S(1)}, f32[16,9,128]{2,1,0:T(8,128)S(1)}, f32[9,256]{1,0:T(8,128)S(1)}, s32[16]{0:T(128)S(1)}, /*index=...) while((s32[]{:T(128)}, f32[16,3,128]{2,1,0:T(4,128)S(1)}, f32[16,9,128]{2,1,0:T(8,128)S(1)}, ...), condition=%wide.region_16.17_spmd, body=%wide.region_13.16_spmd.sunk | while | flops 4228356 | bytes 581285 | solution.py:105
  151.1 0.6 compare_convert_fusion.3
  153.1 0.6 compare_convert_fusion.3
  155.1 0.6 compare_convert_fusion.3
  157.1 0.6 compare_convert_fusion.3
  159.1 0.6 compare_convert_fusion.3
  161.1 0.6 compare_convert_fusion.3
  163.1 0.6 compare_convert_fusion.3
  182.6 536.3 %reduce-scatter.4.cloned.1.call-done = f32[2048,3]{1,0:T(8,128)} async-done(((f32[65536,3]{1,0:T(8,128)}), f32[2048,3]{1,0:T(8,128)}) %reduce-scatter.4.cloned.1.call-update) | async-done | bytes 24592
  719.0 1.6 copy.35
  721.2 76.7 %pmax.7 = f32[]{:T(128)} all-reduce(f32[]{:T(128)} %sqrt_reduce_fusion), channel_id=1, replica_groups=mesh['grp'=8,'dev'=32] {'grp','dev'}, use_global_device_ids=true, to_apply=%region_19.20 | all-reduce | flops 1 | bytes 8 | tf_op jit(solution)/shard_map/pmax | solution.py:109
  (302 shorter events, 56.1 us)
Async XLA Ops:
  7.2 27.8 %copy-start = (f32[9,2048]{1,0:T(8,128)S(1)}, f32[9,2048]{1,0:T(8,128)}, u32[]{:S(2)}) copy-start(f32[9,2048]{1,0:T(8,128)} %param.11) | copy-start | bytes 221188
  7.2 28.0 %copy-start.5 = (s32[16]{0:T(128)S(1)}, s32[16]{0:T(128)}, u32[]{:S(2)}) copy-start(s32[16]{0:T(128)} %param.13) | copy-start | bytes 196
  7.2 110.2 %copy-start.4 = (s32[32,2]{0,1:T(2,128)S(1)}, s32[32,2]{0,1:T(2,128)}, u32[]{:S(2)}) copy-start(s32[32,2]{0,1:T(2,128)} %param.12) | copy-start | bytes 772
  7.2 110.8 %all-gather.2.cloned.1.call-start = ((), (), s32[]{:S(2)}) async-start(), calls=%async_computation.1 | async-start | bytes 4325376 | tf_op jit(solution)/shard_map/all_gather | solution.py:83
  7.9 711.0 %reduce-scatter.4.cloned.1.call-start = ((), (), s32[]{:S(2)}) async-start(), calls=%async_computation.2 | async-start | bytes 34603008
  149.8 0.7 copy-start.1
  149.9 570.7 %copy-start.3 = (f32[2048]{0:T(1024)S(1)}, f32[2048]{0:T(1024)}, u32[]{:S(2)}) copy-start(f32[2048]{0:T(1024)} %param.14) | copy-start | bytes 24580
  720.6 78.6 %copy-start.2 = (f32[3,2048]{1,0:T(4,128)}, f32[3,2048]{1,0:T(4,128)S(1)}, u32[]{:S(2)}) copy-start(f32[3,2048]{1,0:T(4,128)S(1)} %get-tuple-element.154) | copy-start | bytes 73732
Sparse Core Ops, SparseCore 0:
  10.6 83.1 all-gather.1
  150.0 568.9 reduce-scatter.3
where the time goes:
time: 822 us; the launch traced here: 806 us
  waiting for transfers between devices  537 us (65%)
  blocking collectives  159 us (19%)
  local copies, waits for them, and re-layouts  37.7 us (5%)
  matrix products  28.6 us (3%)
  other arithmetic  23.8 us (3%)
  between operations  14.9 us (2%)
    unnamed x3, waiting for transfers between devices  537 us
    psum x1, blocking collectives, body(): moments = lax.psum(local_moments, ('grp', 'dev'))  82 us
    pmax x1, blocking collectives, body(): fastest = lax.pmax(local_fastest, ('grp', 'dev'))  76.7 us
    unnamed x16, local copies, waits for them, and re-layouts  22.2 us
  transfers between devices with their start and end apart: 2, of which 1 were waited for; matrix products, arithmetic and copies ran while one was open for 7% of the time, Pallas kernels for 0%

commit v1 on v0

v1 whole, which is shorter than its diff:
```python
import jax
import jax.numpy as jnp
from jax import lax
from jax.experimental import pallas as pl
from jax.experimental.pallas import tpu as pltpu
from jax.sharding import PartitionSpec as P

NEAR_CORE = 0.25
FAR_CORE = 1.0
STEP_LIMIT = 0.5
BLK = 128
NB = 16
ND = 32
NG = 8
ROWS = 9 * NB + 8
EXTRA = 9 * NB
DUMMY = NB * ND
F32 = jnp.float32
BF16 = jnp.bfloat16
VMEM = pl.BlockSpec(memory_space=pltpu.VMEM)
SMEM = pl.BlockSpec(memory_space=pltpu.SMEM)


def lanes(rows):
    return lax.broadcasted_iota(jnp.int32, (rows, BLK), 1)


def split(x):
    one = x.astype(BF16)
    rest = x - one.astype(F32)
    two = rest.astype(BF16)
    three = (rest - two.astype(F32)).astype(BF16)
    return one, two, three


def pack_kernel(seg, cells, pairs, out):
    for k in range(NB):
        cols = slice(k * BLK, (k + 1) * BLK)
        out[pl.ds(k, 8, stride=NB), :] = seg[0:8, cols]
        out[8 * NB + k : 8 * NB + k + 1, :] = seg[8:9, cols]
    row = lax.broadcasted_iota(jnp.int32, (NB, BLK), 0)
    cell = jnp.zeros((NB, BLK), jnp.int32)
    for k in range(NB):
        cell = jnp.where(row == k, cells[k] & 31, cell)
    hot = (lanes(NB) == cell).astype(F32)
    hot_last = (lanes(NB) == cell + 32).astype(F32)
    rows = []
    for q in range(3):
        for r in range(3):
            outer = out[(6 + q) * NB : (7 + q) * NB, :] * out[(3 + r) * NB : (4 + r) * NB, :]
            total = jnp.sum(outer, axis=1, keepdims=True)
            rows.append(jnp.sum(total * (hot_last if q + r == 4 else hot), axis=0, keepdims=True))
    out[EXTRA : EXTRA + 1, :] = rows[0] + rows[8] + pairs[...]
    for r in range(1, 8):
        out[EXTRA + r : EXTRA + r + 1, :] = rows[r]


def outer_rows(get):
    t = [get(3 + r) for r in range(3)]
    b = [get(6 + q) for q in range(3)]
    return [[b[q] * t[r] for r in range(3)] for q in range(3)]


def main_kernel(rec, mom, cells, centers, mobility, forces, top, gbuf, obuf, lhs, pos, acc, rbuf, lst, smem, sem):
    me = lax.axis_index("dev")

    def couplings(s, carry):
        o = outer_rows(lambda r: rec[s, r * NB : (r + 1) * NB, :])
        for q in range(3):
            for r in range(3):
                gbuf[pl.ds(s * NB * 16 + 3 * q + r, NB, stride=16), :] = o[q][r] + 0.5 * o[r][q]
        return carry

    lax.fori_loop(0, ND, couplings, 0)
    gbuf[pl.ds(DUMMY * 16, 16), :] = jnp.zeros((16, BLK), F32)
    o = outer_rows(lambda r: rec[me, r * NB : (r + 1) * NB, :])
    for q in range(3):
        for r in range(3):
            obuf[pl.ds(3 * q + r, NB, stride=16), :] = o[q][r]

    for s in range(ND):
        rbuf[s : s + 1, :] = rec[s, EXTRA : EXTRA + 1, :]
    lane = lanes(NB)
    cand = jnp.where(lane < 64, pltpu.roll(rbuf[0:16, :], 64, 1), rbuf[16:32, :])
    other = jnp.where((lane & 32) == 0, pltpu.roll(cand, 96, 1), pltpu.roll(cand, 32, 1))
    ci = cand.astype(jnp.int32)
    hit = (ci >> 4) == me
    code = ((ci & 15) * 1024).astype(F32) + other - float(DUMMY)
    hits = hit.astype(F32)
    sq_row = lax.broadcasted_iota(jnp.int32, (BLK, BLK), 0)
    sq_lane = lanes(BLK)
    below = (sq_row < sq_lane).astype(BF16)
    inside = jnp.dot(hits.astype(BF16), below, preferred_element_type=F32)
    totals = jnp.dot(hits.astype(BF16), jnp.ones((BLK, BLK), BF16), preferred_element_type=F32)
    before = jnp.zeros((NB, BLK), F32)
    running = jnp.zeros((1, BLK), F32)
    row16 = lax.broadcasted_iota(jnp.int32, (NB, BLK), 0)
    for s in range(NB):
        before = jnp.where(row16 == s, running, before)
        running = running + totals[s : s + 1, :]
    count = jnp.sum(hits).astype(jnp.int32)
    rank = jnp.where(hit, inside + before, -1.0)
    turned = jnp.concatenate([rank, code, jnp.zeros((BLK - 32, BLK), F32)], axis=0).T

    def listing(chunk, carry):
        slot = (sq_lane + chunk * BLK).astype(F32)
        found = jnp.zeros((BLK, BLK), F32)
        for c in range(NB):
            found = found + jnp.where(turned[:, c : c + 1] == slot, turned[:, NB + c : NB + c + 1], 0.0)
        codes = jnp.sum(found, axis=0, keepdims=True) + float(DUMMY)
        lst[pl.ds(chunk, 1), :] = codes.astype(jnp.int32)
        return carry

    lax.fori_loop(0, (count + BLK - 1) // BLK, listing, 0)
    copy = pltpu.make_async_copy(lst, smem, sem)
    copy.start()

    far_rhs = []
    for half in range(2):
        rows = jnp.zeros((8, BLK), F32)
        last = jnp.zeros((1, BLK), F32)
        for g in range(4):
            tile = mom[half * 4 + g]
            low = jnp.where(lanes(8) < 32, tile, 0.0)
            high = jnp.where((lanes(8) >= 32) & (lanes(8) < 64), tile, 0.0)
            rows = rows + (pltpu.roll(low, 32 * g, 1) if g else low)
            shifted = pltpu.roll(high, (32 * g + 96) % 128, 1)
            last = last + shifted[0:1, :]
        full = jnp.concatenate([rows, last, jnp.zeros((7, BLK), F32)], axis=0)
        m1, m2, m3 = split(full)
        zero = jnp.zeros((32, BLK), BF16)
        far_rhs.append(jnp.concatenate([m1, m2, m1, m3, m2, m1, zero], axis=0))

    def pull(k, rhs, points, core, drop=None):
        c = jnp.dot(lhs[k], rhs, preferred_element_type=F32)
        if drop is not None:
            c = jnp.where(sq_lane == drop, 0.0, c)
        d = [pos[k, a] - points[a] for a in range(3)]
        inv = lax.rsqrt(d[0] * d[0] + d[1] * d[1] + (d[2] * d[2] + core))
        w = c * (inv * inv * inv)
        return [w * d[a] for a in range(3)]

    def block_rhs(f):
        g = gbuf[pl.ds(pl.multiple_of(f * 16, 16), 16), :]
        g = jnp.where(row16 < 9, g, 0.0)
        g1, g2, g3 = split(g)
        return jnp.concatenate([g1, g2, g1, g3, g2, g1, jnp.zeros((32, BLK), BF16)], axis=0)

    def block_points(f):
        return [rec[f >> 4, pl.ds(a * NB + (f & 15), 1), :] for a in range(3)]

    def home(k, carry):
        own = block_points(me * NB + k)
        ob = jnp.where(row16 < 9, obuf[pl.ds(pl.multiple_of(k * 16, 16), 16), :], 0.0)
        o1, o2, o3 = [x.astype(F32) for x in split(ob)]
        points = jnp.concatenate(own + [jnp.zeros((13, BLK), F32)], axis=0)
        turn = jnp.concatenate([o1, o1, o2, o1, o2, o3, points, jnp.zeros((16, BLK), F32)], axis=0).T
        lhs[k] = turn.astype(BF16)
        for a in range(3):
            pos[k, a] = jnp.broadcast_to(turn[:, 96 + a : 97 + a], (BLK, BLK))
        cell = cells[k]
        one = pull(k, far_rhs[0], [centers[a : a + 1, 0:BLK] for a in range(3)], FAR_CORE, cell)
        two = pull(k, far_rhs[1], [centers[a : a + 1, BLK : 2 * BLK] for a in range(3)], FAR_CORE, cell - BLK)
        self_pull = pull(k, block_rhs(me * NB + k), own, NEAR_CORE)
        for a in range(3):
            acc[k, a] = one[a] + two[a] + self_pull[a]
        return carry

    lax.fori_loop(0, NB, home, 0)
    copy.wait()

    def pair_step(i, carry):
        for u in range(2):
            at = 2 * i + u
            entry = smem[at >> 7, at & 127]
            k = entry >> 10
            f = entry & 1023
            near = pull(k, block_rhs(f), block_points(jnp.minimum(f, DUMMY - 1)), NEAR_CORE)
            for a in range(3):
                acc[k, a] = acc[k, a] + near[a]
        return carry

    lax.fori_loop(0, (count + 1) // 2, pair_step, 0)

    for k in range(NB):
        sums = [jnp.sum(acc[k, a], axis=1, keepdims=True) for a in range(3)]
        cols = jnp.where(sq_lane == 0, sums[0], jnp.where(sq_lane == 1, sums[1], sums[2]))
        forces[:, k * BLK : (k + 1) * BLK] = cols.T[0:3, :]
    v = mobility[...] * forces[...]
    speed = jnp.sum(v * v, axis=0, keepdims=True)
    top[...] = jnp.broadcast_to(jnp.max(speed, axis=1, keepdims=True), (1, BLK))


def step_kernel(tops, forces, mobility, out):
    best = jnp.max(jnp.max(tops[...], axis=0, keepdims=True), axis=1, keepdims=True)
    scale = STEP_LIMIT / (jnp.sqrt(best) + 1e-06)
    out[...] = scale * (mobility[...] * forces[...])


def body(segments, pair_blocks, block_cells, mobility, cell_centers):
    params = pltpu.CompilerParams(vmem_limit_bytes=40 * 1024 * 1024)
    listed = jnp.concatenate([jnp.zeros((64,), jnp.int32), pair_blocks[:, 0], pair_blocks[:, 1]])
    payload = pl.pallas_call(
        pack_kernel,
        out_shape=jax.ShapeDtypeStruct((ROWS, BLK), F32),
        in_specs=[VMEM, SMEM, VMEM],
        out_specs=VMEM,
        name="pack",
    )(segments, block_cells, listed.astype(F32)[None, :])
    rec = lax.all_to_all(jnp.broadcast_to(payload[None], (ND, ROWS, BLK)), "dev", 0, 0, tiled=True)
    group = jnp.sum(rec[:, EXTRA:, :], axis=0)
    mom = lax.all_to_all(jnp.broadcast_to(group[None], (NG, 8, BLK)), "grp", 0, 0, tiled=True)
    mob = mobility[None, :]
    forces, top = pl.pallas_call(
        main_kernel,
        out_shape=(jax.ShapeDtypeStruct((3, NB * BLK), F32), jax.ShapeDtypeStruct((1, BLK), F32)),
        in_specs=[VMEM, VMEM, SMEM, VMEM, VMEM],
        out_specs=(VMEM, VMEM),
        scratch_shapes=[
            pltpu.VMEM(((DUMMY + 1) * 16, BLK), F32),
            pltpu.VMEM((NB * 16, BLK), F32),
            pltpu.VMEM((NB, BLK, BLK), BF16),
            pltpu.VMEM((NB, 3, BLK, BLK), F32),
            pltpu.VMEM((NB, 3, BLK, BLK), F32),
            pltpu.VMEM((ND, BLK), F32),
            pltpu.VMEM((NB, BLK), jnp.int32),
            pltpu.SMEM((NB, BLK), jnp.int32),
            pltpu.SemaphoreType.DMA,
        ],
        compiler_params=params,
        name="forces",
    )(rec, mom, block_cells, cell_centers, mob)
    tops = lax.all_to_all(jnp.broadcast_to(top, (ND * NG, BLK)), ("grp", "dev"), 0, 0, tiled=True)
    displacement = pl.pallas_call(
        step_kernel,
        out_shape=jax.ShapeDtypeStruct((3, NB * BLK), F32),
        in_specs=[VMEM, VMEM, VMEM],
        out_specs=VMEM,
        name="step",
    )(tops, forces, mob)
    return forces, displacement


def solution(mesh):
    both = ("grp", "dev")
    in_specs = (P(None, both), P(both, None), P(both), P(both), P())
    out_specs = (P(None, both), P(None, both))
    return jax.shard_map(body, mesh=mesh, in_specs=in_specs, out_specs=out_specs, check_vma=False)
```

time: 822 us -> 120 us (0.15); the launches traced: 806 us -> 119 us
  waiting for transfers between devices: 537 us -> 0 us
  blocking collectives: 159 us -> 101 us
  local copies, waits for them, and re-layouts: 37.7 us -> 1.9 us
  matrix products: 28.6 us -> 0 us
  other arithmetic: 23.8 us -> 0.62 us
  Pallas kernels: 0 us -> 14.9 us
  between operations: 14.9 us -> 0.68 us
    unnamed x3 -> x0, waiting for transfers between devices: 537 us -> none
    all_to_all x0 -> x3, blocking collectives: none -> 101 us  [the longest x1 70.5 us: body(): lax.all_to_all(jnp.broadcast_to(payload[None], (ND, ROWS, BLK)), 'dev', 0...]
    psum x1 -> x0, blocking collectives: 82 us -> none  [body(): moments = lax.psum(local_moments, ('grp', 'dev'))]
    pmax x1 -> x0, blocking collectives: 76.7 us -> none  [body(): fastest = lax.pmax(local_fastest, ('grp', 'dev'))]
    dot_general x85 -> x0, matrix products: 28.6 us -> none  [the longest x17 5.85 us: pair_weights(): cross_two = jnp.dot(first[3:6].T, second[6:9], precision=high)]
    unnamed x16 -> x6, local copies, waits for them, and re-layouts: 22.2 us -> 0.02 us
    pallas_call x0 -> x3, Pallas kernels: none -> 14.9 us  [the longest x1 11.6 us: body(): pl.pallas_call(main_kernel, out_shape=(jax.ShapeDtypeStruct((3, NB * BLK)...]
    reduce_sum x69 -> x1, other arithmetic: 12.1 us -> 0.03 us  [body(): group = jnp.sum(rec[:, EXTRA:, :], axis=0)]
  transfers between devices with their start and end apart: 2 -> 0, of which waited for: 1 -> 0; matrix products, arithmetic and copies ran while one was open for 7% -> 0% of each run, Pallas kernels for 0% -> 0%
where the time goes in v1:
time: 120 us; the launch traced here: 119 us
  blocking collectives  101 us (84%)
  Pallas kernels  14.9 us (12%)
  local copies, waits for them, and re-layouts  1.9 us (2%)
    all_to_all x1, blocking collectives, body(): lax.all_to_all(jnp.broadcast_to(payload[None], (ND, ROWS, BLK)), 'dev', 0...  70.5 us
    all_to_all x1, blocking collectives, body(): lax.all_to_all(jnp.broadcast_to(top, (ND * NG, BLK)), ('grp', 'dev'), 0,...  19.1 us
    pallas_call x1, Pallas kernels, body(): pl.pallas_call(main_kernel, out_shape=(jax.ShapeDtypeStruct((3, NB * BLK)...  11.6 us
    all_to_all x1, blocking collectives, body(): lax.all_to_all(jnp.broadcast_to(group[None], (NG, 8, BLK)), 'grp', 0, 0,...  11.5 us

profile of v1, /device:TPU:1, one launch (start us, length us, event | category | flops | bytes accessed | tf_op | source)
XLA Modules:
  0.0 119.3 jit_solution(12811617569025833209)
XLA Ops:
  0.6 0.8 slice_bitcast_fusion.1
  1.4 0.6 fusion.1.pairs
  2.0 1.7 %pack.1 = f32[152,128]{1,0:T(8,128)} custom-call(f32[9,2048]{1,0:T(8,128)} %seg.1, s32[16]{0:T(128)} %cells.3, f32[1,128]{1,0:T(1,128)} %fusion.1.pairs), custom_call_target="tpu_custom_call" | custom-call | tf_op jit(solution)/shard_map/pack/pallas_call | solution.py:203
  3.6 1.0 broadcast_in_dim.11
  4.7 0.0 copy-start
  4.7 0.0 copy-start.1
  4.7 0.0 copy-start.2
  4.7 70.5 %all_to_all.18.rec = f32[32,152,128]{2,1,0:T(8,128)S(1)} all-to-all(f32[32,152,128]{2,1,0:T(8,128)S(1)} %broadcast_in_dim.11), channel_id=1, replica_groups=mesh['grp'=8,'dev'=32] {'dev'}, dimensions={0} | all-to-all | bytes 4980736 | tf_op jit(solution)/shard_map/all_to_all | solution.py:210
  75.3 11.5 %all_to_all.19.mom = f32[8,8,128]{2,1,0:T(8,128)S(1)} all-to-all(f32[8,8,128]{2,1,0:T(8,128)S(1)} %broadcast_in_dim.12), channel_id=1, replica_groups=mesh['grp'=8,'dev'=32] {'grp'}, dimensions={0} | all-to-all | bytes 65536 | tf_op jit(solution)/shard_map/all_to_all | solution.py:212
  86.8 0.0 copy-done
  86.8 0.0 copy-done.1
  86.8 0.0 copy-done.2
  86.8 11.6 %forces.1 = (f32[3,2048]{1,0:T(4,128)}, f32[1,128]{1,0:T(1,128)S(1)}) custom-call(f32[32,152,128]{2,1,0:T(8,128)S(1)} %all_to_all.18.rec, f32[8,8,128]{2,1,0:T(8,128)S(1)} %all_to_all.19.mom, s32[16]{0:T(128)S(1)} %copy-done.2, f32[3,256]{1,0:T(4,128)S(1)} %copy-done.1, f32[1,2048]{1,0:T(1,128)S(1)} %bitcast.14), custom_call_target="tpu_custom_call" | custom-call | tf_op jit(solution)/shard_map/forces/pallas_call | solution.py:214
  98.4 0.1 broadcast_in_dim.28
  98.5 19.1 %all_to_all.20 = f32[256,1,128]{2,1,0:T(1,128)} all-to-all(f32[256,1,128]{2,1,0:T(1,128)S(1)} %broadcast_in_dim.28), channel_id=1, replica_groups=mesh['grp'=8,'dev'=32] {'grp','dev'}, dimensions={0} | all-to-all | bytes 262144 | tf_op jit(solution)/shard_map/all_to_all | solution.py:233
  117.6 1.7 %step.1 = f32[3,2048]{1,0:T(4,128)} custom-call(f32[256,128]{1,0:T(8,128)} %bitcast.16, f32[3,2048]{1,0:T(4,128)} %get-tuple-element.2.forces, f32[1,2048]{1,0:T(1,128)} %bitcast.13), custom_call_target="tpu_custom_call" | custom-call | tf_op jit(solution)/shard_map/step/pallas_call | solution.py:234
  (3 shorter events, 0.0 us)
Async XLA Ops:
  4.7 82.1 %copy-start = (f32[2048]{0:T(1024)S(1)}, f32[2048]{0:T(1024)}, u32[]{:S(2)}) copy-start(f32[2048]{0:T(1024)} %param.8) | copy-start | bytes 24580
  4.7 82.1 %copy-start.1 = (f32[3,256]{1,0:T(4,128)S(1)}, f32[3,256]{1,0:T(4,128)}, u32[]{:S(2)}) copy-start(f32[3,256]{1,0:T(4,128)} %centers.1) | copy-start | bytes 9220
  4.7 82.1 %copy-start.2 = (s32[16]{0:T(128)S(1)}, s32[16]{0:T(128)}, u32[]{:S(2)}) copy-start(s32[16]{0:T(128)} %cells.3) | copy-start | bytes 196

commit v2 on v1

v2 whole, which is shorter than its diff:
```python
import jax
import jax.numpy as jnp
from jax import lax
from jax.experimental import pallas as pl
from jax.experimental.pallas import tpu as pltpu
from jax.sharding import Mesh
from jax.sharding import PartitionSpec as P

NEAR_CORE = 0.25
FAR_CORE = 1.0
STEP_LIMIT = 0.5
BLK = 128
NB = 16
NZ = 8
NX = 4
NG = 8
EXTRA = 9 * NB
ROWS = EXTRA + 8
CAP = 24
SECT = 9 * CAP
TASKS = 2048
COUNT, ROUNDS = TASKS + 64, TASKS + 65
PAD = 1 << 16
F32 = jnp.float32
BF16 = jnp.bfloat16
VMEM = pl.BlockSpec(memory_space=pltpu.VMEM)
SMEM = pl.BlockSpec(memory_space=pltpu.SMEM)
NT = (((1,), (1,)), ((), ()))


def lanes(rows):
    return lax.broadcasted_iota(jnp.int32, (rows, BLK), 1)


def subs(rows):
    return lax.broadcasted_iota(jnp.int32, (rows, BLK), 0)


def split(x):
    one = x.astype(BF16)
    rest = x - one.astype(F32)
    two = rest.astype(BF16)
    three = (rest - two.astype(F32)).astype(BF16)
    return one, two, three


def pack_kernel(seg, cells, pairs, out):
    for k in range(NB):
        cols = slice(k * BLK, (k + 1) * BLK)
        out[pl.ds(k, 8, stride=NB), :] = seg[0:8, cols]
        out[8 * NB + k : 8 * NB + k + 1, :] = seg[8:9, cols]
    row = subs(NB)
    cell = jnp.zeros((NB, BLK), jnp.int32)
    for k in range(NB):
        cell = jnp.where(row == k, cells[k] & 31, cell)
    hot = (lanes(NB) == cell + 64).astype(F32)
    hot_last = (lanes(NB) == cell + 96).astype(F32)
    rows = []
    for q in range(3):
        for r in range(3):
            outer = out[(6 + q) * NB : (7 + q) * NB, :] * out[(3 + r) * NB : (4 + r) * NB, :]
            total = jnp.sum(outer, axis=1, keepdims=True)
            rows.append(jnp.sum(total * (hot_last if q + r == 4 else hot), axis=0, keepdims=True))
    out[EXTRA : EXTRA + 1, :] = rows[0] + rows[8]
    for r in range(1, 8):
        out[EXTRA + r : EXTRA + r + 1, :] = rows[r]
    out[EXTRA : EXTRA + 2, 0:32] = pairs[...].astype(F32)


def column_kernel(rec_z, out):
    lane = lanes(8)
    first = rec_z[pl.ds(EXTRA, NZ, stride=ROWS), :]
    second = rec_z[pl.ds(EXTRA + 1, NZ, stride=ROWS), :]
    total = rec_z[EXTRA : EXTRA + 8, :]
    for s in range(1, NZ):
        total = total + rec_z[s * ROWS + EXTRA : s * ROWS + EXTRA + 8, :]
    out[...] = jnp.where(lane < 32, first, jnp.where(lane < 64, pltpu.roll(second, 32, 1), total))


def route_kernel(turn_no, rec_t, rec_z, send, tasks, lst, smem, cnt, sem):
    g = lax.axis_index("y") * 2 + lax.axis_index("c")
    zz = lax.axis_index("z")
    xx = lax.axis_index("x")
    rnd = turn_no[0]
    lane = lanes(8)
    a = jnp.zeros((8, BLK), F32)
    b = jnp.zeros((8, BLK), F32)
    for x in range(NX):
        part = rec_t[pl.ds(pl.multiple_of(g * 32 + x * 8, 8), 8), :]
        one = jnp.where(lane < 32, part, 0.0)
        two = jnp.where((lane >= 32) & (lane < 64), part, 0.0)
        a = a + (pltpu.roll(one, 32 * x, 1) if x else one)
        b = b + (pltpu.roll(two, (32 * x + 96) % 128, 1) if x != 1 else two)
    ai = a.astype(jnp.int32)
    bi = b.astype(jnp.int32)
    own_a = ai >> 4
    own_b = bi >> 4

    need = jnp.zeros((32, 16), F32)
    for i in range(8):
        ra, rb = own_a[i : i + 1, :], own_b[i : i + 1, :]
        for here, there in ((ra, rb), (rb, ra)):
            owner = (subs(32) == here).astype(BF16)
            column = (subs(16) == (there & 3)).astype(BF16)
            need = need + lax.dot_general(owner, column, NT, preferred_element_type=F32)
    r32 = lax.broadcasted_iota(jnp.int32, (32, 16), 0)
    c32 = lax.broadcasted_iota(jnp.int32, (32, 16), 1)
    longest = jnp.max(jnp.where((r32 & 3) == c32, 0.0, need)).astype(jnp.int32)

    hits, codes = [], []
    for x in range(NX):
        d = zz * NX + x
        fa = own_a == d
        fb = own_b == d
        swapped = (bi & 15) * 512 + ai
        hits += [fa | fb, fa & fb]
        codes += [jnp.where(fa, (ai & 15) * 512 + bi, swapped), swapped]
    hit = jnp.concatenate([h.astype(F32) for h in hits], axis=0)
    code = jnp.concatenate(codes, axis=0).astype(F32)
    hot = hit.astype(BF16)
    sq_row, sq_lane = subs(BLK), lanes(BLK)
    inside = jnp.dot(hot, (sq_row < sq_lane).astype(BF16), preferred_element_type=F32)
    totals = jnp.dot(hot, jnp.ones((BLK, BLK), BF16), preferred_element_type=F32)
    r64 = lax.broadcasted_iota(jnp.int32, (64, 64), 0)
    c64 = lax.broadcasted_iota(jnp.int32, (64, 64), 1)
    earlier = ((c64 < r64) & ((c64 >> 4) == (r64 >> 4))).astype(BF16)
    before = jnp.dot(earlier, totals.astype(BF16), preferred_element_type=F32)
    rank = jnp.where(hit > 0.0, inside + before, -1.0)
    turned = jnp.concatenate([rank, code], axis=0).T
    counts = [jnp.sum(hit[16 * x : 16 * x + 16]).astype(jnp.int32) for x in range(NX)]
    for x in range(NX):

        def listing(chunk, carry):
            slot = (sq_lane + chunk * BLK).astype(F32)
            found = jnp.zeros((BLK, BLK), F32)
            for c in range(16 * x, 16 * x + 16):
                found = found + jnp.where(turned[:, c : c + 1] == slot, turned[:, 64 + c : 65 + c], 0.0)
            lst[pl.ds(16 * x + chunk, 1), :] = jnp.sum(found, axis=0, keepdims=True).astype(jnp.int32)
            return carry

        lax.fori_loop(0, (counts[x] + BLK - 1) // BLK, listing, 0)
    copy = pltpu.make_async_copy(lst, smem, sem)
    copy.start()
    send[...] = jnp.zeros_like(send)
    for x in range(2 * NX):
        cnt[x] = 0
    copy.wait()

    def receive(i, at):
        entry = smem[xx * 16 + (i >> 7), i & 127]
        f = entry & 511
        column = (f >> 4) & 3
        here = column == xx
        slot = cnt[column] - rnd * CAP
        cnt[column] = cnt[column] + 1
        base = jnp.where(here, (NX + (f >> 6)) * SECT + (f & 15), column * SECT + slot)
        use = jnp.where(here, rnd == 0, (slot >= 0) & (slot < CAP))
        tasks[at] = base | ((entry >> 9) << 12)
        return at + use.astype(jnp.int32)

    mine = jnp.where(xx == 0, counts[0], jnp.where(xx == 1, counts[1], jnp.where(xx == 2, counts[2], counts[3])))
    used = lax.fori_loop(0, mine, receive, 0)
    for u in range(4):
        tasks[used + u] = PAD
    tasks[COUNT] = used
    tasks[ROUNDS] = (longest + CAP - 1) // CAP

    for x in range(NX):

        def deliver(i, carry):
            f = smem[16 * x + (i >> 7), i & 127] & 511

            @pl.when(((f >> 4) & 3) == xx)
            def _():
                slot = cnt[NX + x] - rnd * CAP
                cnt[NX + x] = cnt[NX + x] + 1

                @pl.when((slot >= 0) & (slot < CAP))
                def _():
                    source = (f >> 6) * ROWS + (f & 15)
                    target = x * SECT + slot
                    send[pl.ds(target, 8, stride=CAP), :] = rec_z[pl.ds(source, 8, stride=NB), :]
                    send[pl.ds(target + 8 * CAP, 1), :] = rec_z[pl.ds(source + 8 * NB, 1), :]

            return carry

        lax.fori_loop(0, jnp.where(xx == x, 0, counts[x]), deliver, 0)


def outer_rows(row, symmetric):
    s = subs(16)
    t = [jnp.broadcast_to(row(3 + r), (16, BLK)) for r in range(3)]
    b = [jnp.broadcast_to(row(6 + q), (16, BLK)) for q in range(3)]

    def slow(v):
        return jnp.where(s < 3, v[0], jnp.where(s < 6, v[1], v[2]))

    def fast(v):
        first = (s == 0) | (s == 3) | (s == 6)
        return jnp.where(first, v[0], jnp.where((s == 1) | (s == 4) | (s == 7), v[1], v[2]))

    o = slow(b) * fast(t)
    return o + 0.5 * (fast(b) * slow(t)) if symmetric else o


def right_side(rows):
    one, two, three = split(rows)
    return jnp.concatenate([one, two, one, three, two, one, jnp.zeros((32, BLK), BF16)], axis=0)


def prepare(k, row, lhs, pos):
    o = jnp.where(subs(16) < 9, outer_rows(row, False), 0.0)
    o1, o2, o3 = [x.astype(F32) for x in split(o)]
    points = jnp.concatenate([row(a) for a in range(3)] + [jnp.zeros((13, BLK), F32)], axis=0)
    turn = jnp.concatenate([o1, o1, o2, o1, o2, o3, points, jnp.zeros((16, BLK), F32)], axis=0).T
    lhs[k] = turn.astype(BF16)
    for a in range(3):
        pos[k, a] = jnp.broadcast_to(turn[:, 96 + a : 97 + a], (BLK, BLK))


def pull(k, lhs, pos, rhs, points, core, drop=None):
    c = jnp.dot(lhs[k], rhs, preferred_element_type=F32)
    if drop is not None:
        c = jnp.where(lanes(BLK) == drop, 0.0, c)
    d = [pos[k, a] - points[a] for a in range(3)]
    inv = lax.rsqrt(d[0] * d[0] + d[1] * d[1] + (d[2] * d[2] + core))
    w = c * (inv * inv * inv)
    return [w * d[a] for a in range(3)]


def total_rows(acc, k):
    sums = [jnp.sum(acc[k, a], axis=1, keepdims=True) for a in range(3)]
    lane = lanes(BLK)
    return jnp.where(lane == 0, sums[0], jnp.where(lane == 1, sums[1], sums[2])).T[0:3, :]


def home_kernel(own, rec_t, cells, centers, forces, lhs, pos, acc):
    far_rhs = []
    for half in range(2):
        rows = jnp.zeros((8, BLK), F32)
        last = jnp.zeros((8, BLK), F32)
        for i in range(4):
            at = (half * 4 + i) * 32
            tile = rec_t[at : at + 8, :]
            for x in range(1, NX):
                tile = tile + rec_t[at + 8 * x : at + 8 * x + 8, :]
            low = jnp.where((lanes(8) >= 64) & (lanes(8) < 96), tile, 0.0)
            high = jnp.where(lanes(8) >= 96, tile, 0.0)
            rows = rows + (pltpu.roll(low, (32 * i + 64) % 128, 1) if i != 2 else low)
            last = last + (pltpu.roll(high, (32 * i + 32) % 128, 1) if i != 3 else high)
        far_rhs.append(right_side(jnp.concatenate([rows, last[0:1, :], jnp.zeros((7, BLK), F32)], axis=0)))

    def step(k, carry):
        def row(r):
            return own[pl.ds(r * NB + k, 1), :]

        prepare(k, row, lhs, pos)
        cell = cells[k]
        self_rhs = right_side(jnp.where(subs(16) < 9, outer_rows(row, True), 0.0))
        one = pull(k, lhs, pos, far_rhs[0], [centers[a : a + 1, 0:BLK] for a in range(3)], FAR_CORE, cell)
        two = pull(k, lhs, pos, far_rhs[1], [centers[a : a + 1, BLK:] for a in range(3)], FAR_CORE, cell - BLK)
        same = pull(k, lhs, pos, self_rhs, [row(a) for a in range(3)], NEAR_CORE)
        for a in range(3):
            acc[k, a] = one[a] + two[a] + same[a]
        return carry

    lax.fori_loop(0, NB, step, 0)
    for k in range(NB):
        forces[:, k * BLK : (k + 1) * BLK] = total_rows(acc, k)


def near_kernel(rec_x, rec_z, tasks, so_far, mobility, forces, top, blocks, lhs, pos, acc):
    zz = lax.axis_index("z")
    blocks[0 : NX * SECT, :] = rec_x[...]
    for s in range(NZ):
        for r in range(9):
            at = (NX + s) * SECT + r * CAP
            blocks[at : at + NB, :] = rec_z[s * ROWS + r * NB : s * ROWS + (r + 1) * NB, :]

    def ready(k, carry):
        prepare(k, lambda r: blocks[pl.ds((NX + zz) * SECT + r * CAP + k, 1), :], lhs, pos)
        for a in range(3):
            acc[k, a] = jnp.zeros((BLK, BLK), F32)
        return carry

    lax.fori_loop(0, NB, ready, 0)

    def pair_step(i, carry):
        for u in range(2):
            entry = tasks[2 * i + u]
            base = entry & 4095
            k = (entry >> 12) & 15
            limit = jnp.where(entry >= PAD, 0, 9)

            def row(r):
                return blocks[pl.ds(base + r * CAP, 1), :]

            rhs = right_side(jnp.where(subs(16) < limit, outer_rows(row, True), 0.0))
            near = pull(k, lhs, pos, rhs, [row(a) for a in range(3)], NEAR_CORE)
            for a in range(3):
                acc[k, a] = acc[k, a] + near[a]
        return carry

    lax.fori_loop(0, (tasks[COUNT] + 1) // 2, pair_step, 0)
    for k in range(NB):
        cols = slice(k * BLK, (k + 1) * BLK)
        forces[:, cols] = so_far[:, cols] + total_rows(acc, k)
    v = mobility[...] * forces[...]
    speed = jnp.sum(v * v, axis=0, keepdims=True)
    top[...] = jnp.broadcast_to(jnp.max(speed, axis=1, keepdims=True), (1, BLK))


def step_kernel(tops, forces, mobility, out):
    best = jnp.max(jnp.max(tops[...], axis=0, keepdims=True), axis=1, keepdims=True)
    scale = STEP_LIMIT / (jnp.sqrt(best) + 1e-06)
    out[...] = scale * (mobility[...] * forces[...])


def shape(*dims, kind=F32):
    return jax.ShapeDtypeStruct(dims, kind)


def work_scratch():
    return [
        pltpu.VMEM((NB, BLK, BLK), BF16),
        pltpu.VMEM((NB, 3, BLK, BLK), F32),
        pltpu.VMEM((NB, 3, BLK, BLK), F32),
    ]


def body(segments, pair_blocks, block_cells, mobility, cell_centers):
    params = pltpu.CompilerParams(vmem_limit_bytes=24 * 1024 * 1024)
    seg_count = segments.shape[1]
    own = pl.pallas_call(
        pack_kernel,
        out_shape=shape(ROWS, BLK),
        in_specs=[VMEM, SMEM, VMEM],
        out_specs=VMEM,
        name="pack",
    )(segments, block_cells, pair_blocks.T)
    rec_z = lax.all_to_all(jnp.broadcast_to(own[None], (NZ, ROWS, BLK)), "z", 0, 0, tiled=True)
    rec_z = rec_z.reshape(NZ * ROWS, BLK)
    column = pl.pallas_call(
        column_kernel, out_shape=shape(8, BLK), in_specs=[VMEM], out_specs=VMEM, name="column"
    )(rec_z)
    rec_t = lax.all_to_all(jnp.broadcast_to(column[None], (NG * NX, 8, BLK)), ("y", "c", "x"), 0, 0, tiled=True)
    rec_t = rec_t.reshape(NG * NX * 8, BLK)

    def exchange(number):
        send, tasks = pl.pallas_call(
            route_kernel,
            out_shape=(shape(NX * SECT, BLK), shape(TASKS + 128, kind=jnp.int32)),
            in_specs=[SMEM, VMEM, VMEM],
            out_specs=(VMEM, SMEM),
            scratch_shapes=[
                pltpu.VMEM((NX * 16, BLK), jnp.int32),
                pltpu.SMEM((NX * 16, BLK), jnp.int32),
                pltpu.SMEM((2 * NX,), jnp.int32),
                pltpu.SemaphoreType.DMA,
            ],
            compiler_params=params,
            name="route",
        )(number, rec_t, rec_z)
        rec_x = lax.all_to_all(send.reshape(NX, SECT, BLK), "x", 0, 0, tiled=True)
        return rec_x.reshape(NX * SECT, BLK), tasks

    def add_near(rec_x, tasks, so_far):
        return pl.pallas_call(
            near_kernel,
            out_shape=(shape(3, seg_count), shape(1, BLK)),
            in_specs=[VMEM, VMEM, SMEM, VMEM, VMEM],
            out_specs=(VMEM, VMEM),
            scratch_shapes=[pltpu.VMEM(((NX + NZ) * SECT, BLK), F32)] + work_scratch(),
            compiler_params=params,
            name="near",
        )(rec_x, rec_z, tasks, so_far, mob)

    mob = mobility[None, :]
    rec_x, tasks = exchange(jnp.zeros((1,), jnp.int32))
    home = pl.pallas_call(
        home_kernel,
        out_shape=shape(3, seg_count),
        in_specs=[VMEM, VMEM, SMEM, VMEM],
        out_specs=VMEM,
        scratch_shapes=work_scratch(),
        compiler_params=params,
        cost_estimate=pl.CostEstimate(flops=6 * 10**9, bytes_accessed=10**6, transcendentals=0),
        name="home",
    )(own, rec_t, block_cells, cell_centers)
    forces, top = add_near(rec_x, tasks, home)

    def more(carry):
        number, so_far, _ = carry
        rec_x, tasks = exchange(number[None])
        forces, top = add_near(rec_x, tasks, so_far)
        return number + 1, forces, top

    rounds = tasks[ROUNDS]
    _, forces, top = lax.while_loop(lambda c: c[0] < rounds, more, (jnp.ones((), jnp.int32), forces, top))
    tops = lax.all_to_all(jnp.broadcast_to(top, (8 * NG * NX, BLK)), ("y", "c", "z", "x"), 0, 0, tiled=True)
    displacement = pl.pallas_call(
        step_kernel, out_shape=shape(3, seg_count), in_specs=[VMEM, VMEM, VMEM], out_specs=VMEM, name="step"
    )(tops, forces, mob)
    return forces, displacement


def solution(mesh):
    names = ("y", "c", "z", "x")
    fine = Mesh(mesh.devices.reshape(NG // 2, 2, NZ, NX), names)
    in_specs = (P(None, names), P(names, None), P(names), P(names), P())
    out_specs = (P(None, names), P(None, names))
    return jax.shard_map(body, mesh=fine, in_specs=in_specs, out_specs=out_specs, check_vma=False)
```

time: 120 us -> 100 us (0.83); the launches traced: 119 us -> 101 us
  blocking collectives: 101 us -> 45.8 us
  Pallas kernels: 14.9 us -> 27.7 us
  starting transfers between devices: 0 us -> 12.7 us
  waiting for transfers between devices: 0 us -> 9.6 us
  local copies, waits for them, and re-layouts: 1.9 us -> 3.53 us
    all_to_all x3 -> x2, blocking collectives: 101 us -> 45.8 us  [the longest x1 27.4 us: body(): lax.all_to_all(jnp.broadcast_to(own[None], (NZ, ROWS, BLK)), 'z', 0, 0, t...]
    pallas_call x3 -> x6, Pallas kernels: 14.9 us -> 27.7 us  [the longest x1 9.73 us: add_near(): pl.pallas_call(near_kernel, out_shape=(shape(3, seg_count), shape(1, BLK)...]
    all_to_all x0 -> x2, starting transfers between devices: none -> 12.7 us  [the longest x1 9.08 us: body(): lax.all_to_all(jnp.broadcast_to(column[None], (NG * NX, 8, BLK)), ('y', '...]
    all_to_all x0 -> x2, waiting for transfers between devices: none -> 9.6 us  [the longest x1 7.62 us: body(): lax.all_to_all(jnp.broadcast_to(column[None], (NG * NX, 8, BLK)), ('y', '...]
    broadcast_in_dim x4 -> x3, local copies, waits for them, and re-layouts: 1.12 us -> 2.35 us  [the longest x1 1.35 us: body(): jnp.broadcast_to(column[None], (NG * NX, 8, BLK))]
  transfers between devices with their start and end apart: 0 -> 2, of which waited for: 0 -> 2; matrix products, arithmetic and copies ran while one was open for 0% -> 0% of each run, Pallas kernels for 0% -> 7%
where the time goes in v2:
time: 100 us; the launch traced here: 101 us
  blocking collectives  45.8 us (46%)
  Pallas kernels  27.7 us (28%)
  starting transfers between devices  12.7 us (13%)
  waiting for transfers between devices  9.6 us (10%)
  local copies, waits for them, and re-layouts  3.53 us (4%)
    all_to_all x1, blocking collectives, body(): lax.all_to_all(jnp.broadcast_to(own[None], (NZ, ROWS, BLK)), 'z', 0, 0, t...  27.4 us
    all_to_all x1, blocking collectives, body(): lax.all_to_all(jnp.broadcast_to(top, (8 * NG * NX, BLK)), ('y', 'c', 'z',...  18.4 us
    pallas_call x1, Pallas kernels, add_near(): pl.pallas_call(near_kernel, out_shape=(shape(3, seg_count), shape(1, BLK)...  9.73 us
    all_to_all x1, starting transfers between devices, body(): lax.all_to_all(jnp.broadcast_to(column[None], (NG * NX, 8, BLK)), ('y', '...  9.08 us
    all_to_all x1, waiting for transfers between devices, body(): lax.all_to_all(jnp.broadcast_to(column[None], (NG * NX, 8, BLK)), ('y', '...  7.62 us
    pallas_call x1, Pallas kernels, exchange(): pl.pallas_call(route_kernel, out_shape=(shape(NX * SECT, BLK), shape(TASK...  7.22 us
    pallas_call x1, Pallas kernels, body(): pl.pallas_call(home_kernel, out_shape=shape(3, seg_count), in_specs=[VMEM...  6.81 us
    all_to_all x1, starting transfers between devices, exchange(): rec_x = lax.all_to_all(send.reshape(NX, SECT, BLK), 'x', 0, 0, tiled=True)  3.59 us
  transfers between devices with their start and end apart: 2, of which 2 were waited for; matrix products, arithmetic and copies ran while one was open for 0% of the time, Pallas kernels for 7%

profile of v2, /device:TPU:1, one launch (start us, length us, event | category | flops | bytes accessed | tf_op | source)
XLA Modules:
  0.0 100.7 jit_solution(12674697572672716916)
XLA Ops:
  0.6 1.7 %pack.1.own = f32[152,128]{1,0:T(8,128)} custom-call(f32[9,2048]{1,0:T(8,128)} %seg.1, s32[16]{0:T(128)} %cells.3, s32[2,32]{1,0:T(2,128)} %bitcast.30), custom_call_target="tpu_custom_call" | custom-call | tf_op jit(solution)/shard_map/pack/pallas_call | solution.py:334
  2.3 0.9 broadcast_in_dim.11
  3.2 27.4 %all_to_all.29 = f32[8,152,128]{2,1,0:T(8,128)S(1)} all-to-all(f32[8,152,128]{2,1,0:T(8,128)S(1)} %broadcast_in_dim.11), channel_id=1, replica_groups=mesh['y'=4,'c'=2,'z'=8,'x'=4] {'z'}, dimensions={0} | all-to-all | bytes 1245184 | tf_op jit(solution)/shard_map/all_to_all | solution.py:341
  30.6 0.7 column.1
  31.3 1.4 %broadcast_in_dim.12 = f32[32,8,128]{2,1,0:T(8,128)} broadcast(f32[8,128]{1,0:T(8,128)} %column.1), dimensions={1,2} | broadcast | bytes 135168 | tf_op jit(solution)/shard_map/broadcast_in_dim | solution.py:346
  32.6 9.1 %all-to-all-start.2 = ((f32[32,8,128]{2,1,0:T(8,128)}), f32[32,8,128]{2,1,0:T(8,128)S(1)}, u32[]{:S(2)}, u32[]{:S(2)}) async-start(f32[32,8,128]{2,1,0:T(8,128)} %broadcast_in_dim.12), calls=%async_computation.2 | async-start | bytes 262144 | tf_op jit(solution)/shard_map/all_to_all | solution.py:346
  41.7 7.6 %all-to-all-done.2 = f32[32,8,128]{2,1,0:T(8,128)S(1)} async-done(((f32[32,8,128]{2,1,0:T(8,128)}), f32[32,8,128]{2,1,0:T(8,128)S(1)}, u32[]{:S(2)}, u32[]{:S(2)}) %all-to-all-start.2) | async-done | bytes 131104 | tf_op jit(solution)/shard_map/all_to_all | solution.py:346
  49.3 7.2 %route.2 = (f32[864,128]{1,0:T(8,128)}, s32[2176]{0:T(1024)S(1)}) custom-call(s32[1]{0:T(128)} %constant.2.clone.1.turn_no, f32[256,128]{1,0:T(8,128)S(1)} %bitcast.24, f32[1216,128]{1,0:T(8,128)S(1)} %bitcast.21), custom_call_target="tpu_custom_call" | custom-call | tf_op jit(solution)/shard_map/route/pallas_call | solution.py:350
  56.6 0.6 slice.3
  57.2 3.6 %all-to-all-start.3 = ((f32[4,216,128]{2,1,0:T(8,128)}), f32[4,216,128]{2,1,0:T(8,128)S(1)}, u32[]{:S(2)}, u32[]{:S(2)}) async-start(f32[4,216,128]{2,1,0:T(8,128)} %bitcast.6), calls=%async_computation.3 | async-start | bytes 884736 | tf_op jit(solution)/shard_map/all_to_all | solution.py:364
  60.8 0.0 copy-done
  60.8 0.0 copy-done.1
  60.8 0.0 copy-done.2
  60.8 0.0 copy-start.4
  60.8 6.8 %home.1.so_far = f32[3,2048]{1,0:T(4,128)S(1)} custom-call(f32[152,128]{1,0:T(8,128)S(1)} %copy-done, f32[256,128]{1,0:T(8,128)S(1)} %bitcast.25, s32[16]{0:T(128)S(1)} %copy-done.1, f32[3,256]{1,0:T(4,128)S(1)} %copy-done.2), custom_call_target="tpu_custom_call" | custom-call | flops 6000000000 | bytes 1000000 | tf_op jit(solution)/shard_map/home/pallas_call | solution.py:380
  67.6 2.0 %all-to-all-done.3 = f32[4,216,128]{2,1,0:T(8,128)S(1)} async-done(((f32[4,216,128]{2,1,0:T(8,128)}), f32[4,216,128]{2,1,0:T(8,128)S(1)}, u32[]{:S(2)}, u32[]{:S(2)}) %all-to-all-start.3) | async-done | bytes 442400 | tf_op jit(solution)/shard_map/all_to_all | solution.py:364
  69.6 0.0 copy-done.4
  69.6 9.7 %near.2 = (f32[3,2048]{1,0:T(4,128)S(1)}, f32[1,128]{1,0:T(1,128)}) custom-call(f32[864,128]{1,0:T(8,128)S(1)} %bitcast.19, f32[1216,128]{1,0:T(8,128)S(1)} %bitcast.22, s32[2176]{0:T(1024)S(1)} %get-tuple-element.49.tasks, f32[3,2048]{1,0:T(4,128)S(1)} %home.1.so_far, f32[1,2048]{1,0:T(1,128)S(1)} %bitcast.28), custom_call_target="tpu_custom_call" | custom-call | tf_op jit(solution)/shard_map/near/pallas_call | solution.py:368
  79.3 0.7 while.15
  80.0 0.0 copy-start.3
  80.0 0.6 copy-done.5
  80.6 0.1 broadcast_in_dim.26
  80.6 18.4 %all_to_all.30 = f32[256,1,128]{2,1,0:T(1,128)} all-to-all(f32[256,1,128]{2,1,0:T(1,128)S(1)} %broadcast_in_dim.26), channel_id=1, replica_groups=mesh['y'=4,'c'=2,'z'=8,'x'=4] {'y','c','z','x'}, dimensions={0} | all-to-all | bytes 262144 | tf_op jit(solution)/shard_map/all_to_all | solution.py:400
  99.0 1.6 %step.1 = f32[3,2048]{1,0:T(4,128)} custom-call(f32[256,128]{1,0:T(8,128)} %bitcast.27, f32[3,2048]{1,0:T(4,128)S(1)} %get-tuple-element.46.forces, f32[1,2048]{1,0:T(1,128)S(1)} %get-tuple-element.145), custom_call_target="tpu_custom_call" | custom-call | tf_op jit(solution)/shard_map/step/pallas_call | solution.py:401
  (5 shorter events, 0.0 us)
Async XLA Ops:
  32.6 16.7 %all-to-all-start.2 = ((f32[32,8,128]{2,1,0:T(8,128)}), f32[32,8,128]{2,1,0:T(8,128)S(1)}, u32[]{:S(2)}, u32[]{:S(2)}) async-start(f32[32,8,128]{2,1,0:T(8,128)} %broadcast_in_dim.12), calls=%async_computation.2 | async-start | bytes 262144 | tf_op jit(solution)/shard_map/all_to_all | solution.py:346
  57.1 3.6 %copy-start = (f32[152,128]{1,0:T(8,128)S(1)}, f32[152,128]{1,0:T(8,128)}, u32[]{:S(2)}) copy-start(f32[152,128]{1,0:T(8,128)} %pack.1.own) | copy-start | bytes 233476
  57.1 3.6 %copy-start.1 = (s32[16]{0:T(128)S(1)}, s32[16]{0:T(128)}, u32[]{:S(2)}) copy-start(s32[16]{0:T(128)} %cells.3) | copy-start | bytes 196
  57.1 3.6 %copy-start.2 = (f32[3,256]{1,0:T(4,128)S(1)}, f32[3,256]{1,0:T(4,128)}, u32[]{:S(2)}) copy-start(f32[3,256]{1,0:T(4,128)} %centers.1) | copy-start | bytes 9220
  57.2 12.4 %all-to-all-start.3 = ((f32[4,216,128]{2,1,0:T(8,128)}), f32[4,216,128]{2,1,0:T(8,128)S(1)}, u32[]{:S(2)}, u32[]{:S(2)}) async-start(f32[4,216,128]{2,1,0:T(8,128)} %bitcast.6), calls=%async_computation.3 | async-start | bytes 884736 | tf_op jit(solution)/shard_map/all_to_all | solution.py:364
  60.8 8.8 %copy-start.4 = (f32[2048]{0:T(1024)S(1)}, f32[2048]{0:T(1024)}, u32[]{:S(2)}) copy-start(f32[2048]{0:T(1024)} %param.10) | copy-start | bytes 24580
  80.0 19.1 %copy-start.3 = (f32[3,2048]{1,0:T(4,128)}, f32[3,2048]{1,0:T(4,128)S(1)}, u32[]{:S(2)}) copy-start(f32[3,2048]{1,0:T(4,128)S(1)} %get-tuple-element.46.forces) | copy-start | bytes 73732
  80.0 0.6 copy-start.5

commit v3 on v2

v3 whole, which is shorter than its diff:
```python
import jax
import jax.numpy as jnp
from jax import lax
from jax.experimental import pallas as pl
from jax.experimental.pallas import tpu as pltpu
from jax.sharding import Mesh
from jax.sharding import PartitionSpec as P

NEAR_CORE = 0.25
FAR_CORE = 1.0
STEP_LIMIT = 0.5
BLK = 128
NB = 16
NZ = 8
NX = 4
NG = 8
EXTRA = 9 * NB
ROWS = EXTRA + 8
CAP = 24
SECT = 9 * CAP
LOCAL = NX * SECT
TASKS = 2048
COUNT = TASKS + 64
UNROLL = 2
PAD = 1 << 16
F32 = jnp.float32
BF16 = jnp.bfloat16
VMEM = pl.BlockSpec(memory_space=pltpu.VMEM)
SMEM = pl.BlockSpec(memory_space=pltpu.SMEM)
ANY = pl.BlockSpec(memory_space=pl.ANY)
NT = (((1,), (1,)), ((), ()))


def lanes(rows):
    return lax.broadcasted_iota(jnp.int32, (rows, BLK), 1)


def subs(rows):
    return lax.broadcasted_iota(jnp.int32, (rows, BLK), 0)


def split(x):
    one = x.astype(BF16)
    rest = x - one.astype(F32)
    two = rest.astype(BF16)
    three = (rest - two.astype(F32)).astype(BF16)
    return one, two, three


def pack_kernel(seg, cells, pairs, packed, out):
    for k in range(NB):
        cols = slice(k * BLK, (k + 1) * BLK)
        out[pl.ds(k, 8, stride=NB), :] = seg[0:8, cols]
        out[8 * NB + k : 8 * NB + k + 1, :] = seg[8:9, cols]
    row = subs(NB)
    cell = jnp.zeros((NB, BLK), jnp.int32)
    for k in range(NB):
        cell = jnp.where(row == k, cells[k] & 31, cell)
    hot = (lanes(NB) == cell + 64).astype(F32)
    hot_last = (lanes(NB) == cell + 96).astype(F32)
    rows = []
    for q in range(3):
        for r in range(3):
            outer = out[(6 + q) * NB : (7 + q) * NB, :] * out[(3 + r) * NB : (4 + r) * NB, :]
            total = jnp.sum(outer, axis=1, keepdims=True)
            rows.append(jnp.sum(total * (hot_last if q + r == 4 else hot), axis=0, keepdims=True))
    out[EXTRA : EXTRA + 1, :] = rows[0] + rows[8]
    for r in range(1, 8):
        out[EXTRA + r : EXTRA + r + 1, :] = rows[r]
    out[EXTRA : EXTRA + 2, 0:32] = pairs[...].astype(F32)
    whole = out[...]
    for copy in range(NZ):
        packed[copy * ROWS : (copy + 1) * ROWS, :] = whole


def column_kernel(*refs):
    out = refs[NZ]
    lane = lanes(8)
    first = jnp.concatenate([ref[0:1, :] for ref in refs[:NZ]], axis=0)
    second = jnp.concatenate([ref[1:2, :] for ref in refs[:NZ]], axis=0)
    total = refs[0][...]
    for ref in refs[1:NZ]:
        total = total + ref[...]
    tile = jnp.where(lane < 32, first, jnp.where(lane < 64, pltpu.roll(second, 32, 1), total))
    for copy in range(NG * NX):
        out[8 * copy : 8 * copy + 8, :] = tile


def group_pairs(rec_t):
    g = lax.axis_index("y") * 2 + lax.axis_index("c")
    lane = lanes(8)
    a = jnp.zeros((8, BLK), F32)
    b = jnp.zeros((8, BLK), F32)
    for x in range(NX):
        part = rec_t[pl.ds(pl.multiple_of(g * 32 + x * 8, 8), 8), :]
        one = jnp.where(lane < 32, part, 0.0)
        two = jnp.where((lane >= 32) & (lane < 64), part, 0.0)
        a = a + (pltpu.roll(one, 32 * x, 1) if x else one)
        b = b + (pltpu.roll(two, (32 * x + 96) % 128, 1) if x != 1 else two)
    return a.astype(jnp.int32), b.astype(jnp.int32)


def list_hits(hit, code, lst, smem, sem):
    rows = hit.shape[0]
    hits = hit.astype(F32)
    hot = jnp.concatenate([hits, jnp.zeros((16 - rows, BLK), F32)], axis=0) if rows < 16 else hits
    hot = hot.astype(BF16)
    sq_row, sq_lane = subs(BLK), lanes(BLK)
    inside = jnp.dot(hot, (sq_row < sq_lane).astype(BF16), preferred_element_type=F32)
    totals = jnp.dot(hot, jnp.ones((BLK, BLK), BF16), preferred_element_type=F32)
    before = jnp.zeros((16, BLK), F32)
    running = jnp.zeros((1, BLK), F32)
    for s in range(rows):
        before = jnp.where(subs(16) == s, running, before)
        running = running + totals[s : s + 1, :]
    count = jnp.max(running).astype(jnp.int32)
    rank = jnp.where(hits > 0.0, (inside + before)[0:rows, :], -1.0)
    code = code.astype(F32)

    def listing(chunk, carry):
        slot = (sq_row + chunk * BLK).astype(F32)
        found = jnp.zeros((BLK, BLK), F32)
        for c in range(rows):
            found = found + jnp.where(rank[c : c + 1, :] == slot, code[c : c + 1, :], 0.0)
        lst[pl.ds(chunk, 1), :] = jnp.sum(found.T, axis=0, keepdims=True).astype(jnp.int32)
        return carry

    listing(0, 0)
    lax.fori_loop(1, (count + BLK - 1) // BLK, listing, 0)
    copy = pltpu.make_async_copy(lst, smem, sem)
    copy.start()
    return copy, count


def send_kernel(turn_no, rec_t, rec_z_ref, send, lst, smem, cnt, sem, rec_z, sem_z):
    bring = pltpu.make_async_copy(rec_z_ref, rec_z, sem_z)
    bring.start()
    zz = lax.axis_index("z")
    xx = lax.axis_index("x")
    rnd = turn_no[0]
    ai, bi = group_pairs(rec_t)
    own_a, own_b = ai >> 4, bi >> 4
    xa, xb = own_a & 3, own_b & 3
    to_a = ((own_a >> 2) == zz) & (xa != xx) & (xb == xx)
    to_b = ((own_b >> 2) == zz) & (xb != xx) & (xa == xx)
    code = jnp.where(to_a, xa * 512 + bi, xb * 512 + ai)
    copy, count = list_hits(to_a | to_b, code, lst, smem, sem)
    send[...] = jnp.zeros_like(send)
    for x in range(NX):
        cnt[x] = 0
    copy.wait()
    bring.wait()

    def deliver(i, carry):
        entry = smem[i >> 7, i & 127]
        f = entry & 511
        x = entry >> 9
        slot = cnt[x] - rnd * CAP
        cnt[x] = cnt[x] + 1

        @pl.when((slot >= 0) & (slot < CAP))
        def _():
            source = (f >> 6) * ROWS + (f & 15)
            target = x * SECT + slot
            send[pl.ds(target, 8, stride=CAP), :] = rec_z[pl.ds(source, 8, stride=NB), :]
            send[pl.ds(target + 8 * CAP, 1), :] = rec_z[pl.ds(source + 8 * NB, 1), :]

        return carry

    lax.fori_loop(0, count, deliver, 0)


def tasks_kernel(turn_no, rec_t, tasks, rounds, lst, smem, cnt, sem):
    zz = lax.axis_index("z")
    xx = lax.axis_index("x")
    rnd = turn_no[0]
    ai, bi = group_pairs(rec_t)
    own_a, own_b = ai >> 4, bi >> 4
    me = zz * NX + xx
    fa, fb = own_a == me, own_b == me
    swapped = (bi & 15) * 512 + ai
    hits = jnp.concatenate([(fa | fb).astype(F32), (fa & fb).astype(F32)], axis=0)
    code = jnp.concatenate([jnp.where(fa, (ai & 15) * 512 + bi, swapped), swapped], axis=0)
    copy, count = list_hits(hits > 0.0, code, lst, smem, sem)

    owner, column = [], []
    for here, there in ((own_a, own_b), (own_b, own_a)):
        for i in range(8):
            owner.append((subs(32) == here[i : i + 1, :]).astype(BF16))
            column.append((subs(16) == (there[i : i + 1, :] & 3)).astype(BF16))
    owner, column = jnp.concatenate(owner, axis=1), jnp.concatenate(column, axis=1)
    need = lax.dot_general(owner, column, NT, preferred_element_type=F32)
    r32 = lax.broadcasted_iota(jnp.int32, (32, 16), 0)
    c32 = lax.broadcasted_iota(jnp.int32, (32, 16), 1)
    longest = jnp.max(jnp.where((r32 & 3) == c32, 0.0, need)).astype(jnp.int32)
    rounds[0] = (longest + CAP - 1) // CAP
    for x in range(NX):
        cnt[x] = 0
    copy.wait()

    def receive(i, at):
        entry = smem[i >> 7, i & 127]
        f = entry & 511
        column = (f >> 4) & 3
        here = column == xx
        slot = cnt[column] - rnd * CAP
        cnt[column] = cnt[column] + 1
        base = jnp.where(here, LOCAL + (f >> 6) * ROWS + (f & 15), column * SECT + slot)
        use = jnp.where(here, rnd == 0, (slot >= 0) & (slot < CAP))
        tasks[at] = base | ((entry >> 9) << 12)
        return at + use.astype(jnp.int32)

    used = lax.fori_loop(0, count, receive, 0)
    for u in range(8):
        tasks[used + u] = PAD
    tasks[COUNT] = used


def outer_rows(row, symmetric):
    s = subs(16)
    t = [jnp.broadcast_to(row(3 + r), (16, BLK)) for r in range(3)]
    b = [jnp.broadcast_to(row(6 + q), (16, BLK)) for q in range(3)]

    def slow(v):
        return jnp.where(s < 3, v[0], jnp.where(s < 6, v[1], v[2]))

    def fast(v):
        first = (s == 0) | (s == 3) | (s == 6)
        return jnp.where(first, v[0], jnp.where((s == 1) | (s == 4) | (s == 7), v[1], v[2]))

    o = slow(b) * fast(t)
    return o + 0.5 * (fast(b) * slow(t)) if symmetric else o


def right_side(rows):
    one, two, three = split(rows)
    return jnp.concatenate([one, two, one, three, two, one, jnp.zeros((32, BLK), BF16)], axis=0)


def prepare(k, row, left):
    o = jnp.where(subs(16) < 9, outer_rows(row, False), 0.0)
    o1, o2, o3 = [x.astype(F32) for x in split(o)]
    points = jnp.concatenate([row(a) for a in range(3)] + [jnp.zeros((13, BLK), F32)], axis=0)
    left[k] = jnp.concatenate([o1, o1, o2, o1, o2, o3, points, jnp.zeros((16, BLK), F32)], axis=0).T


def spread(left):
    return [jnp.broadcast_to(left[:, 96 + a : 97 + a], (BLK, BLK)) for a in range(3)]


def pull(left, here, rhs, there, core, drop=None):
    c = jnp.dot(left, rhs, preferred_element_type=F32)
    if drop is not None:
        c = jnp.where(lanes(BLK) == drop, 0.0, c)
    d = [here[a] - there[a] for a in range(3)]
    inv = lax.rsqrt(d[0] * d[0] + d[1] * d[1] + (d[2] * d[2] + core))
    w = c * (inv * inv * inv)
    return [w * d[a] for a in range(3)]


def total_rows(acc, k):
    return jnp.concatenate([jnp.sum(acc[k, a].T, axis=0, keepdims=True) for a in range(3)], axis=0)


def own_kernel(own, left, forces, acc):
    def step(k, carry):
        def row(r):
            return own[pl.ds(r * NB + k, 1), :]

        prepare(k, row, left)
        rhs = right_side(jnp.where(subs(16) < 9, outer_rows(row, True), 0.0))
        mine = left[k]
        same = pull(mine.astype(BF16), spread(mine), rhs, [row(a) for a in range(3)], NEAR_CORE)
        for a in range(3):
            acc[k, a] = same[a]
        return carry

    lax.fori_loop(0, NB, step, 0)
    for k in range(NB):
        forces[:, k * BLK : (k + 1) * BLK] = total_rows(acc, k)


def far_kernel(rec_t, cells, centers, left_ref, so_far, forces, left, acc, sem):
    bring = pltpu.make_async_copy(left_ref, left, sem)
    bring.start()
    far_rhs = []
    for half in range(2):
        rows = jnp.zeros((8, BLK), F32)
        last = jnp.zeros((8, BLK), F32)
        for i in range(4):
            at = (half * 4 + i) * 32
            tile = rec_t[at : at + 8, :]
            for x in range(1, NX):
                tile = tile + rec_t[at + 8 * x : at + 8 * x + 8, :]
            low = jnp.where((lanes(8) >= 64) & (lanes(8) < 96), tile, 0.0)
            high = jnp.where(lanes(8) >= 96, tile, 0.0)
            rows = rows + (pltpu.roll(low, (32 * i + 64) % 128, 1) if i != 2 else low)
            last = last + (pltpu.roll(high, (32 * i + 32) % 128, 1) if i != 3 else high)
        far_rhs.append(right_side(jnp.concatenate([rows, last[0:1, :], jnp.zeros((7, BLK), F32)], axis=0)))

    bring.wait()

    def step(k, carry):
        cell = cells[k]
        mine = left[k]
        side, here = mine.astype(BF16), spread(mine)
        one = pull(side, here, far_rhs[0], [centers[a : a + 1, 0:BLK] for a in range(3)], FAR_CORE, cell)
        two = pull(side, here, far_rhs[1], [centers[a : a + 1, BLK:] for a in range(3)], FAR_CORE, cell - BLK)
        for a in range(3):
            acc[k, a] = one[a] + two[a]
        return carry

    lax.fori_loop(0, NB, step, 0)
    for k in range(NB):
        cols = slice(k * BLK, (k + 1) * BLK)
        forces[:, cols] = so_far[:, cols] + total_rows(acc, k)


def gather_blocks(rec_x, rec_z, blocks, sems):
    copies = [
        pltpu.make_async_copy(rec_x, blocks.at[pl.ds(0, LOCAL)], sems.at[0]),
        pltpu.make_async_copy(rec_z, blocks.at[pl.ds(LOCAL, NZ * ROWS)], sems.at[1]),
    ]
    for copy in copies:
        copy.start()
    return copies


def add_pairs(tasks, blocks, left, acc):
    def pair_step(i, carry):
        for u in range(UNROLL):
            entry = tasks[UNROLL * i + u]
            base = entry & 4095
            k = (entry >> 12) & 15
            limit = jnp.where(entry >= PAD, 0, 9)
            apart = jnp.where(base >= LOCAL, NB, CAP)

            def row(r):
                return blocks[pl.ds(base + r * apart, 1), :]

            rhs = right_side(jnp.where(subs(16) < limit, outer_rows(row, True), 0.0))
            mine = left[k]
            near = pull(mine.astype(BF16), spread(mine), rhs, [row(a) for a in range(3)], NEAR_CORE)
            for a in range(3):
                acc[k, a] = acc[k, a] + near[a]
        return carry

    lax.fori_loop(0, (tasks[COUNT] + UNROLL - 1) // UNROLL, pair_step, 0)


def speeds(mobility, forces, tops):
    v = mobility[...] * forces[...]
    speed = jnp.sum(v * v, axis=0, keepdims=True)
    tops[...] = jnp.broadcast_to(jnp.max(speed, axis=1, keepdims=True), tops.shape)


def near_kernel(rec_x, rec_z, tasks, left_ref, so_far, mobility, forces, tops, blocks, left, acc, sems):
    copies = gather_blocks(rec_x, rec_z, blocks, sems)
    copies.append(pltpu.make_async_copy(left_ref, left, sems.at[2]))
    copies[2].start()
    acc[...] = jnp.zeros_like(acc)
    for copy in copies:
        copy.wait()
    add_pairs(tasks, blocks, left, acc)
    for k in range(NB):
        cols = slice(k * BLK, (k + 1) * BLK)
        forces[:, cols] = so_far[:, cols] + total_rows(acc, k)
    speeds(mobility, forces, tops)


def late_kernel(rec_x, rec_z, tasks, so_far, mobility, forces, tops, blocks, left, acc, sems):
    zz = lax.axis_index("z")
    for copy in gather_blocks(rec_x, rec_z, blocks, sems):
        copy.wait()

    def ready(k, carry):
        prepare(k, lambda r: blocks[pl.ds(LOCAL + zz * ROWS + r * NB + k, 1), :], left)
        for a in range(3):
            acc[k, a] = jnp.zeros((BLK, BLK), F32)
        return carry

    lax.fori_loop(0, NB, ready, 0)
    add_pairs(tasks, blocks, left, acc)
    for k in range(NB):
        cols = slice(k * BLK, (k + 1) * BLK)
        forces[:, cols] = so_far[:, cols] + total_rows(acc, k)
    speeds(mobility, forces, tops)


def step_kernel(tops, forces, mobility, out):
    best = jnp.max(jnp.max(tops[...], axis=0, keepdims=True), axis=1, keepdims=True)
    scale = STEP_LIMIT / (jnp.sqrt(best) + 1e-06)
    out[...] = scale * (mobility[...] * forces[...])


def shape(*dims, kind=F32):
    return jax.ShapeDtypeStruct(dims, kind)


def cost(flops):
    return pl.CostEstimate(flops=flops, bytes_accessed=10**6, transcendentals=0)


LEFT = (NB, BLK, BLK)
PARTS = (NB, 3, BLK, BLK)


def body(segments, pair_blocks, block_cells, mobility, cell_centers):
    params = pltpu.CompilerParams(vmem_limit_bytes=8 * 1024 * 1024)
    small = pltpu.CompilerParams(vmem_limit_bytes=4 * 1024 * 1024)
    seg_count = segments.shape[1]
    devices = 8 * NG * NX
    mob = mobility[None, :]
    packed, own = pl.pallas_call(
        pack_kernel,
        out_shape=(shape(NZ * ROWS, BLK), shape(ROWS, BLK)),
        in_specs=[VMEM, SMEM, VMEM],
        out_specs=(VMEM, VMEM),
        name="pack",
    )(segments, block_cells, pair_blocks.T)
    rec_z = lax.all_to_all(packed.reshape(NZ, ROWS, BLK), "z", 0, 0, tiled=True).reshape(NZ * ROWS, BLK)
    left, same = pl.pallas_call(
        own_kernel,
        out_shape=(shape(*LEFT), shape(3, seg_count)),
        in_specs=[VMEM],
        out_specs=(VMEM, VMEM),
        scratch_shapes=[pltpu.VMEM(PARTS, F32)],
        compiler_params=params,
        cost_estimate=cost(10**9),
        name="own",
    )(own)
    rec_z, left, same = lax.optimization_barrier((rec_z, left, same))
    column = pl.pallas_call(
        column_kernel,
        out_shape=shape(NG * NX * 8, BLK),
        grid=(1,),
        in_specs=[pl.BlockSpec((8, BLK), lambda i, s=s: ((s * ROWS + EXTRA) // 8, 0)) for s in range(NZ)],
        out_specs=pl.BlockSpec((NG * NX * 8, BLK), lambda i: (0, 0)),
        compiler_params=small,
        name="column",
    )(*([rec_z] * NZ))
    rec_t = lax.all_to_all(column.reshape(NG * NX, 8, BLK), ("y", "c", "x"), 0, 0, tiled=True)
    rec_t = rec_t.reshape(NG * NX * 8, BLK)

    def lists(rows):
        return [
            pltpu.VMEM((rows, BLK), jnp.int32),
            pltpu.SMEM((rows, BLK), jnp.int32),
            pltpu.SMEM((NX,), jnp.int32),
            pltpu.SemaphoreType.DMA,
        ]

    def exchange(number):
        send = pl.pallas_call(
            send_kernel,
            out_shape=shape(NX * SECT, BLK),
            in_specs=[SMEM, VMEM, ANY],
            out_specs=VMEM,
            scratch_shapes=lists(8) + [pltpu.VMEM((NZ * ROWS, BLK), F32), pltpu.SemaphoreType.DMA],
            compiler_params=small,
            name="send",
        )(number, rec_t, rec_z)
        rec_x = lax.all_to_all(send.reshape(NX, SECT, BLK), "x", 0, 0, tiled=True)
        tasks, rounds = pl.pallas_call(
            tasks_kernel,
            out_shape=(shape(TASKS + 128, kind=jnp.int32), shape(1, kind=jnp.int32)),
            in_specs=[SMEM, VMEM],
            out_specs=(SMEM, SMEM),
            scratch_shapes=lists(16),
            compiler_params=small,
            cost_estimate=cost(10**8),
            name="tasks",
        )(number, rec_t)
        return rec_x.reshape(NX * SECT, BLK), tasks, rounds

    blocks = pltpu.VMEM((LOCAL + NZ * ROWS, BLK), F32)
    sems = pltpu.SemaphoreType.DMA((3,))
    results = (shape(3, seg_count), shape(devices, BLK))
    rec_x, tasks, rounds = exchange(jnp.zeros((1,), jnp.int32))
    home = pl.pallas_call(
        far_kernel,
        out_shape=shape(3, seg_count),
        in_specs=[VMEM, SMEM, VMEM, ANY, VMEM],
        out_specs=VMEM,
        scratch_shapes=[pltpu.VMEM(LEFT, F32), pltpu.VMEM(PARTS, F32), pltpu.SemaphoreType.DMA],
        compiler_params=params,
        cost_estimate=cost(10**8),
        name="far",
    )(rec_t, block_cells, cell_centers, left, same)
    forces, tops = pl.pallas_call(
        near_kernel,
        out_shape=results,
        in_specs=[ANY, ANY, SMEM, ANY, VMEM, VMEM],
        out_specs=(VMEM, VMEM),
        scratch_shapes=[blocks, pltpu.VMEM(LEFT, F32), pltpu.VMEM(PARTS, F32), sems],
        compiler_params=params,
        name="near",
    )(rec_x, rec_z, tasks, left, home, mob)

    def more(carry):
        number, so_far, _ = carry
        rec_x, tasks, _ = exchange(number[None])
        forces, tops = pl.pallas_call(
            late_kernel,
            out_shape=results,
            in_specs=[ANY, ANY, SMEM, VMEM, VMEM],
            out_specs=(VMEM, VMEM),
            scratch_shapes=[blocks, pltpu.VMEM(LEFT, F32), pltpu.VMEM(PARTS, F32), sems],
            compiler_params=params,
            name="late",
        )(rec_x, rec_z, tasks, so_far, mob)
        return number + 1, forces, tops

    _, forces, tops = lax.while_loop(lambda c: c[0] < rounds[0], more, (jnp.ones((), jnp.int32), forces, tops))
    tops = lax.all_to_all(tops.reshape(devices, 1, BLK), ("y", "c", "z", "x"), 0, 0, tiled=True)
    displacement = pl.pallas_call(
        step_kernel,
        out_shape=shape(3, seg_count),
        in_specs=[VMEM, VMEM, VMEM],
        out_specs=VMEM,
        compiler_params=small,
        name="step",
    )(tops.reshape(devices, BLK), forces, mob)
    return forces, displacement


def solution(mesh):
    names = ("y", "c", "z", "x")
    fine = Mesh(mesh.devices.reshape(NG // 2, 2, NZ, NX), names)
    in_specs = (P(None, names), P(names, None), P(names), P(names), P())
    out_specs = (P(None, names), P(None, names))
    return jax.shard_map(body, mesh=fine, in_specs=in_specs, out_specs=out_specs, check_vma=False)
```

time: 100 us -> 87.6 us (0.88); the launches traced: 101 us -> 87.1 us
  blocking collectives: 45.8 us -> 34.3 us
  waiting for transfers between devices: 9.6 us -> 16.8 us
  Pallas kernels: 27.7 us -> 22 us
  local copies, waits for them, and re-layouts: 3.53 us -> 0.03 us
    all_to_all x2, blocking collectives: 45.8 us -> 34.3 us  [the longest x1 19.3 us: body(): lax.all_to_all(tops.reshape(devices, 1, BLK), ('y', 'c', 'z', 'x'), 0, 0,...]
    all_to_all x1, waiting for transfers between devices: 7.62 us -> 15 us  [body(): lax.all_to_all(packed.reshape(NZ, ROWS, BLK), 'z', 0, 0, tiled=True)]
    pallas_call x5 -> x7, Pallas kernels: 26.1 us -> 21.2 us  [the longest x1 5.27 us: body(): pl.pallas_call(near_kernel, out_shape=results, in_specs=[ANY, ANY, SMEM,...]
    broadcast_in_dim x3 -> x0, local copies, waits for them, and re-layouts: 2.35 us -> none  [the longest x1 1.35 us: body(): jnp.broadcast_to(column[None], (NG * NX, 8, BLK))]
  transfers between devices with their start and end apart: 2 -> 2, of which waited for: 2 -> 2; matrix products, arithmetic and copies ran while one was open for 0% -> 0% of each run, Pallas kernels for 7% -> 13%
where the time goes in v3:
time: 87.6 us; the launch traced here: 87.1 us
  blocking collectives  34.3 us (39%)
  Pallas kernels  22 us (25%)
  waiting for transfers between devices  16.8 us (19%)
  starting transfers between devices  12.6 us (14%)
    all_to_all x1, blocking collectives, body(): lax.all_to_all(tops.reshape(devices, 1, BLK), ('y', 'c', 'z', 'x'), 0, 0,...  19.3 us
    all_to_all x1, waiting for transfers between devices, body(): lax.all_to_all(packed.reshape(NZ, ROWS, BLK), 'z', 0, 0, tiled=True)  15 us
    all_to_all x1, blocking collectives, body(): lax.all_to_all(column.reshape(NG * NX, 8, BLK), ('y', 'c', 'x'), 0, 0, ti...  15 us
    all_to_all x1, starting transfers between devices, body(): lax.all_to_all(packed.reshape(NZ, ROWS, BLK), 'z', 0, 0, tiled=True)  9.15 us
    pallas_call x1, Pallas kernels, body(): pl.pallas_call(near_kernel, out_shape=results, in_specs=[ANY, ANY, SMEM,...  5.27 us
    pallas_call x1, Pallas kernels, body(): pl.pallas_call(own_kernel, out_shape=(shape(*LEFT), shape(3, seg_count)),...  5.02 us
    pallas_call x1, Pallas kernels, body(): pl.pallas_call(far_kernel, out_shape=shape(3, seg_count), in_specs=[VMEM,...  4.49 us
    all_to_all x1, starting transfers between devices, exchange(): rec_x = lax.all_to_all(send.reshape(NX, SECT, BLK), 'x', 0, 0, tiled=True)  3.47 us
  transfers between devices with their start and end apart: 2, of which 2 were waited for; matrix products, arithmetic and copies ran while one was open for 0% of the time, Pallas kernels for 13%

profile of v3, /device:TPU:1, one launch (start us, length us, event | category | flops | bytes accessed | tf_op | source)
XLA Modules:
  0.0 87.1 jit_solution(15194459596632033912)
XLA Ops:
  0.6 1.9 %pack.1 = (f32[1216,128]{1,0:T(8,128)}, f32[152,128]{1,0:T(8,128)}) custom-call(f32[9,2048]{1,0:T(8,128)} %seg.1, s32[16]{0:T(128)} %cells.3, s32[2,32]{1,0:T(2,128)} %bitcast.44), custom_call_target="tpu_custom_call" | custom-call | tf_op jit(solution)/shard_map/pack/pallas_call | solution.py:414
  2.5 9.1 %all-to-all-start.1 = ((f32[8,152,128]{2,1,0:T(8,128)}), f32[8,152,128]{2,1,0:T(8,128)S(1)}, u32[]{:S(2)}, u32[]{:S(2)}) async-start(f32[8,152,128]{2,1,0:T(8,128)} %bitcast.40), calls=%async_computation.1 | async-start | bytes 1245184 | tf_op jit(solution)/shard_map/all_to_all | solution.py:421
  11.7 0.0 copy-done.2
  11.7 5.0 %own.1 = (f32[16,128,128]{2,1,0:T(8,128)S(1)}, f32[3,2048]{1,0:T(4,128)S(1)}) custom-call(f32[152,128]{1,0:T(8,128)S(1)} %copy-done.2), custom_call_target="tpu_custom_call" | custom-call | flops 1000000000 | bytes 1000000 | tf_op jit(solution)/shard_map/own/pallas_call | solution.py:422
  16.7 15.0 %all-to-all-done.1 = f32[8,152,128]{2,1,0:T(8,128)S(1)} async-done(((f32[8,152,128]{2,1,0:T(8,128)}), f32[8,152,128]{2,1,0:T(8,128)S(1)}, u32[]{:S(2)}, u32[]{:S(2)}) %all-to-all-start.1) | async-done | bytes 622624 | tf_op jit(solution)/shard_map/all_to_all | solution.py:421
  31.8 0.1 column.1
  31.8 15.0 %all_to_all.26 = f32[32,8,128]{2,1,0:T(8,128)S(1)} all-to-all(f32[32,8,128]{2,1,0:T(8,128)S(1)} %bitcast.23), channel_id=1, replica_groups=mesh['y'=4,'c'=2,'z'=8,'x'=4] {'y','c','x'}, dimensions={0} | all-to-all | bytes 262144 | tf_op jit(solution)/shard_map/all_to_all | solution.py:442
  46.8 2.3 %send.2 = f32[864,128]{1,0:T(8,128)} custom-call(s32[1]{0:T(128)} %constant.2.clone.1.turn_no, f32[256,128]{1,0:T(8,128)S(1)} %bitcast.36, f32[1216,128]{1,0:T(8,128)S(1)} %bitcast.33), custom_call_target="tpu_custom_call" | custom-call | tf_op jit(solution)/shard_map/send/pallas_call | solution.py:454
  49.2 3.5 %all-to-all-start.3 = ((f32[4,216,128]{2,1,0:T(8,128)}), f32[4,216,128]{2,1,0:T(8,128)S(1)}, u32[]{:S(2)}, u32[]{:S(2)}) async-start(f32[4,216,128]{2,1,0:T(8,128)} %bitcast.9), calls=%async_computation.3 | async-start | bytes 884736 | tf_op jit(solution)/shard_map/all_to_all | solution.py:463
  52.6 0.0 copy-start
  52.7 0.0 copy-start.1
  52.7 2.2 %tasks.2 = (s32[2176]{0:T(1024)S(1)}, s32[1]{0:T(128)}) custom-call(s32[1]{0:T(128)} %constant.2.clone.1.turn_no, f32[256,128]{1,0:T(8,128)S(1)} %bitcast.37), custom_call_target="tpu_custom_call" | custom-call | flops 100000000 | bytes 1000000 | tf_op jit(solution)/shard_map/tasks/pallas_call | solution.py:464
  54.8 0.0 copy-done
  54.9 0.0 copy-done.1
  54.9 0.0 copy-start.4
  54.9 4.5 %far.1.so_far = f32[3,2048]{1,0:T(4,128)S(1)} custom-call(f32[256,128]{1,0:T(8,128)S(1)} %bitcast.38, s32[16]{0:T(128)S(1)} %copy-done.1, f32[3,256]{1,0:T(4,128)S(1)} %copy-done, f32[16,128,128]{2,1,0:T(8,128)S(1)} %get-tuple-element.60.left_ref, f32[3,2048]{1,0:T(4,128)S(1)} %get-tuple-element.61.so_far), custom_call_target="tpu_custom_call" | custom-call | flops 100000000 | bytes 1000000 | tf_op jit(solution)/shard_map/far/pallas_call | solution.py:480
  59.4 1.8 %all-to-all-done.3 = f32[4,216,128]{2,1,0:T(8,128)S(1)} async-done(((f32[4,216,128]{2,1,0:T(8,128)}), f32[4,216,128]{2,1,0:T(8,128)S(1)}, u32[]{:S(2)}, u32[]{:S(2)}) %all-to-all-start.3) | async-done | bytes 442400 | tf_op jit(solution)/shard_map/all_to_all | solution.py:463
  61.1 0.0 copy-done.4
  61.1 5.3 %near.1 = (f32[3,2048]{1,0:T(4,128)S(1)}, f32[256,128]{1,0:T(8,128)}) custom-call(f32[864,128]{1,0:T(8,128)S(1)} %bitcast.22, f32[1216,128]{1,0:T(8,128)S(1)} %bitcast.34, s32[2176]{0:T(1024)S(1)} %get-tuple-element.59.tasks, f32[16,128,128]{2,1,0:T(8,128)S(1)} %get-tuple-element.60.left_ref, f32[3,2048]{1,0:T(4,128)S(1)} %far.1.so_far, f32[1,2048]{1,0:T(1,128)S(1)} %bitcast.41), custom_call_target="tpu_custom_call" | custom-call | tf_op jit(solution)/shard_map/near/pallas_call | solution.py:490
  66.4 0.7 while.12
  67.1 0.0 copy-start.3
  67.1 19.3 %all_to_all.27 = f32[256,1,128]{2,1,0:T(1,128)S(1)} all-to-all(f32[256,1,128]{2,1,0:T(1,128)} %bitcast.43), channel_id=1, replica_groups=mesh['y'=4,'c'=2,'z'=8,'x'=4] {'y','c','z','x'}, dimensions={0} | all-to-all | bytes 262144 | tf_op jit(solution)/shard_map/all_to_all | solution.py:515
  86.3 0.0 copy-done.3
  86.3 0.7 step.1
  (1 shorter events, 0.0 us)
Async XLA Ops:
  2.5 9.2 %copy-start.2 = (f32[152,128]{1,0:T(8,128)S(1)}, f32[152,128]{1,0:T(8,128)}, u32[]{:S(2)}) copy-start(f32[152,128]{1,0:T(8,128)} %get-tuple-element.55.own) | copy-start | bytes 233476
  2.5 29.2 %all-to-all-start.1 = ((f32[8,152,128]{2,1,0:T(8,128)}), f32[8,152,128]{2,1,0:T(8,128)S(1)}, u32[]{:S(2)}, u32[]{:S(2)}) async-start(f32[8,152,128]{2,1,0:T(8,128)} %bitcast.40), calls=%async_computation.1 | async-start | bytes 1245184 | tf_op jit(solution)/shard_map/all_to_all | solution.py:421
  49.2 12.0 %all-to-all-start.3 = ((f32[4,216,128]{2,1,0:T(8,128)}), f32[4,216,128]{2,1,0:T(8,128)S(1)}, u32[]{:S(2)}, u32[]{:S(2)}) async-start(f32[4,216,128]{2,1,0:T(8,128)} %bitcast.9), calls=%async_computation.3 | async-start | bytes 884736 | tf_op jit(solution)/shard_map/all_to_all | solution.py:463
  52.6 2.2 %copy-start = (f32[3,256]{1,0:T(4,128)S(1)}, f32[3,256]{1,0:T(4,128)}, u32[]{:S(2)}) copy-start(f32[3,256]{1,0:T(4,128)} %centers.1) | copy-start | bytes 9220
  52.7 2.2 %copy-start.1 = (s32[16]{0:T(128)S(1)}, s32[16]{0:T(128)}, u32[]{:S(2)}) copy-start(s32[16]{0:T(128)} %cells.3) | copy-start | bytes 196
  54.9 6.3 %copy-start.4 = (f32[2048]{0:T(1024)S(1)}, f32[2048]{0:T(1024)}, u32[]{:S(2)}) copy-start(f32[2048]{0:T(1024)} %param.10) | copy-start | bytes 24580
  67.1 19.3 %copy-start.3 = (f32[3,2048]{1,0:T(4,128)}, f32[3,2048]{1,0:T(4,128)S(1)}, u32[]{:S(2)}) copy-start(f32[3,2048]{1,0:T(4,128)S(1)} %get-tuple-element.52.forces) | copy-start | bytes 73732

commit v4 on v3

v4 whole, which is shorter than its diff:
```python
import jax
import jax.numpy as jnp
from jax import lax
from jax.experimental import pallas as pl
from jax.experimental.pallas import tpu as pltpu
from jax.sharding import Mesh
from jax.sharding import PartitionSpec as P

NEAR_CORE = 0.25
FAR_CORE = 1.0
STEP_LIMIT = 0.5
BLK = 128
NB = 16
NZ = 8
NX = 4
NG = 8
EXTRA = 9 * NB
ROWS = EXTRA + 8
CAP = 24
SECT = 9 * CAP
LOCAL = NX * SECT
TASKS = 2048
COUNT = TASKS + 64
UNROLL = 4
PAD = 1 << 16
F32 = jnp.float32
BF16 = jnp.bfloat16
VMEM = pl.BlockSpec(memory_space=pltpu.VMEM)
SMEM = pl.BlockSpec(memory_space=pltpu.SMEM)
NT = (((1,), (1,)), ((), ()))


def lanes(rows):
    return lax.broadcasted_iota(jnp.int32, (rows, BLK), 1)


def subs(rows):
    return lax.broadcasted_iota(jnp.int32, (rows, BLK), 0)


def split(x):
    one = x.astype(BF16)
    rest = x - one.astype(F32)
    two = rest.astype(BF16)
    three = (rest - two.astype(F32)).astype(BF16)
    return one, two, three


def pack_kernel(seg, cells, pairs, packed, out):
    for k in range(NB):
        cols = slice(k * BLK, (k + 1) * BLK)
        out[pl.ds(k, 8, stride=NB), :] = seg[0:8, cols]
        out[8 * NB + k : 8 * NB + k + 1, :] = seg[8:9, cols]
    row = subs(NB)
    cell = jnp.zeros((NB, BLK), jnp.int32)
    for k in range(NB):
        cell = jnp.where(row == k, cells[k] & 31, cell)
    hot = (lanes(NB) == cell + 64).astype(F32)
    hot_last = (lanes(NB) == cell + 96).astype(F32)
    rows = []
    for q in range(3):
        for r in range(3):
            outer = out[(6 + q) * NB : (7 + q) * NB, :] * out[(3 + r) * NB : (4 + r) * NB, :]
            total = jnp.sum(outer, axis=1, keepdims=True)
            rows.append(jnp.sum(total * (hot_last if q + r == 4 else hot), axis=0, keepdims=True))
    out[EXTRA : EXTRA + 1, :] = rows[0] + rows[8]
    for r in range(1, 8):
        out[EXTRA + r : EXTRA + r + 1, :] = rows[r]
    out[EXTRA : EXTRA + 2, 0:32] = pairs[...].astype(F32)
    whole = out[...]
    for copy in range(NZ):
        packed[copy * ROWS : (copy + 1) * ROWS, :] = whole


def column_kernel(*refs):
    out = refs[NZ]
    lane = lanes(8)
    first = jnp.concatenate([ref[0:1, :] for ref in refs[:NZ]], axis=0)
    second = jnp.concatenate([ref[1:2, :] for ref in refs[:NZ]], axis=0)
    total = refs[0][...]
    for ref in refs[1:NZ]:
        total = total + ref[...]
    tile = jnp.where(lane < 32, first, jnp.where(lane < 64, pltpu.roll(second, 32, 1), total))
    for copy in range(NG * NX):
        out[8 * copy : 8 * copy + 8, :] = tile


def group_pairs(rec_t):
    g = lax.axis_index("y") * 2 + lax.axis_index("c")
    lane = lanes(8)
    a = jnp.zeros((8, BLK), F32)
    b = jnp.zeros((8, BLK), F32)
    for x in range(NX):
        part = rec_t[pl.ds(pl.multiple_of(g * 32 + x * 8, 8), 8), :]
        one = jnp.where(lane < 32, part, 0.0)
        two = jnp.where((lane >= 32) & (lane < 64), part, 0.0)
        a = a + (pltpu.roll(one, 32 * x, 1) if x else one)
        b = b + (pltpu.roll(two, (32 * x + 96) % 128, 1) if x != 1 else two)
    return a.astype(jnp.int32), b.astype(jnp.int32)


def list_hits(hit, code, lst, smem, sem):
    rows = hit.shape[0]
    hits = hit.astype(F32)
    hot = jnp.concatenate([hits, jnp.zeros((16 - rows, BLK), F32)], axis=0) if rows < 16 else hits
    hot = hot.astype(BF16)
    sq_row, sq_lane = subs(BLK), lanes(BLK)
    inside = jnp.dot(hot, (sq_row < sq_lane).astype(BF16), preferred_element_type=F32)
    totals = jnp.dot(hot, jnp.ones((BLK, BLK), BF16), preferred_element_type=F32)
    before = jnp.zeros((16, BLK), F32)
    running = jnp.zeros((1, BLK), F32)
    for s in range(rows):
        before = jnp.where(subs(16) == s, running, before)
        running = running + totals[s : s + 1, :]
    count = jnp.max(running).astype(jnp.int32)
    rank = jnp.where(hits > 0.0, (inside + before)[0:rows, :], -1.0)
    code = code.astype(F32)

    def listing(chunk, carry):
        slot = (sq_row + chunk * BLK).astype(F32)
        found = jnp.zeros((BLK, BLK), F32)
        for c in range(rows):
            found = found + jnp.where(rank[c : c + 1, :] == slot, code[c : c + 1, :], 0.0)
        lst[pl.ds(chunk, 1), :] = jnp.sum(found.T, axis=0, keepdims=True).astype(jnp.int32)
        return carry

    listing(0, 0)
    lax.fori_loop(1, (count + BLK - 1) // BLK, listing, 0)
    copy = pltpu.make_async_copy(lst, smem, sem)
    copy.start()
    return copy, count


def send_kernel(turn_no, rec_t, rec_z, send, lst, smem, cnt, sem):
    zz = lax.axis_index("z")
    xx = lax.axis_index("x")
    rnd = turn_no[0]
    ai, bi = group_pairs(rec_t)
    own_a, own_b = ai >> 4, bi >> 4
    xa, xb = own_a & 3, own_b & 3
    to_a = ((own_a >> 2) == zz) & (xa != xx) & (xb == xx)
    to_b = ((own_b >> 2) == zz) & (xb != xx) & (xa == xx)
    code = jnp.where(to_a, xa * 512 + bi, xb * 512 + ai)
    copy, count = list_hits(to_a | to_b, code, lst, smem, sem)
    send[...] = jnp.zeros_like(send)
    for x in range(NX):
        cnt[x] = 0
    copy.wait()

    def deliver(i, carry):
        entry = smem[i >> 7, i & 127]
        f = entry & 511
        x = entry >> 9
        slot = cnt[x] - rnd * CAP
        cnt[x] = cnt[x] + 1

        @pl.when((slot >= 0) & (slot < CAP))
        def _():
            source = (f >> 6) * ROWS + (f & 15)
            target = x * SECT + slot
            send[pl.ds(target, 8, stride=CAP), :] = rec_z[pl.ds(source, 8, stride=NB), :]
            send[pl.ds(target + 8 * CAP, 1), :] = rec_z[pl.ds(source + 8 * NB, 1), :]

        return carry

    lax.fori_loop(0, count, deliver, 0)


def rounds_needed(ai, bi):
    own_a, own_b = ai >> 4, bi >> 4
    owner, column = [], []
    for here, there in ((own_a, own_b), (own_b, own_a)):
        for i in range(8):
            owner.append((subs(32) == here[i : i + 1, :]).astype(BF16))
            column.append((subs(16) == (there[i : i + 1, :] & 3)).astype(BF16))
    owner, column = jnp.concatenate(owner, axis=1), jnp.concatenate(column, axis=1)
    need = lax.dot_general(owner, column, NT, preferred_element_type=F32)
    r32 = lax.broadcasted_iota(jnp.int32, (32, 16), 0)
    c32 = lax.broadcasted_iota(jnp.int32, (32, 16), 1)
    longest = jnp.max(jnp.where((r32 & 3) == c32, 0.0, need)).astype(jnp.int32)
    return (longest + CAP - 1) // CAP


def list_tasks(rec_t, lst, smem, sem):
    me = lax.axis_index("z") * NX + lax.axis_index("x")
    ai, bi = group_pairs(rec_t)
    fa, fb = (ai >> 4) == me, (bi >> 4) == me
    swapped = (bi & 15) * 512 + ai
    hits = jnp.concatenate([(fa | fb).astype(F32), (fa & fb).astype(F32)], axis=0)
    code = jnp.concatenate([jnp.where(fa, (ai & 15) * 512 + bi, swapped), swapped], axis=0)
    return list_hits(hits > 0.0, code, lst, smem, sem)


def place_tasks(rnd, count, tasks, smem, cnt):
    xx = lax.axis_index("x")
    for x in range(NX):
        cnt[x] = 0

    def receive(i, at):
        entry = smem[i >> 7, i & 127]
        f = entry & 511
        column = (f >> 4) & 3
        here = column == xx
        slot = cnt[column] - rnd * CAP
        cnt[column] = cnt[column] + 1
        base = jnp.where(here, LOCAL + (f >> 6) * ROWS + (f & 15), column * SECT + slot)
        use = jnp.where(here, rnd == 0, (slot >= 0) & (slot < CAP))
        tasks[at] = base | ((entry >> 9) << 12)
        return at + use.astype(jnp.int32)

    used = lax.fori_loop(0, count, receive, 0)
    for u in range(8):
        tasks[used + u] = PAD
    tasks[COUNT] = used


def tasks_kernel(turn_no, rec_t, tasks, lst, smem, cnt, sem):
    copy, count = list_tasks(rec_t, lst, smem, sem)
    copy.wait()
    place_tasks(turn_no[0], count, tasks, smem, cnt)


def outer_rows(row, symmetric):
    s = subs(16)
    t = [jnp.broadcast_to(row(3 + r), (16, BLK)) for r in range(3)]
    b = [jnp.broadcast_to(row(6 + q), (16, BLK)) for q in range(3)]

    def slow(v):
        return jnp.where(s < 3, v[0], jnp.where(s < 6, v[1], v[2]))

    def fast(v):
        first = (s == 0) | (s == 3) | (s == 6)
        return jnp.where(first, v[0], jnp.where((s == 1) | (s == 4) | (s == 7), v[1], v[2]))

    o = slow(b) * fast(t)
    return o + 0.5 * (fast(b) * slow(t)) if symmetric else o


def other_side(rows, points):
    one, two, three = [x.astype(F32) for x in split(rows)]
    points = jnp.concatenate(points + [jnp.zeros((29, BLK), F32)], axis=0)
    return jnp.concatenate([one, two, one, three, two, one, points], axis=0).T


def own_side(row):
    o = jnp.where(subs(16) < 9, outer_rows(row, False), 0.0)
    one, two, three = split(o)
    return jnp.concatenate([one, one, two, one, two, three, jnp.zeros((32, BLK), BF16)], axis=0)


def own_sides(own, sides):
    for k in range(NB):
        sides[k] = own_side(lambda r: own[r * NB + k : r * NB + k + 1, :])


def spread(turned):
    return [jnp.broadcast_to(turned[:, 96 + a : 97 + a], (BLK, BLK)) for a in range(3)]


def fold(v):
    total = v[0:8, :]
    for i in range(1, BLK // 8):
        total = total + v[8 * i : 8 * i + 8, :]
    return total


def pull(other, there, mine, here, core, drop=None):
    c = jnp.dot(other, mine, preferred_element_type=F32)
    if drop is not None:
        c = jnp.where(subs(BLK) == drop, 0.0, c)
    d = [here[a] - there[a] for a in range(3)]
    inv = lax.rsqrt(d[0] * d[0] + d[1] * d[1] + (d[2] * d[2] + core))
    w = c * (inv * inv * inv)
    return [fold(w * d[a]) for a in range(3)]


def point_columns():
    row = lax.broadcasted_iota(jnp.int32, (BLK, 3 * BLK), 0) - 96
    axis = lax.broadcasted_iota(jnp.int32, (BLK, 3 * BLK), 1) // BLK
    return ((row == axis) | (row == axis + 3) | (row == axis + 6)).astype(BF16)


def source_pull(row, limit, mine, here, columns):
    rows = jnp.where(subs(16) < limit, outer_rows(row, True), 0.0)
    one, two, three = split(rows)
    s = subs(16)
    p = [row(a) for a in range(3)]
    points = jnp.concatenate(p + p + p + [jnp.zeros((7, BLK), F32)], axis=0)
    p1, p2, p3 = [x.astype(F32) for x in split(points)]
    pieces = jnp.where(s < 3, p1, jnp.where(s < 6, p2, p3)).astype(BF16)
    side = jnp.concatenate([one, two, one, three, two, one, pieces, jnp.zeros((16, BLK), BF16)], axis=0).T
    spots = jnp.dot(side, columns, preferred_element_type=F32)
    there = [spots[:, a * BLK : (a + 1) * BLK] for a in range(3)]
    return pull(side, there, mine, here, NEAR_CORE)


def write_forces(acc, forces, so_far=None):
    for k in range(NB):
        cols = slice(k * BLK, (k + 1) * BLK)
        rows = jnp.concatenate([jnp.sum(acc[k, a], axis=0, keepdims=True) for a in range(3)], axis=0)
        forces[:, cols] = rows if so_far is None else so_far[:, cols] + rows


def own_kernel(own, forces, acc):
    columns = point_columns()

    def step(i, carry):
        for u in range(4):
            k = 4 * i + u

            def row(r):
                return own[pl.ds(r * NB + k, 1), :]

            same = source_pull(row, 9, own_side(row), [row(a) for a in range(3)], columns)
            for a in range(3):
                acc[k, a] = same[a]
        return carry

    lax.fori_loop(0, NB // 4, step, 0)
    write_forces(acc, forces)


def far_kernel(own, rec_t, cells, centers, so_far, forces, rounds, tasks, there, sides, acc, lst, smem, cnt, sem):
    copy, count = list_tasks(rec_t, lst, smem, sem)
    rounds[0] = rounds_needed(*group_pairs(rec_t))
    others = []
    for half in range(2):
        rows = jnp.zeros((8, BLK), F32)
        last = jnp.zeros((8, BLK), F32)
        for i in range(4):
            at = (half * 4 + i) * 32
            tile = rec_t[at : at + 8, :]
            for x in range(1, NX):
                tile = tile + rec_t[at + 8 * x : at + 8 * x + 8, :]
            low = jnp.where((lanes(8) >= 64) & (lanes(8) < 96), tile, 0.0)
            high = jnp.where(lanes(8) >= 96, tile, 0.0)
            rows = rows + (pltpu.roll(low, (32 * i + 64) % 128, 1) if i != 2 else low)
            last = last + (pltpu.roll(high, (32 * i + 32) % 128, 1) if i != 3 else high)
        rows = jnp.concatenate([rows, last[0:1, :], jnp.zeros((7, BLK), F32)], axis=0)
        cols = slice(half * BLK, (half + 1) * BLK)
        turned = other_side(rows, [centers[a : a + 1, cols] for a in range(3)])
        others.append(turned.astype(BF16))
        for a, point in enumerate(spread(turned)):
            there[half, a] = point
    own_sides(own, sides)

    def step(i, carry):
        for u in range(2):
            k = 2 * i + u
            here = [own[pl.ds(a * NB + k, 1), :] for a in range(3)]
            parts = [
                pull(others[h], [there[h, a] for a in range(3)], sides[k], here, FAR_CORE, cells[k] - h * BLK)
                for h in range(2)
            ]
            for a in range(3):
                acc[k, a] = parts[0][a] + parts[1][a]
        return carry

    lax.fori_loop(0, NB // 2, step, 0)
    write_forces(acc, forces, so_far)
    copy.wait()
    place_tasks(0, count, tasks, smem, cnt)


def near_kernel(rec_x, rec_z, tasks, own, so_far, mobility, forces, tops, sides, acc):
    acc[...] = jnp.zeros_like(acc)
    own_sides(own, sides)
    columns = point_columns()

    def pair_step(i, carry):
        for u in range(UNROLL):
            entry = tasks[UNROLL * i + u]
            base = entry & 4095
            k = (entry >> 12) & 15
            here = base >= LOCAL
            at_z = jnp.where(here, base - LOCAL, 0)
            at_x = jnp.where(here, 0, base)

            def row(r):
                return jnp.where(here, rec_z[pl.ds(at_z + r * NB, 1), :], rec_x[pl.ds(at_x + r * CAP, 1), :])

            mine = [own[pl.ds(a * NB + k, 1), :] for a in range(3)]
            near = source_pull(row, jnp.where(entry >= PAD, 0, 9), sides[k], mine, columns)
            for a in range(3):
                acc[k, a] = acc[k, a] + near[a]
        return carry

    lax.fori_loop(0, (tasks[COUNT] + UNROLL - 1) // UNROLL, pair_step, 0)
    write_forces(acc, forces, so_far)
    v = mobility[...] * forces[...]
    speed = jnp.sum(v * v, axis=0, keepdims=True)
    tops[...] = jnp.broadcast_to(jnp.max(speed, axis=1, keepdims=True), tops.shape)


def step_kernel(tops, forces, mobility, out):
    best = jnp.max(jnp.max(tops[...], axis=0, keepdims=True), axis=1, keepdims=True)
    scale = STEP_LIMIT / (jnp.sqrt(best) + 1e-06)
    out[...] = scale * (mobility[...] * forces[...])


def shape(*dims, kind=F32):
    return jax.ShapeDtypeStruct(dims, kind)


def cost(flops):
    return pl.CostEstimate(flops=flops, bytes_accessed=1, transcendentals=0)


def body(segments, pair_blocks, block_cells, mobility, cell_centers):
    small = pltpu.CompilerParams(vmem_limit_bytes=6 * 1024 * 1024)
    seg_count = segments.shape[1]
    devices = 8 * NG * NX
    mob = mobility[None, :]
    packed, own = pl.pallas_call(
        pack_kernel,
        out_shape=(shape(NZ * ROWS, BLK), shape(ROWS, BLK)),
        in_specs=[VMEM, SMEM, VMEM],
        out_specs=(VMEM, VMEM),
        name="pack",
    )(segments, block_cells, pair_blocks.T)
    rec_z = lax.all_to_all(packed.reshape(NZ, ROWS, BLK), "z", 0, 0, tiled=True).reshape(NZ * ROWS, BLK)
    sides = pltpu.VMEM((NB, BLK, BLK), BF16)
    sums = pltpu.VMEM((NB, 3, 8, BLK), F32)
    same = pl.pallas_call(
        own_kernel,
        out_shape=shape(3, seg_count),
        in_specs=[VMEM],
        out_specs=VMEM,
        scratch_shapes=[sums],
        compiler_params=small,
        cost_estimate=cost(10**9),
        name="own",
    )(own)
    rec_z, same = lax.optimization_barrier((rec_z, same))
    column = pl.pallas_call(
        column_kernel,
        out_shape=shape(NG * NX * 8, BLK),
        grid=(1,),
        in_specs=[pl.BlockSpec((8, BLK), lambda i, s=s: ((s * ROWS + EXTRA) // 8, 0)) for s in range(NZ)],
        out_specs=pl.BlockSpec((NG * NX * 8, BLK), lambda i: (0, 0)),
        compiler_params=small,
        name="column",
    )(*([rec_z] * NZ))
    rec_t = lax.all_to_all(column.reshape(NG * NX, 8, BLK), ("y", "c", "x"), 0, 0, tiled=True)
    rec_t = rec_t.reshape(NG * NX * 8, BLK)

    def lists(rows):
        return [
            pltpu.VMEM((rows, BLK), jnp.int32),
            pltpu.SMEM((rows, BLK), jnp.int32),
            pltpu.SMEM((NX,), jnp.int32),
            pltpu.SemaphoreType.DMA,
        ]

    def to_send(number):
        return pl.pallas_call(
            send_kernel,
            out_shape=shape(NX * SECT, BLK),
            in_specs=[SMEM, VMEM, VMEM],
            out_specs=VMEM,
            scratch_shapes=lists(8),
            compiler_params=small,
            name="send",
        )(number, rec_t, rec_z).reshape(NX, SECT, BLK)

    def to_do(number):
        return pl.pallas_call(
            tasks_kernel,
            out_shape=shape(TASKS + 128, kind=jnp.int32),
            in_specs=[SMEM, VMEM],
            out_specs=SMEM,
            scratch_shapes=lists(16),
            compiler_params=small,
            cost_estimate=cost(1),
            name="tasks",
        )(number, rec_t)

    def add_near(rec_x, tasks, so_far):
        return pl.pallas_call(
            near_kernel,
            out_shape=(shape(3, seg_count), shape(devices, BLK)),
            in_specs=[VMEM, VMEM, SMEM, VMEM, VMEM, VMEM],
            out_specs=(VMEM, VMEM),
            scratch_shapes=[sides, sums],
            compiler_params=small,
            name="near",
        )(rec_x, rec_z, tasks, own, so_far, mob)

    first = jnp.zeros((1,), jnp.int32)
    rec_x = lax.all_to_all(to_send(first), "x", 0, 0, tiled=True)
    home, rounds, tasks = pl.pallas_call(
        far_kernel,
        out_shape=(shape(3, seg_count), shape(1, kind=jnp.int32), shape(TASKS + 128, kind=jnp.int32)),
        in_specs=[VMEM, VMEM, SMEM, VMEM, VMEM],
        out_specs=(VMEM, SMEM, SMEM),
        scratch_shapes=[pltpu.VMEM((2, 3, BLK, BLK), F32), sides, sums] + lists(16),
        compiler_params=small,
        cost_estimate=cost(1),
        name="far",
    )(own, rec_t, block_cells, cell_centers, same)

    def more(carry):
        left, so_far = carry
        number = left - 1
        send = to_send(number)
        late = to_do(number)
        x = lax.axis_index("x")
        got = jnp.zeros_like(send)
        for k in range(1, NX):
            part = lax.dynamic_index_in_dim(send, (x + k) % NX, 0, keepdims=True)
            part = lax.ppermute(part, "x", [(i, (i + k) % NX) for i in range(NX)])
            got = lax.dynamic_update_slice_in_dim(got, part, (x + NX - k) % NX, 0)
        return number, add_near(got.reshape(NX * SECT, BLK), late, so_far)[0]

    _, home = lax.while_loop(lambda c: c[0][0] > 1, more, (rounds, home))
    forces, tops = add_near(rec_x.reshape(NX * SECT, BLK), tasks, home)
    tops = lax.all_to_all(tops.reshape(devices, 1, BLK), ("y", "c", "z", "x"), 0, 0, tiled=True)
    displacement = pl.pallas_call(
        step_kernel,
        out_shape=shape(3, seg_count),
        in_specs=[VMEM, VMEM, VMEM],
        out_specs=VMEM,
        compiler_params=small,
        name="step",
    )(tops.reshape(devices, BLK), forces, mob)
    return forces, displacement


def solution(mesh):
    names = ("y", "c", "z", "x")
    fine = Mesh(mesh.devices.reshape(NG // 2, 2, NZ, NX), names)
    in_specs = (P(None, names), P(names, None), P(names), P(names), P())
    out_specs = (P(None, names), P(None, names))
    return jax.shard_map(body, mesh=fine, in_specs=in_specs, out_specs=out_specs, check_vma=False)
```

time: 87.6 us -> 83.8 us (0.957)
  Pallas kernels: 22 us -> 14.5 us
  waiting for transfers between devices: 16.8 us -> 21.6 us
  blocking collectives: 34.3 us -> 33.2 us
    pallas_call x5 -> x4, Pallas kernels: 19.3 us -> 11.8 us  [the longest x1 4.57 us: body(): pl.pallas_call(far_kernel, out_shape=(shape(3, seg_count), shape(1, kind=...]
    all_to_all x1, waiting for transfers between devices: 15 us -> 18.4 us  [body(): lax.all_to_all(packed.reshape(NZ, ROWS, BLK), 'z', 0, 0, tiled=True)]
    all_to_all x1, waiting for transfers between devices: 1.76 us -> 3.21 us  [body(): rec_x = lax.all_to_all(to_send(first), 'x', 0, 0, tiled=True)]
    all_to_all x1, blocking collectives: 19.3 us -> 18.2 us  [body(): lax.all_to_all(tops.reshape(devices, 1, BLK), ('y', 'c', 'z', 'x'), 0, 0,...]
  transfers between devices with their start and end apart: 2 -> 2, of which waited for: 2 -> 2; matrix products, arithmetic and copies ran while one was open for 0% -> 0% of each run, Pallas kernels for 13% -> 7%
where the time goes in v4:
time: 83.8 us; the launch traced here: 83.3 us
  blocking collectives  33.2 us (40%)
  waiting for transfers between devices  21.6 us (26%)
  Pallas kernels  14.5 us (17%)
  starting transfers between devices  12.5 us (15%)
    all_to_all x1, waiting for transfers between devices, body(): lax.all_to_all(packed.reshape(NZ, ROWS, BLK), 'z', 0, 0, tiled=True)  18.4 us
    all_to_all x1, blocking collectives, body(): lax.all_to_all(tops.reshape(devices, 1, BLK), ('y', 'c', 'z', 'x'), 0, 0,...  18.2 us
    all_to_all x1, blocking collectives, body(): lax.all_to_all(column.reshape(NG * NX, 8, BLK), ('y', 'c', 'x'), 0, 0, ti...  15 us
    all_to_all x1, starting transfers between devices, body(): lax.all_to_all(packed.reshape(NZ, ROWS, BLK), 'z', 0, 0, tiled=True)  9.01 us
    pallas_call x1, Pallas kernels, body(): pl.pallas_call(far_kernel, out_shape=(shape(3, seg_count), shape(1, kind=...  4.57 us
    all_to_all x1, starting transfers between devices, body(): rec_x = lax.all_to_all(to_send(first), 'x', 0, 0, tiled=True)  3.47 us
    pallas_call x1, Pallas kernels, add_near(): pl.pallas_call(near_kernel, out_shape=(shape(3, seg_count), shape(devices...  3.44 us
    all_to_all x1, waiting for transfers between devices, body(): rec_x = lax.all_to_all(to_send(first), 'x', 0, 0, tiled=True)  3.21 us
  transfers between devices with their start and end apart: 2, of which 2 were waited for; matrix products, arithmetic and copies ran while one was open for 0% of the time, Pallas kernels for 7%

profile of v4, /device:TPU:1, one launch (start us, length us, event | category | flops | bytes accessed | tf_op | source)
XLA Modules:
  0.0 83.3 jit_solution(2810818647012443903)
XLA Ops:
  0.6 1.9 %pack.1 = (f32[1216,128]{1,0:T(8,128)}, f32[152,128]{1,0:T(8,128)S(1)}) custom-call(f32[9,2048]{1,0:T(8,128)} %seg.1, s32[16]{0:T(128)} %cells.3, s32[2,32]{1,0:T(2,128)} %bitcast.41), custom_call_target="tpu_custom_call" | custom-call | tf_op jit(solution)/shard_map/pack/pallas_call | solution.py:414
  2.5 9.0 %all-to-all-start = ((f32[8,152,128]{2,1,0:T(8,128)}), f32[8,152,128]{2,1,0:T(8,128)S(1)}, u32[]{:S(2)}, u32[]{:S(2)}) async-start(f32[8,152,128]{2,1,0:T(8,128)} %bitcast.39), calls=%async_computation | async-start | bytes 1245184 | tf_op jit(solution)/shard_map/all_to_all | solution.py:421
  11.5 1.6 %own.1.so_far = f32[3,2048]{1,0:T(4,128)S(1)} custom-call(f32[152,128]{1,0:T(8,128)S(1)} %get-tuple-element.214.own), custom_call_target="tpu_custom_call" | custom-call | flops 1000000000 | bytes 1 | tf_op jit(solution)/shard_map/own/pallas_call | solution.py:424
  13.2 18.4 %all-to-all-done = f32[8,152,128]{2,1,0:T(8,128)S(1)} async-done(((f32[8,152,128]{2,1,0:T(8,128)}), f32[8,152,128]{2,1,0:T(8,128)S(1)}, u32[]{:S(2)}, u32[]{:S(2)}) %all-to-all-start) | async-done | bytes 622624 | tf_op jit(solution)/shard_map/all_to_all | solution.py:421
  31.6 0.1 column.1
  31.7 15.0 %all_to_all.20 = f32[32,8,128]{2,1,0:T(8,128)S(1)} all-to-all(f32[32,8,128]{2,1,0:T(8,128)S(1)} %bitcast.23), channel_id=1, replica_groups=mesh['y'=4,'c'=2,'z'=8,'x'=4] {'y','c','x'}, dimensions={0} | all-to-all | bytes 262144 | tf_op jit(solution)/shard_map/all_to_all | solution.py:444
  46.7 2.1 %send.8 = f32[864,128]{1,0:T(8,128)} custom-call(s32[1]{0:T(128)} %constant.134.clone.1.turn_no, f32[256,128]{1,0:T(8,128)S(1)} %bitcast.36, f32[1216,128]{1,0:T(8,128)S(1)} %bitcast.34), custom_call_target="tpu_custom_call" | custom-call | tf_op jit(solution)/shard_map/send/pallas_call | solution.py:456
  48.8 0.0 copy-start.1
  48.9 0.0 copy-start.2
  48.9 3.5 %all-to-all-start.2 = ((f32[4,216,128]{2,1,0:T(8,128)}), f32[4,216,128]{2,1,0:T(8,128)S(1)}, u32[]{:S(2)}, u32[]{:S(2)}) async-start(f32[4,216,128]{2,1,0:T(8,128)} %bitcast.8), calls=%async_computation.2 | async-start | bytes 884736 | tf_op jit(solution)/shard_map/all_to_all | solution.py:490
  52.3 0.0 copy-done.1
  52.4 0.0 copy-done.2
  52.4 0.0 copy-start.3
  52.4 4.6 %far.1 = (f32[3,2048]{1,0:T(4,128)S(1)}, s32[1]{0:T(128)}, s32[2176]{0:T(1024)S(1)}) custom-call(f32[152,128]{1,0:T(8,128)S(1)} %get-tuple-element.214.own, f32[256,128]{1,0:T(8,128)S(1)} %bitcast.37, s32[16]{0:T(128)S(1)} %copy-done.2, f32[3,256]{1,0:T(4,128)S(1)} %copy-done.1, f32[3,2048]{1,0:T(4,128)S(1)} %own.1.so_far), custom_call_target="tpu_custom_call" | custom-call | flops 1 | bytes 1 | tf_op jit(solution)/shard_map/far/pallas_call | solution.py:491
  57.0 0.0 copy-done.3
  57.0 0.7 while.14
  57.6 3.2 %all-to-all-done.2 = f32[4,216,128]{2,1,0:T(8,128)S(1)} async-done(((f32[4,216,128]{2,1,0:T(8,128)}), f32[4,216,128]{2,1,0:T(8,128)S(1)}, u32[]{:S(2)}, u32[]{:S(2)}) %all-to-all-start.2) | async-done | bytes 442400 | tf_op jit(solution)/shard_map/all_to_all | solution.py:490
  60.8 3.4 %near.8 = (f32[3,2048]{1,0:T(4,128)}, f32[256,128]{1,0:T(8,128)S(1)}) custom-call(f32[864,128]{1,0:T(8,128)S(1)} %bitcast.22, f32[1216,128]{1,0:T(8,128)S(1)} %get-tuple-element.254, s32[2176]{0:T(1024)S(1)} %get-tuple-element.144.tasks, f32[152,128]{1,0:T(8,128)S(1)} %get-tuple-element.255, f32[3,2048]{1,0:T(4,128)S(1)} %get-tuple-element.147.so_far, ...), custom_call_target="tpu_custom_call" | custom-call | tf_op jit(solution)/shard_map/near/pallas_call | solution.py:479
  64.3 0.0 copy-start
  64.3 18.2 %all_to_all.21 = f32[256,1,128]{2,1,0:T(1,128)S(1)} all-to-all(f32[256,1,128]{2,1,0:T(1,128)S(1)} %bitcast.25), channel_id=1, replica_groups=mesh['y'=4,'c'=2,'z'=8,'x'=4] {'y','c','z','x'}, dimensions={0} | all-to-all | bytes 262144 | tf_op jit(solution)/shard_map/all_to_all | solution.py:517
  82.5 0.0 copy-done
  82.5 0.7 step.1
Async XLA Ops:
  2.5 29.1 %all-to-all-start = ((f32[8,152,128]{2,1,0:T(8,128)}), f32[8,152,128]{2,1,0:T(8,128)S(1)}, u32[]{:S(2)}, u32[]{:S(2)}) async-start(f32[8,152,128]{2,1,0:T(8,128)} %bitcast.39), calls=%async_computation | async-start | bytes 1245184 | tf_op jit(solution)/shard_map/all_to_all | solution.py:421
  48.8 3.5 %copy-start.1 = (f32[3,256]{1,0:T(4,128)S(1)}, f32[3,256]{1,0:T(4,128)}, u32[]{:S(2)}) copy-start(f32[3,256]{1,0:T(4,128)} %centers.1) | copy-start | bytes 9220
  48.9 3.5 %copy-start.2 = (s32[16]{0:T(128)S(1)}, s32[16]{0:T(128)}, u32[]{:S(2)}) copy-start(s32[16]{0:T(128)} %cells.3) | copy-start | bytes 196
  48.9 12.0 %all-to-all-start.2 = ((f32[4,216,128]{2,1,0:T(8,128)}), f32[4,216,128]{2,1,0:T(8,128)S(1)}, u32[]{:S(2)}, u32[]{:S(2)}) async-start(f32[4,216,128]{2,1,0:T(8,128)} %bitcast.8), calls=%async_computation.2 | async-start | bytes 884736 | tf_op jit(solution)/shard_map/all_to_all | solution.py:490
  52.4 4.6 %copy-start.3 = (f32[2048]{0:T(1024)S(1)}, f32[2048]{0:T(1024)}, u32[]{:S(2)}) copy-start(f32[2048]{0:T(1024)} %param.10) | copy-start | bytes 24580
  64.3 18.2 %copy-start = (f32[3,2048]{1,0:T(4,128)S(1)}, f32[3,2048]{1,0:T(4,128)}, u32[]{:S(2)}) copy-start(f32[3,2048]{1,0:T(4,128)} %get-tuple-element.138.forces) | copy-start | bytes 73732

commit v5 on v4

--- a/solution.py
+++ b/solution.py
@@ -16,9 +16,8 @@
 NG = 8
 EXTRA = 9 * NB
 ROWS = EXTRA + 8
-CAP = 24
-SECT = 9 * CAP
-LOCAL = NX * SECT
+CAP = 20
+SECT = 9 * CAP + 4
 TASKS = 2048
 COUNT = TASKS + 64
 UNROLL = 4
@@ -191,33 +190,58 @@
     return list_hits(hits > 0.0, code, lst, smem, sem)
 
 
-def place_tasks(rnd, count, tasks, smem, cnt):
+def place_tasks(rnd, count, local, tasks, smem, cnt):
     xx = lax.axis_index("x")
     for x in range(NX):
         cnt[x] = 0
 
-    def receive(i, at):
+    def receive(i, carry):
+        at_local, at = carry
         entry = smem[i >> 7, i & 127]
         f = entry & 511
+        k = (entry >> 9) << 12
         column = (f >> 4) & 3
         here = column == xx
         slot = cnt[column] - rnd * CAP
         cnt[column] = cnt[column] + 1
-        base = jnp.where(here, LOCAL + (f >> 6) * ROWS + (f & 15), column * SECT + slot)
-        use = jnp.where(here, rnd == 0, (slot >= 0) & (slot < CAP))
-        tasks[at] = base | ((entry >> 9) << 12)
-        return at + use.astype(jnp.int32)
-
-    used = lax.fori_loop(0, count, receive, 0)
+        local[at_local] = ((f >> 6) * ROWS + (f & 15)) | k
+        tasks[at] = (column * SECT + slot) | k
+        use = jnp.logical_not(here) & (slot >= 0) & (slot < CAP)
+        return at_local + here.astype(jnp.int32), at + use.astype(jnp.int32)
+
+    used_local, used = lax.fori_loop(0, count, receive, (0, 0))
     for u in range(8):
+        local[used_local + u] = PAD
         tasks[used + u] = PAD
     tasks[COUNT] = used
-
-
-def tasks_kernel(turn_no, rec_t, tasks, lst, smem, cnt, sem):
+    return used_local
+
+
+def run_tasks(listed, count, blocks, apart, own, sides, acc):
+    columns = point_columns()
+
+    def step(i, carry):
+        for u in range(UNROLL):
+            entry = listed[UNROLL * i + u]
+            base = entry & 4095
+            k = (entry >> 12) & 15
+
+            def row(r):
+                return blocks[pl.ds(base + r * apart, 1), :]
+
+            here = [own[pl.ds(a * NB + k, 1), :] for a in range(3)]
+            near = source_pull(row, jnp.where(entry >= PAD, 0, 9), sides[k], here, columns)
+            for a in range(3):
+                acc[k, a] = acc[k, a] + near[a]
+        return carry
+
+    lax.fori_loop(0, (count + UNROLL - 1) // UNROLL, step, 0)
+
+
+def tasks_kernel(turn_no, rec_t, tasks, lst, smem, cnt, sem, local):
     copy, count = list_tasks(rec_t, lst, smem, sem)
     copy.wait()
-    place_tasks(turn_no[0], count, tasks, smem, cnt)
+    place_tasks(turn_no[0], count, local, tasks, smem, cnt)
 
 
 def outer_rows(row, symmetric):
@@ -320,7 +344,9 @@
     write_forces(acc, forces)
 
 
-def far_kernel(own, rec_t, cells, centers, so_far, forces, rounds, tasks, there, sides, acc, lst, smem, cnt, sem):
+def far_kernel(
+    own, rec_t, rec_z, cells, centers, so_far, forces, rounds, tasks, there, sides, acc, lst, smem, cnt, sem, local
+):
     copy, count = list_tasks(rec_t, lst, smem, sem)
     rounds[0] = rounds_needed(*group_pairs(rec_t))
     others = []
@@ -357,35 +383,16 @@
         return carry
 
     lax.fori_loop(0, NB // 2, step, 0)
+    copy.wait()
+    used = place_tasks(0, count, local, tasks, smem, cnt)
+    run_tasks(local, used, rec_z, NB, own, sides, acc)
     write_forces(acc, forces, so_far)
-    copy.wait()
-    place_tasks(0, count, tasks, smem, cnt)
-
-
-def near_kernel(rec_x, rec_z, tasks, own, so_far, mobility, forces, tops, sides, acc):
+
+
+def near_kernel(rec_x, tasks, own, so_far, mobility, forces, tops, sides, acc):
     acc[...] = jnp.zeros_like(acc)
     own_sides(own, sides)
-    columns = point_columns()
-
-    def pair_step(i, carry):
-        for u in range(UNROLL):
-            entry = tasks[UNROLL * i + u]
-            base = entry & 4095
-            k = (entry >> 12) & 15
-            here = base >= LOCAL
-            at_z = jnp.where(here, base - LOCAL, 0)
-            at_x = jnp.where(here, 0, base)
-
-            def row(r):
-                return jnp.where(here, rec_z[pl.ds(at_z + r * NB, 1), :], rec_x[pl.ds(at_x + r * CAP, 1), :])
-
-            mine = [own[pl.ds(a * NB + k, 1), :] for a in range(3)]
-            near = source_pull(row, jnp.where(entry >= PAD, 0, 9), sides[k], mine, columns)
-            for a in range(3):
-                acc[k, a] = acc[k, a] + near[a]
-        return carry
-
-    lax.fori_loop(0, (tasks[COUNT] + UNROLL - 1) // UNROLL, pair_step, 0)
+    run_tasks(tasks, tasks[COUNT], rec_x, CAP, own, sides, acc)
     write_forces(acc, forces, so_far)
     v = mobility[...] * forces[...]
     speed = jnp.sum(v * v, axis=0, keepdims=True)
@@ -469,7 +476,7 @@
             out_shape=shape(TASKS + 128, kind=jnp.int32),
             in_specs=[SMEM, VMEM],
             out_specs=SMEM,
-            scratch_shapes=lists(16),
+            scratch_shapes=lists(16) + [pltpu.SMEM((TASKS + 128,), jnp.int32)],
             compiler_params=small,
             cost_estimate=cost(1),
             name="tasks",
@@ -479,25 +486,27 @@
         return pl.pallas_call(
             near_kernel,
             out_shape=(shape(3, seg_count), shape(devices, BLK)),
-            in_specs=[VMEM, VMEM, SMEM, VMEM, VMEM, VMEM],
+            in_specs=[VMEM, SMEM, VMEM, VMEM, VMEM],
             out_specs=(VMEM, VMEM),
             scratch_shapes=[sides, sums],
             compiler_params=small,
             name="near",
-        )(rec_x, rec_z, tasks, own, so_far, mob)
+        )(rec_x, tasks, own, so_far, mob)
 
     first = jnp.zeros((1,), jnp.int32)
     rec_x = lax.all_to_all(to_send(first), "x", 0, 0, tiled=True)
     home, rounds, tasks = pl.pallas_call(
         far_kernel,
         out_shape=(shape(3, seg_count), shape(1, kind=jnp.int32), shape(TASKS + 128, kind=jnp.int32)),
-        in_specs=[VMEM, VMEM, SMEM, VMEM, VMEM],
+        in_specs=[VMEM, VMEM, VMEM, SMEM, VMEM, VMEM],
         out_specs=(VMEM, SMEM, SMEM),
-        scratch_shapes=[pltpu.VMEM((2, 3, BLK, BLK), F32), sides, sums] + lists(16),
+        scratch_shapes=[pltpu.VMEM((2, 3, BLK, BLK), F32), sides, sums]
+        + lists(16)
+        + [pltpu.SMEM((TASKS + 128,), jnp.int32)],
         compiler_params=small,
         cost_estimate=cost(1),
         name="far",
-    )(own, rec_t, block_cells, cell_centers, same)
+    )(own, rec_t, rec_z, block_cells, cell_centers, same)
 
     def more(carry):
         left, so_far = carry

time: 83.8 us -> 83.6 us (level)
  waiting for transfers between devices: 21.6 us -> 20 us
    all_to_all x1, waiting for transfers between devices: 3.21 us -> 1.57 us  [body(): rec_x = lax.all_to_all(to_send(first), 'x', 0, 0, tiled=True)]
    pallas_call x1, Pallas kernels: 4.57 us -> 5.45 us  [body(): pl.pallas_call(far_kernel, out_shape=(shape(3, seg_count), shape(1, kind=...]
  transfers between devices with their start and end apart: 2 -> 2, of which waited for: 2 -> 2; matrix products, arithmetic and copies ran while one was open for 0% -> 0% of each run, Pallas kernels for 7% -> 9%
where the time goes in v5:
time: 83.6 us; the launch traced here: 83 us
  blocking collectives  33.8 us (40%)
  waiting for transfers between devices  20 us (24%)
  Pallas kernels  15.3 us (18%)
  starting transfers between devices  12.5 us (15%)
    all_to_all x1, blocking collectives, body(): lax.all_to_all(tops.reshape(devices, 1, BLK), ('y', 'c', 'z', 'x'), 0, 0,...  18.8 us
    all_to_all x1, waiting for transfers between devices, body(): lax.all_to_all(packed.reshape(NZ, ROWS, BLK), 'z', 0, 0, tiled=True)  18.4 us
    all_to_all x1, blocking collectives, body(): lax.all_to_all(column.reshape(NG * NX, 8, BLK), ('y', 'c', 'x'), 0, 0, ti...  15 us
    all_to_all x1, starting transfers between devices, body(): lax.all_to_all(packed.reshape(NZ, ROWS, BLK), 'z', 0, 0, tiled=True)  9.01 us
    pallas_call x1, Pallas kernels, body(): pl.pallas_call(far_kernel, out_shape=(shape(3, seg_count), shape(1, kind=...  5.45 us
    all_to_all x1, starting transfers between devices, body(): rec_x = lax.all_to_all(to_send(first), 'x', 0, 0, tiled=True)  3.47 us
    pallas_call x1, Pallas kernels, add_near(): pl.pallas_call(near_kernel, out_shape=(shape(3, seg_count), shape(devices...  3.42 us
    pallas_call x1, Pallas kernels, to_send(): pl.pallas_call(send_kernel, out_shape=shape(NX * SECT, BLK), in_specs=[SM...  2.1 us
  transfers between devices with their start and end apart: 2, of which 2 were waited for; matrix products, arithmetic and copies ran while one was open for 0% of the time, Pallas kernels for 9%

profile of v5, /device:TPU:1, one launch (start us, length us, event | category | flops | bytes accessed | tf_op | source)
XLA Modules:
  0.0 83.0 jit_solution(17888190585555708418)
XLA Ops:
  0.6 1.9 %pack.1 = (f32[1216,128]{1,0:T(8,128)}, f32[152,128]{1,0:T(8,128)S(1)}) custom-call(f32[9,2048]{1,0:T(8,128)} %seg.1, s32[16]{0:T(128)} %cells.3, s32[2,32]{1,0:T(2,128)} %bitcast.42), custom_call_target="tpu_custom_call" | custom-call | tf_op jit(solution)/shard_map/pack/pallas_call | solution.py:421
  2.5 9.0 %all-to-all-start = ((f32[8,152,128]{2,1,0:T(8,128)}), f32[8,152,128]{2,1,0:T(8,128)S(1)}, u32[]{:S(2)}, u32[]{:S(2)}) async-start(f32[8,152,128]{2,1,0:T(8,128)} %bitcast.40), calls=%async_computation | async-start | bytes 1245184 | tf_op jit(solution)/shard_map/all_to_all | solution.py:428
  11.5 1.6 %own.1.so_far = f32[3,2048]{1,0:T(4,128)S(1)} custom-call(f32[152,128]{1,0:T(8,128)S(1)} %get-tuple-element.214.own), custom_call_target="tpu_custom_call" | custom-call | flops 1000000000 | bytes 1 | tf_op jit(solution)/shard_map/own/pallas_call | solution.py:431
  13.2 18.4 %all-to-all-done = f32[8,152,128]{2,1,0:T(8,128)S(1)} async-done(((f32[8,152,128]{2,1,0:T(8,128)}), f32[8,152,128]{2,1,0:T(8,128)S(1)}, u32[]{:S(2)}, u32[]{:S(2)}) %all-to-all-start) | async-done | bytes 622624 | tf_op jit(solution)/shard_map/all_to_all | solution.py:428
  31.6 0.1 column.1
  31.7 15.0 %all_to_all.20 = f32[32,8,128]{2,1,0:T(8,128)S(1)} all-to-all(f32[32,8,128]{2,1,0:T(8,128)S(1)} %bitcast.23), channel_id=1, replica_groups=mesh['y'=4,'c'=2,'z'=8,'x'=4] {'y','c','x'}, dimensions={0} | all-to-all | bytes 262144 | tf_op jit(solution)/shard_map/all_to_all | solution.py:451
  46.7 2.1 %send.8 = f32[736,128]{1,0:T(8,128)} custom-call(s32[1]{0:T(128)} %constant.134.clone.1.turn_no, f32[256,128]{1,0:T(8,128)S(1)} %bitcast.37, f32[1216,128]{1,0:T(8,128)S(1)} %bitcast.34), custom_call_target="tpu_custom_call" | custom-call | tf_op jit(solution)/shard_map/send/pallas_call | solution.py:463
  48.8 0.0 copy-start.1
  48.8 0.0 copy-start.2
  48.8 3.5 %all-to-all-start.2 = ((f32[4,184,128]{2,1,0:T(8,128)}), f32[4,184,128]{2,1,0:T(8,128)S(1)}, u32[]{:S(2)}, u32[]{:S(2)}) async-start(f32[4,184,128]{2,1,0:T(8,128)} %bitcast.8), calls=%async_computation.2 | async-start | bytes 753664 | tf_op jit(solution)/shard_map/all_to_all | solution.py:497
  52.3 0.0 copy-done.1
  52.3 0.0 copy-done.2
  52.3 0.0 copy-start.3
  52.3 5.5 %far.1 = (f32[3,2048]{1,0:T(4,128)S(1)}, s32[1]{0:T(128)}, s32[2176]{0:T(1024)S(1)}) custom-call(f32[152,128]{1,0:T(8,128)S(1)} %get-tuple-element.214.own, f32[256,128]{1,0:T(8,128)S(1)} %bitcast.38, f32[1216,128]{1,0:T(8,128)S(1)} %bitcast.35, s32[16]{0:T(128)S(1)} %copy-done.2, f32[3,256]{1,0:T(4,128)S(1)} %copy-done.1, f32[3,2048]{1,0:T(4,128)S(1)} %own.1.so_far), custom_call_target="tpu_custom_call" | custom-call | flops 1 | bytes 1 | tf_op jit(solution)/shard_map/far/pallas_call | solution.py:498
  57.8 0.0 copy-done.3
  57.8 0.7 while.14
  58.5 1.6 %all-to-all-done.2 = f32[4,184,128]{2,1,0:T(8,128)S(1)} async-done(((f32[4,184,128]{2,1,0:T(8,128)}), f32[4,184,128]{2,1,0:T(8,128)S(1)}, u32[]{:S(2)}, u32[]{:S(2)}) %all-to-all-start.2) | async-done | bytes 376864 | tf_op jit(solution)/shard_map/all_to_all | solution.py:497
  60.0 3.4 %near.8 = (f32[3,2048]{1,0:T(4,128)}, f32[256,128]{1,0:T(8,128)S(1)}) custom-call(f32[736,128]{1,0:T(8,128)S(1)} %bitcast.22, s32[2176]{0:T(1024)S(1)} %get-tuple-element.144.tasks, f32[152,128]{1,0:T(8,128)S(1)} %get-tuple-element.254, f32[3,2048]{1,0:T(4,128)S(1)} %get-tuple-element.147.so_far, f32[1,2048]{1,0:T(1,128)S(1)} %get-tuple-element.263), custom_call_target="tpu_custom_call" | custom-call | tf_op jit(solution)/shard_map/near/pallas_call | solution.py:486
  63.4 0.0 copy-start
  63.4 18.8 %all_to_all.21 = f32[256,1,128]{2,1,0:T(1,128)S(1)} all-to-all(f32[256,1,128]{2,1,0:T(1,128)S(1)} %bitcast.25), channel_id=1, replica_groups=mesh['y'=4,'c'=2,'z'=8,'x'=4] {'y','c','z','x'}, dimensions={0} | all-to-all | bytes 262144 | tf_op jit(solution)/shard_map/all_to_all | solution.py:526
  82.3 0.0 copy-done
  82.3 0.7 step.1
Async XLA Ops:
  2.5 29.1 %all-to-all-start = ((f32[8,152,128]{2,1,0:T(8,128)}), f32[8,152,128]{2,1,0:T(8,128)S(1)}, u32[]{:S(2)}, u32[]{:S(2)}) async-start(f32[8,152,128]{2,1,0:T(8,128)} %bitcast.40), calls=%async_computation | async-start | bytes 1245184 | tf_op jit(solution)/shard_map/all_to_all | solution.py:428
  48.8 3.5 %copy-start.1 = (f32[3,256]{1,0:T(4,128)S(1)}, f32[3,256]{1,0:T(4,128)}, u32[]{:S(2)}) copy-start(f32[3,256]{1,0:T(4,128)} %centers.1) | copy-start | bytes 9220
  48.8 3.5 %copy-start.2 = (s32[16]{0:T(128)S(1)}, s32[16]{0:T(128)}, u32[]{:S(2)}) copy-start(s32[16]{0:T(128)} %cells.3) | copy-start | bytes 196
  48.8 11.2 %all-to-all-start.2 = ((f32[4,184,128]{2,1,0:T(8,128)}), f32[4,184,128]{2,1,0:T(8,128)S(1)}, u32[]{:S(2)}, u32[]{:S(2)}) async-start(f32[4,184,128]{2,1,0:T(8,128)} %bitcast.8), calls=%async_computation.2 | async-start | bytes 753664 | tf_op jit(solution)/shard_map/all_to_all | solution.py:497
  52.3 5.5 %copy-start.3 = (f32[2048]{0:T(1024)S(1)}, f32[2048]{0:T(1024)}, u32[]{:S(2)}) copy-start(f32[2048]{0:T(1024)} %param.10) | copy-start | bytes 24580
  63.4 18.8 %copy-start = (f32[3,2048]{1,0:T(4,128)S(1)}, f32[3,2048]{1,0:T(4,128)}, u32[]{:S(2)}) copy-start(f32[3,2048]{1,0:T(4,128)} %get-tuple-element.138.forces) | copy-start | bytes 73732

commit v6 on v5

--- a/solution.py
+++ b/solution.py
@@ -16,8 +16,8 @@
 NG = 8
 EXTRA = 9 * NB
 ROWS = EXTRA + 8
-CAP = 20
-SECT = 9 * CAP + 4
+CAP = 14
+SECT = 9 * CAP + 2
 TASKS = 2048
 COUNT = TASKS + 64
 UNROLL = 4
@@ -45,7 +45,7 @@
     return one, two, three
 
 
-def pack_kernel(seg, cells, pairs, packed, out):
+def pack_kernel(seg, cells, pairs, packed, out, same_cells):
     for k in range(NB):
         cols = slice(k * BLK, (k + 1) * BLK)
         out[pl.ds(k, 8, stride=NB), :] = seg[0:8, cols]
@@ -54,6 +54,7 @@
     cell = jnp.zeros((NB, BLK), jnp.int32)
     for k in range(NB):
         cell = jnp.where(row == k, cells[k] & 31, cell)
+        same_cells[k] = cells[k]
     hot = (lanes(NB) == cell + 64).astype(F32)
     hot_last = (lanes(NB) == cell + 96).astype(F32)
     rows = []
@@ -67,30 +68,30 @@
         out[EXTRA + r : EXTRA + r + 1, :] = rows[r]
     out[EXTRA : EXTRA + 2, 0:32] = pairs[...].astype(F32)
     whole = out[...]
-    for copy in range(NZ):
+    for copy in range(NX):
         packed[copy * ROWS : (copy + 1) * ROWS, :] = whole
 
 
-def column_kernel(*refs):
-    out = refs[NZ]
+def row_kernel(*refs):
+    out = refs[NX]
     lane = lanes(8)
-    first = jnp.concatenate([ref[0:1, :] for ref in refs[:NZ]], axis=0)
-    second = jnp.concatenate([ref[1:2, :] for ref in refs[:NZ]], axis=0)
+    rest = [jnp.zeros((8 - NX, BLK), F32)]
+    first = jnp.concatenate([ref[0:1, :] for ref in refs[:NX]] + rest, axis=0)
+    second = jnp.concatenate([ref[1:2, :] for ref in refs[:NX]] + rest, axis=0)
     total = refs[0][...]
-    for ref in refs[1:NZ]:
+    for ref in refs[1:NX]:
         total = total + ref[...]
     tile = jnp.where(lane < 32, first, jnp.where(lane < 64, pltpu.roll(second, 32, 1), total))
-    for copy in range(NG * NX):
+    for copy in range(NZ):
         out[8 * copy : 8 * copy + 8, :] = tile
 
 
 def group_pairs(rec_t):
-    g = lax.axis_index("y") * 2 + lax.axis_index("c")
     lane = lanes(8)
     a = jnp.zeros((8, BLK), F32)
     b = jnp.zeros((8, BLK), F32)
     for x in range(NX):
-        part = rec_t[pl.ds(pl.multiple_of(g * 32 + x * 8, 8), 8), :]
+        part = rec_t[pl.ds(x, NZ, stride=8), :]
         one = jnp.where(lane < 32, part, 0.0)
         two = jnp.where((lane >= 32) & (lane < 64), part, 0.0)
         a = a + (pltpu.roll(one, 32 * x, 1) if x else one)
@@ -130,35 +131,36 @@
     return copy, count
 
 
-def send_kernel(turn_no, rec_t, rec_z, send, lst, smem, cnt, sem):
+def send_kernel(turn_no, rec_t, rec_x, send, start, none, lst, smem, cnt, sem):
+    start[0] = 0
+    none[COUNT] = 0
     zz = lax.axis_index("z")
     xx = lax.axis_index("x")
     rnd = turn_no[0]
     ai, bi = group_pairs(rec_t)
-    own_a, own_b = ai >> 4, bi >> 4
-    xa, xb = own_a & 3, own_b & 3
-    to_a = ((own_a >> 2) == zz) & (xa != xx) & (xb == xx)
-    to_b = ((own_b >> 2) == zz) & (xb != xx) & (xa == xx)
-    code = jnp.where(to_a, xa * 512 + bi, xb * 512 + ai)
-    copy, count = list_hits(to_a | to_b, code, lst, smem, sem)
+    za, zb = ai >> 6, bi >> 6
+    to_a = (za != zz) & (((ai >> 4) & 3) == xx) & (zb == zz)
+    to_b = (zb != zz) & (((bi >> 4) & 3) == xx) & (za == zz)
+    code = jnp.where(to_a, za * 512 + bi, zb * 512 + ai)
+    copy, count = list_hits((to_a & (ai >= 0)) | (to_b & (bi >= 0)), code, lst, smem, sem)
     send[...] = jnp.zeros_like(send)
-    for x in range(NX):
-        cnt[x] = 0
+    for z in range(NZ):
+        cnt[z] = 0
     copy.wait()
 
     def deliver(i, carry):
         entry = smem[i >> 7, i & 127]
         f = entry & 511
-        x = entry >> 9
-        slot = cnt[x] - rnd * CAP
-        cnt[x] = cnt[x] + 1
+        z = entry >> 9
+        slot = cnt[z] - rnd * CAP
+        cnt[z] = cnt[z] + 1
 
         @pl.when((slot >= 0) & (slot < CAP))
         def _():
-            source = (f >> 6) * ROWS + (f & 15)
-            target = x * SECT + slot
-            send[pl.ds(target, 8, stride=CAP), :] = rec_z[pl.ds(source, 8, stride=NB), :]
-            send[pl.ds(target + 8 * CAP, 1), :] = rec_z[pl.ds(source + 8 * NB, 1), :]
+            source = ((f >> 4) & 3) * ROWS + (f & 15)
+            target = z * SECT + slot
+            send[pl.ds(target, 8, stride=CAP), :] = rec_x[pl.ds(source, 8, stride=NB), :]
+            send[pl.ds(target + 8 * CAP, 1), :] = rec_x[pl.ds(source + 8 * NB, 1), :]
 
         return carry
 
@@ -171,12 +173,12 @@
     for here, there in ((own_a, own_b), (own_b, own_a)):
         for i in range(8):
             owner.append((subs(32) == here[i : i + 1, :]).astype(BF16))
-            column.append((subs(16) == (there[i : i + 1, :] & 3)).astype(BF16))
+            column.append((subs(16) == (there[i : i + 1, :] >> 2)).astype(BF16))
     owner, column = jnp.concatenate(owner, axis=1), jnp.concatenate(column, axis=1)
     need = lax.dot_general(owner, column, NT, preferred_element_type=F32)
     r32 = lax.broadcasted_iota(jnp.int32, (32, 16), 0)
     c32 = lax.broadcasted_iota(jnp.int32, (32, 16), 1)
-    longest = jnp.max(jnp.where((r32 & 3) == c32, 0.0, need)).astype(jnp.int32)
+    longest = jnp.max(jnp.where((r32 >> 2) == c32, 0.0, need)).astype(jnp.int32)
     return (longest + CAP - 1) // CAP
 
 
@@ -191,21 +193,21 @@
 
 
 def place_tasks(rnd, count, local, tasks, smem, cnt):
-    xx = lax.axis_index("x")
-    for x in range(NX):
-        cnt[x] = 0
+    zz = lax.axis_index("z")
+    for z in range(NZ):
+        cnt[z] = 0
 
     def receive(i, carry):
         at_local, at = carry
         entry = smem[i >> 7, i & 127]
         f = entry & 511
         k = (entry >> 9) << 12
-        column = (f >> 4) & 3
-        here = column == xx
-        slot = cnt[column] - rnd * CAP
-        cnt[column] = cnt[column] + 1
-        local[at_local] = ((f >> 6) * ROWS + (f & 15)) | k
-        tasks[at] = (column * SECT + slot) | k
+        z = f >> 6
+        here = z == zz
+        slot = cnt[z] - rnd * CAP
+        cnt[z] = cnt[z] + 1
+        local[at_local] = (((f >> 4) & 3) * ROWS + (f & 15)) | k
+        tasks[at] = (z * SECT + slot) | k
         use = jnp.logical_not(here) & (slot >= 0) & (slot < CAP)
         return at_local + here.astype(jnp.int32), at + use.astype(jnp.int32)
 
@@ -344,24 +346,36 @@
     write_forces(acc, forces)
 
 
-def far_kernel(
-    own, rec_t, rec_z, cells, centers, so_far, forces, rounds, tasks, there, sides, acc, lst, smem, cnt, sem, local
-):
+def row_pairs_kernel(own, rec_t, rec_x, so_far, forces, rounds, tasks, sides, acc, lst, smem, cnt, sem, local):
     copy, count = list_tasks(rec_t, lst, smem, sem)
     rounds[0] = rounds_needed(*group_pairs(rec_t))
+    own_sides(own, sides)
+    acc[...] = jnp.zeros_like(acc)
+    copy.wait()
+    used = place_tasks(0, count, local, tasks, smem, cnt)
+    run_tasks(local, used, rec_x, NB, own, sides, acc)
+    write_forces(acc, forces, so_far)
+
+
+def far_kernel(own, m0, m1, m2, m3, cells, centers, so_far, forces, there, sides, acc):
+    lane = lanes(8)
+    parts = []
+    for i, ref in enumerate((m0, m1, m2, m3)):
+        for h in range(2):
+            y = (lax.axis_index("y") + 4 - i) & 3
+            c = lax.axis_index("c")
+            at = 32 * ((2 * y + (1 - c if h else c)) & 3)
+            tile = ref[8 * h : 8 * h + 8, :]
+            low = pltpu.roll(jnp.where((lane >= 64) & (lane < 96), tile, 0.0), (at + 64) & 127, 1)
+            high = pltpu.roll(jnp.where(lane >= 96, tile, 0.0), (at + 32) & 127, 1)
+            parts.append((y >> 1, low, high))
     others = []
     for half in range(2):
         rows = jnp.zeros((8, BLK), F32)
         last = jnp.zeros((8, BLK), F32)
-        for i in range(4):
-            at = (half * 4 + i) * 32
-            tile = rec_t[at : at + 8, :]
-            for x in range(1, NX):
-                tile = tile + rec_t[at + 8 * x : at + 8 * x + 8, :]
-            low = jnp.where((lanes(8) >= 64) & (lanes(8) < 96), tile, 0.0)
-            high = jnp.where(lanes(8) >= 96, tile, 0.0)
-            rows = rows + (pltpu.roll(low, (32 * i + 64) % 128, 1) if i != 2 else low)
-            last = last + (pltpu.roll(high, (32 * i + 32) % 128, 1) if i != 3 else high)
+        for which, low, high in parts:
+            rows = rows + jnp.where(which == half, low, 0.0)
+            last = last + jnp.where(which == half, high, 0.0)
         rows = jnp.concatenate([rows, last[0:1, :], jnp.zeros((7, BLK), F32)], axis=0)
         cols = slice(half * BLK, (half + 1) * BLK)
         turned = other_side(rows, [centers[a : a + 1, cols] for a in range(3)])
@@ -383,16 +397,13 @@
         return carry
 
     lax.fori_loop(0, NB // 2, step, 0)
-    copy.wait()
-    used = place_tasks(0, count, local, tasks, smem, cnt)
-    run_tasks(local, used, rec_z, NB, own, sides, acc)
     write_forces(acc, forces, so_far)
 
 
-def near_kernel(rec_x, tasks, own, so_far, mobility, forces, tops, sides, acc):
+def near_kernel(rec_z, tasks, own, so_far, mobility, forces, tops, sides, acc):
     acc[...] = jnp.zeros_like(acc)
     own_sides(own, sides)
-    run_tasks(tasks, tasks[COUNT], rec_x, CAP, own, sides, acc)
+    run_tasks(tasks, tasks[COUNT], rec_z, CAP, own, sides, acc)
     write_forces(acc, forces, so_far)
     v = mobility[...] * forces[...]
     speed = jnp.sum(v * v, axis=0, keepdims=True)
@@ -418,14 +429,14 @@
     seg_count = segments.shape[1]
     devices = 8 * NG * NX
     mob = mobility[None, :]
-    packed, own = pl.pallas_call(
+    packed, own, cells = pl.pallas_call(
         pack_kernel,
-        out_shape=(shape(NZ * ROWS, BLK), shape(ROWS, BLK)),
+        out_shape=(shape(NX * ROWS, BLK), shape(ROWS, BLK), shape(NB, kind=jnp.int32)),
         in_specs=[VMEM, SMEM, VMEM],
-        out_specs=(VMEM, VMEM),
+        out_specs=(VMEM, VMEM, SMEM),
         name="pack",
     )(segments, block_cells, pair_blocks.T)
-    rec_z = lax.all_to_all(packed.reshape(NZ, ROWS, BLK), "z", 0, 0, tiled=True).reshape(NZ * ROWS, BLK)
+    rec_x = lax.all_to_all(packed.reshape(NX, ROWS, BLK), "x", 0, 0, tiled=True).reshape(NX * ROWS, BLK)
     sides = pltpu.VMEM((NB, BLK, BLK), BF16)
     sums = pltpu.VMEM((NB, 3, 8, BLK), F32)
     same = pl.pallas_call(
@@ -438,37 +449,38 @@
         cost_estimate=cost(10**9),
         name="own",
     )(own)
-    rec_z, same = lax.optimization_barrier((rec_z, same))
-    column = pl.pallas_call(
-        column_kernel,
-        out_shape=shape(NG * NX * 8, BLK),
+    rec_x, same = lax.optimization_barrier((rec_x, same))
+    row = pl.pallas_call(
+        row_kernel,
+        out_shape=shape(NZ * 8, BLK),
         grid=(1,),
-        in_specs=[pl.BlockSpec((8, BLK), lambda i, s=s: ((s * ROWS + EXTRA) // 8, 0)) for s in range(NZ)],
-        out_specs=pl.BlockSpec((NG * NX * 8, BLK), lambda i: (0, 0)),
+        in_specs=[pl.BlockSpec((8, BLK), lambda i, s=s: ((s * ROWS + EXTRA) // 8, 0)) for s in range(NX)],
+        out_specs=pl.BlockSpec((NZ * 8, BLK), lambda i: (0, 0)),
         compiler_params=small,
-        name="column",
-    )(*([rec_z] * NZ))
-    rec_t = lax.all_to_all(column.reshape(NG * NX, 8, BLK), ("y", "c", "x"), 0, 0, tiled=True)
-    rec_t = rec_t.reshape(NG * NX * 8, BLK)
+        name="row",
+    )(*([rec_x] * NX))
+    rec_t = lax.all_to_all(row.reshape(NZ, 8, BLK), "z", 0, 0, tiled=True)
+    group = jnp.sum(rec_t, axis=0)
+    rec_t = rec_t.reshape(NZ * 8, BLK)
 
     def lists(rows):
         return [
             pltpu.VMEM((rows, BLK), jnp.int32),
             pltpu.SMEM((rows, BLK), jnp.int32),
-            pltpu.SMEM((NX,), jnp.int32),
+            pltpu.SMEM((NZ,), jnp.int32),
             pltpu.SemaphoreType.DMA,
         ]
 
     def to_send(number):
         return pl.pallas_call(
             send_kernel,
-            out_shape=shape(NX * SECT, BLK),
+            out_shape=(shape(NZ * SECT, BLK), shape(1, kind=jnp.int32), shape(TASKS + 128, kind=jnp.int32)),
             in_specs=[SMEM, VMEM, VMEM],
-            out_specs=VMEM,
+            out_specs=(VMEM, SMEM, SMEM),
             scratch_shapes=lists(8),
             compiler_params=small,
             name="send",
-        )(number, rec_t, rec_z).reshape(NX, SECT, BLK)
+        )(number, rec_t, rec_x)
 
     def to_do(number):
         return pl.pallas_call(
@@ -482,7 +494,7 @@
             name="tasks",
         )(number, rec_t)
 
-    def add_near(rec_x, tasks, so_far):
+    def add_near(rec_z, tasks, so_far):
         return pl.pallas_call(
             near_kernel,
             out_shape=(shape(3, seg_count), shape(devices, BLK)),
@@ -491,38 +503,53 @@
             scratch_shapes=[sides, sums],
             compiler_params=small,
             name="near",
-        )(rec_x, tasks, own, so_far, mob)
-
-    first = jnp.zeros((1,), jnp.int32)
-    rec_x = lax.all_to_all(to_send(first), "x", 0, 0, tiled=True)
-    home, rounds, tasks = pl.pallas_call(
-        far_kernel,
-        out_shape=(shape(3, seg_count), shape(1, kind=jnp.int32), shape(TASKS + 128, kind=jnp.int32)),
-        in_specs=[VMEM, VMEM, VMEM, SMEM, VMEM, VMEM],
-        out_specs=(VMEM, SMEM, SMEM),
-        scratch_shapes=[pltpu.VMEM((2, 3, BLK, BLK), F32), sides, sums]
-        + lists(16)
-        + [pltpu.SMEM((TASKS + 128,), jnp.int32)],
-        compiler_params=small,
-        cost_estimate=cost(1),
-        name="far",
-    )(own, rec_t, rec_z, block_cells, cell_centers, same)
+        )(rec_z, tasks, own, so_far, mob)
 
     def more(carry):
         left, so_far = carry
         number = left - 1
-        send = to_send(number)
+        send = to_send(number)[0].reshape(NZ, SECT, BLK)
         late = to_do(number)
-        x = lax.axis_index("x")
+        z = lax.axis_index("z")
         got = jnp.zeros_like(send)
-        for k in range(1, NX):
-            part = lax.dynamic_index_in_dim(send, (x + k) % NX, 0, keepdims=True)
-            part = lax.ppermute(part, "x", [(i, (i + k) % NX) for i in range(NX)])
-            got = lax.dynamic_update_slice_in_dim(got, part, (x + NX - k) % NX, 0)
-        return number, add_near(got.reshape(NX * SECT, BLK), late, so_far)[0]
-
-    _, home = lax.while_loop(lambda c: c[0][0] > 1, more, (rounds, home))
-    forces, tops = add_near(rec_x.reshape(NX * SECT, BLK), tasks, home)
+        for k in range(1, NZ):
+            part = lax.dynamic_index_in_dim(send, (z + k) % NZ, 0, keepdims=True)
+            part = lax.ppermute(part, "z", [(i, (i + k) % NZ) for i in range(NZ)])
+            got = lax.dynamic_update_slice_in_dim(got, part, (z + NZ - k) % NZ, 0)
+        return number, add_near(got.reshape(NZ * SECT, BLK), late, so_far)[0]
+
+    def beside(carry):
+        turn, so_far, _, moments = carry
+        groups = [moments] + [lax.ppermute(moments, "y", [(i, (i + k) % 4) for i in range(4)]) for k in range(1, 4)]
+        some, rounds, tasks = pl.pallas_call(
+            row_pairs_kernel,
+            out_shape=(shape(3, seg_count), shape(1, kind=jnp.int32), shape(TASKS + 128, kind=jnp.int32)),
+            in_specs=[VMEM] * 4,
+            out_specs=(VMEM, SMEM, SMEM),
+            scratch_shapes=[sides, sums] + lists(16) + [pltpu.SMEM((TASKS + 128,), jnp.int32)],
+            compiler_params=small,
+            cost_estimate=cost(4 * 10**9),
+            name="row_pairs",
+        )(own, rec_t, rec_x, so_far)
+        home = pl.pallas_call(
+            far_kernel,
+            out_shape=shape(3, seg_count),
+            in_specs=[VMEM] * 5 + [SMEM, VMEM, VMEM],
+            out_specs=VMEM,
+            scratch_shapes=[pltpu.VMEM((2, 3, BLK, BLK), F32), sides, sums],
+            compiler_params=small,
+            cost_estimate=cost(1),
+            name="far",
+        )(own, *groups, cells, cell_centers, some)
+        _, home = lax.while_loop(lambda c: c[0][0] > 1, more, (rounds, home))
+        return turn + 1, home, tasks, groups[1]
+
+    both = jnp.concatenate([group, lax.ppermute(group, "c", [(0, 1), (1, 0)])], axis=0)
+    first = jnp.zeros((1,), jnp.int32)
+    send, start, no_tasks = to_send(first)
+    rec_z = lax.all_to_all(send.reshape(NZ, SECT, BLK), "z", 0, 0, tiled=True)
+    _, home, tasks, _ = lax.while_loop(lambda c: c[0][0] < 1, beside, (start, same, no_tasks, both))
+    forces, tops = add_near(rec_z.reshape(NZ * SECT, BLK), tasks, home)
     tops = lax.all_to_all(tops.reshape(devices, 1, BLK), ("y", "c", "z", "x"), 0, 0, tiled=True)
     displacement = pl.pallas_call(
         step_kernel,

time: 83.6 us -> 79.7 us (0.953)
  waiting for transfers between devices: 20 us -> 7.4 us
  starting transfers between devices: 12.5 us -> 17 us
  loops' own time: 0.65 us -> 3.07 us
  Pallas kernels: 15.3 us -> 17.6 us
    all_to_all x2, waiting for transfers between devices: 20 us -> 7.38 us  [the longest x1 4.15 us: body(): lax.all_to_all(packed.reshape(NX, ROWS, BLK), 'x', 0, 0, tiled=True)]
    ppermute x0 -> x4, starting transfers between devices: none -> 8.63 us  [the longest x3 5.06 us: beside(): lax.ppermute(moments, 'y', [(i, (i + k) % 4) for i in range(4)])]
    all_to_all x2, starting transfers between devices: 12.5 us -> 8.36 us  [the longest x1 4.85 us: body(): lax.all_to_all(packed.reshape(NX, ROWS, BLK), 'x', 0, 0, tiled=True)]
    another operation x1 -> x2, loops' own time: 0.65 us -> 3.07 us  [the longest x1 2.5 us: body(): lax.while_loop(lambda c: c[0][0] < 1, beside, (start, same, no_tasks, both))]
    pallas_call x1, Pallas kernels: 3.42 us -> 5.13 us  [add_near(): pl.pallas_call(near_kernel, out_shape=(shape(3, seg_count), shape(devices...]
    all_to_all x1, blocking collectives: 18.8 us -> 17.9 us  [body(): lax.all_to_all(tops.reshape(devices, 1, BLK), ('y', 'c', 'z', 'x'), 0, 0,...]
    pallas_call x4 -> x5, Pallas kernels: 9.53 us -> 10.1 us  [the longest x1 3.1 us: beside(): pl.pallas_call(far_kernel, out_shape=shape(3, seg_count), in_specs=[VMEM]...]
  transfers between devices with their start and end apart: 2 -> 6, of which waited for: 2 -> 2; matrix products, arithmetic and copies ran while one was open for 0% -> 0% of each run, Pallas kernels for 9% -> 9%
where the time goes in v6:
time: 79.7 us; the launch traced here: 79.5 us
  blocking collectives  33 us (41%)
  Pallas kernels  17.6 us (22%)
  starting transfers between devices  17 us (21%)
  waiting for transfers between devices  7.4 us (9%)
  loops' own time  3.07 us (4%)
    all_to_all x1, blocking collectives, body(): lax.all_to_all(tops.reshape(devices, 1, BLK), ('y', 'c', 'z', 'x'), 0, 0,...  17.9 us
    all_to_all x1, blocking collectives, body(): rec_t = lax.all_to_all(row.reshape(NZ, 8, BLK), 'z', 0, 0, tiled=True)  15.1 us
    pallas_call x1, Pallas kernels, add_near(): pl.pallas_call(near_kernel, out_shape=(shape(3, seg_count), shape(devices...  5.13 us
    ppermute x3, starting transfers between devices, beside(): lax.ppermute(moments, 'y', [(i, (i + k) % 4) for i in range(4)])  5.06 us
    all_to_all x1, starting transfers between devices, body(): lax.all_to_all(packed.reshape(NX, ROWS, BLK), 'x', 0, 0, tiled=True)  4.85 us
    all_to_all x1, waiting for transfers between devices, body(): lax.all_to_all(packed.reshape(NX, ROWS, BLK), 'x', 0, 0, tiled=True)  4.15 us
    ppermute x1, starting transfers between devices, body(): lax.ppermute(group, 'c', [(0, 1), (1, 0)])  3.57 us
    all_to_all x1, starting transfers between devices, body(): rec_z = lax.all_to_all(send.reshape(NZ, SECT, BLK), 'z', 0, 0, tiled=True)  3.5 us
  transfers between devices with their start and end apart: 6, of which 2 were waited for; matrix products, arithmetic and copies ran while one was open for 0% of the time, Pallas kernels for 9%

profile of v6, /device:TPU:1, one launch (start us, length us, event | category | flops | bytes accessed | tf_op | source)
XLA Modules:
  0.0 79.5 jit_solution(10525321113734565270)
XLA Ops:
  0.6 1.8 %pack.1 = (f32[608,128]{1,0:T(8,128)}, f32[152,128]{1,0:T(8,128)S(1)}, s32[16]{0:T(128)S(1)}) custom-call(f32[9,2048]{1,0:T(8,128)} %seg.1, s32[16]{0:T(128)} %cells.1, s32[2,32]{1,0:T(2,128)} %bitcast.38), custom_call_target="tpu_custom_call" | custom-call | tf_op jit(solution)/shard_map/pack/pallas_call | solution.py:432
  2.4 4.9 %all-to-all-start = ((f32[4,152,128]{2,1,0:T(8,128)}), f32[4,152,128]{2,1,0:T(8,128)S(1)}, u32[]{:S(2)}, u32[]{:S(2)}) async-start(f32[4,152,128]{2,1,0:T(8,128)} %bitcast.37), calls=%async_computation | async-start | bytes 622592 | tf_op jit(solution)/shard_map/all_to_all | solution.py:439
  7.3 1.6 %own.1 = f32[3,2048]{1,0:T(4,128)S(1)} custom-call(f32[152,128]{1,0:T(8,128)S(1)} %get-tuple-element.631.own), custom_call_target="tpu_custom_call" | custom-call | flops 1000000000 | bytes 1 | tf_op jit(solution)/shard_map/own/pallas_call | solution.py:442
  8.9 4.1 %all-to-all-done = f32[4,152,128]{2,1,0:T(8,128)S(1)} async-done(((f32[4,152,128]{2,1,0:T(8,128)}), f32[4,152,128]{2,1,0:T(8,128)S(1)}, u32[]{:S(2)}, u32[]{:S(2)}) %all-to-all-start) | async-done | bytes 311328 | tf_op jit(solution)/shard_map/all_to_all | solution.py:439
  13.1 0.1 row.1
  13.1 15.1 %all_to_all.20 = f32[8,8,128]{2,1,0:T(8,128)S(1)} all-to-all(f32[8,8,128]{2,1,0:T(8,128)S(1)} %bitcast.26), channel_id=1, replica_groups=mesh['y'=4,'c'=2,'z'=8,'x'=4] {'z'}, dimensions={0} | all-to-all | bytes 65536 | tf_op jit(solution)/shard_map/all_to_all | solution.py:462
  28.2 3.6 %collective-permute-start.10 = (f32[8,128]{1,0:T(8,128)S(1)}, f32[8,128]{1,0:T(8,128)S(1)}, u32[]{:S(2)}, u32[]{:S(2)}) collective-permute-start(f32[8,128]{1,0:T(8,128)S(1)} %reduce_sum.9), channel_id=1, source_target_pairs={{0,32},{32,0},{1,33},{33,1},{2,34},{34,2},{3,35},{35,3},{4,36},{36... | collective-permute-start | bytes 12296 | tf_op jit(solution)/shard_map/ppermute | solution.py:547
  31.8 2.4 %send.7 = (f32[1024,128]{1,0:T(8,128)}, s32[1]{0:T(128)}, s32[2176]{0:T(1024)}) custom-call(s32[1]{0:T(128)} %constant.297.clone.1.turn_no, f32[64,128]{1,0:T(8,128)S(1)} %bitcast.34, f32[608,128]{1,0:T(8,128)S(1)} %bitcast.32), custom_call_target="tpu_custom_call" | custom-call | tf_op jit(solution)/shard_map/send/pallas_call | solution.py:475
  34.2 3.5 %all-to-all-start.2 = ((f32[8,128,128]{2,1,0:T(8,128)}), f32[8,128,128]{2,1,0:T(8,128)S(1)}, u32[]{:S(2)}, u32[]{:S(2)}) async-start(f32[8,128,128]{2,1,0:T(8,128)} %bitcast.9), calls=%async_computation.2 | async-start | bytes 1048576 | tf_op jit(solution)/shard_map/all_to_all | solution.py:550
  37.7 0.0 copy-start.1
  37.8 0.0 copy-start.2
  37.8 0.7 copy-done.1
  38.4 0.0 copy-done.2
  38.4 14.0 %while.40 = (s32[1]{0:T(128)}, f32[3,2048]{1,0:T(4,128)S(1)}, s32[2176]{0:T(1024)}, f32[16,128]{1,0:T(8,128)S(1)}, f32[152,128]{1,0:T(8,128)S(1)}, /*index=5*/f3...) while((s32[1]{0:T(128)}, f32[3,2048]{1,0:T(4,128)S(1)}, ...), condition=%wide.region_4.5_spmd, body=%wide.region_1.4_spmd.sunk | while | flops 4000000000 | bytes 4360270 | solution.py:551
  39.1 1.3 %collective-permute-start.7 = (f32[16,128]{1,0:T(8,128)S(1)}, f32[16,128]{1,0:T(8,128)S(1)}, u32[]{:S(2)}, u32[]{:S(2)}) collective-permute-start(f32[16,128]{1,0:T(8,128)S(1)} %copy.28.m0), channel_id=1, source_target_pairs={{0,64},{64,128},{128,192},{192,0},{1,65},{65,129},{129,193},{193,1... | collective-permute-start | bytes 24584 | tf_op jit(solution)/shard_map/while/body/ppermute | solution.py:523
  40.4 2.8 %collective-permute-start.8 = (f32[16,128]{1,0:T(8,128)S(1)}, f32[16,128]{1,0:T(8,128)S(1)}, u32[]{:S(2)}, u32[]{:S(2)}) collective-permute-start(f32[16,128]{1,0:T(8,128)S(1)} %copy.28.m0), channel_id=1, source_target_pairs={{0,128},{64,192},{128,0},{192,64},{1,129},{65,193},{129,1},{193,65... | collective-permute-start | bytes 24584 | tf_op jit(solution)/shard_map/while/body/ppermute | solution.py:523
  43.2 0.9 %collective-permute-start.9 = (f32[16,128]{1,0:T(8,128)S(1)}, f32[16,128]{1,0:T(8,128)S(1)}, u32[]{:S(2)}, u32[]{:S(2)}) collective-permute-start(f32[16,128]{1,0:T(8,128)S(1)} %copy.28.m0), channel_id=1, source_target_pairs={{0,192},{64,0},{128,64},{192,128},{1,193},{65,1},{129,65},{193,129... | collective-permute-start | bytes 24584 | tf_op jit(solution)/shard_map/while/body/ppermute | solution.py:523
  44.2 2.8 %row_pairs.7 = (f32[3,2048]{1,0:T(4,128)S(1)}, s32[1]{0:T(128)}, s32[2176]{0:T(1024)}) custom-call(f32[152,128]{1,0:T(8,128)S(1)} %get-tuple-element.679.own, f32[64,128]{1,0:T(8,128)S(1)} %get-tuple-element.680.rec_t, f32[608,128]{1,0:T(8,128)S(1)} %get-tuple-element.681.rec_x, f32[3,2048]{1,0:T(4,128)S(1)} %get-tuple-element.652.so_far), custom_call_target="tpu_custom_call" | custom-call | flops 4000000000 | bytes 1 | tf_op jit(solution)/shard_map/while/body/row_pairs/pallas_call | solution.py:524
  47.6 3.1 %far.7 = f32[3,2048]{1,0:T(4,128)S(1)} custom-call(f32[152,128]{1,0:T(8,128)S(1)} %get-tuple-element.679.own, f32[16,128]{1,0:T(8,128)S(1)} %copy.28.m0, f32[16,128]{1,0:T(8,128)S(1)} %collective-permute-done.7.m1, f32[16,128]{1,0:T(8,128)S(1)} %collective-permute-done.8.m2, f32[16,128]{1,0:T(8,128)S(1)} %collective-permute-done.9.m3, ...), custom_call_target="tpu_custom_call" | custom-call | flops 1 | bytes 1 | tf_op jit(solution)/shard_map/while/body/far/pallas_call | solution.py:534
  50.7 0.6 while.41
  52.5 3.2 %all-to-all-done.2 = f32[8,128,128]{2,1,0:T(8,128)S(1)} async-done(((f32[8,128,128]{2,1,0:T(8,128)}), f32[8,128,128]{2,1,0:T(8,128)S(1)}, u32[]{:S(2)}, u32[]{:S(2)}) %all-to-all-start.2) | async-done | bytes 524320 | tf_op jit(solution)/shard_map/all_to_all | solution.py:550
  55.7 5.1 %near.7 = (f32[3,2048]{1,0:T(4,128)}, f32[256,128]{1,0:T(8,128)S(1)}) custom-call(f32[1024,128]{1,0:T(8,128)S(1)} %bitcast.24, s32[2176]{0:T(1024)} %get-tuple-element.726, f32[152,128]{1,0:T(8,128)S(1)} %get-tuple-element.728, f32[3,2048]{1,0:T(4,128)S(1)} %get-tuple-element.725, f32[1,2048]{1,0:T(1,128)S(1)} %get-tuple-element.733), custom_call_target="tpu_custom_call" | custom-call | tf_op jit(solution)/shard_map/near/pallas_call | solution.py:498
  60.8 17.9 %all_to_all.21 = f32[256,1,128]{2,1,0:T(1,128)S(1)} all-to-all(f32[256,1,128]{2,1,0:T(1,128)S(1)} %bitcast.27), channel_id=1, replica_groups=mesh['y'=4,'c'=2,'z'=8,'x'=4] {'y','c','z','x'}, dimensions={0} | all-to-all | bytes 262144 | tf_op jit(solution)/shard_map/all_to_all | solution.py:553
  78.7 0.7 step.1
  (9 shorter events, 0.0 us)
Async XLA Ops:
  2.4 10.6 %all-to-all-start = ((f32[4,152,128]{2,1,0:T(8,128)}), f32[4,152,128]{2,1,0:T(8,128)S(1)}, u32[]{:S(2)}, u32[]{:S(2)}) async-start(f32[4,152,128]{2,1,0:T(8,128)} %bitcast.37), calls=%async_computation | async-start | bytes 622592 | tf_op jit(solution)/shard_map/all_to_all | solution.py:439
  28.2 9.5 %collective-permute-start.10 = (f32[8,128]{1,0:T(8,128)S(1)}, f32[8,128]{1,0:T(8,128)S(1)}, u32[]{:S(2)}, u32[]{:S(2)}) collective-permute-start(f32[8,128]{1,0:T(8,128)S(1)} %reduce_sum.9), channel_id=1, source_target_pairs={{0,32},{32,0},{1,33},{33,1},{2,34},{34,2},{3,35},{35,3},{4,36},{36... | collective-permute-start | bytes 12296 | tf_op jit(solution)/shard_map/ppermute | solution.py:547
  34.2 21.5 %all-to-all-start.2 = ((f32[8,128,128]{2,1,0:T(8,128)}), f32[8,128,128]{2,1,0:T(8,128)S(1)}, u32[]{:S(2)}, u32[]{:S(2)}) async-start(f32[8,128,128]{2,1,0:T(8,128)} %bitcast.9), calls=%async_computation.2 | async-start | bytes 1048576 | tf_op jit(solution)/shard_map/all_to_all | solution.py:550
  37.7 0.7 copy-start.1
  37.8 0.7 copy-start.2
  39.1 8.5 %collective-permute-start.7 = (f32[16,128]{1,0:T(8,128)S(1)}, f32[16,128]{1,0:T(8,128)S(1)}, u32[]{:S(2)}, u32[]{:S(2)}) collective-permute-start(f32[16,128]{1,0:T(8,128)S(1)} %copy.28.m0), channel_id=1, source_target_pairs={{0,64},{64,128},{128,192},{192,0},{1,65},{65,129},{129,193},{193,1... | collective-permute-start | bytes 24584 | tf_op jit(solution)/shard_map/while/body/ppermute | solution.py:523
  40.4 7.2 %collective-permute-start.8 = (f32[16,128]{1,0:T(8,128)S(1)}, f32[16,128]{1,0:T(8,128)S(1)}, u32[]{:S(2)}, u32[]{:S(2)}) collective-permute-start(f32[16,128]{1,0:T(8,128)S(1)} %copy.28.m0), channel_id=1, source_target_pairs={{0,128},{64,192},{128,0},{192,64},{1,129},{65,193},{129,1},{193,65... | collective-permute-start | bytes 24584 | tf_op jit(solution)/shard_map/while/body/ppermute | solution.py:523
  43.2 4.4 %collective-permute-start.9 = (f32[16,128]{1,0:T(8,128)S(1)}, f32[16,128]{1,0:T(8,128)S(1)}, u32[]{:S(2)}, u32[]{:S(2)}) collective-permute-start(f32[16,128]{1,0:T(8,128)S(1)} %copy.28.m0), channel_id=1, source_target_pairs={{0,192},{64,0},{128,64},{192,128},{1,193},{65,1},{129,65},{193,129... | collective-permute-start | bytes 24584 | tf_op jit(solution)/shard_map/while/body/ppermute | solution.py:523
  60.8 17.9 %copy-start = (f32[3,2048]{1,0:T(4,128)S(1)}, f32[3,2048]{1,0:T(4,128)}, u32[]{:S(2)}) copy-start(f32[3,2048]{1,0:T(4,128)} %get-tuple-element.383.forces) | copy-start | bytes 73732

commit v7 on v6

--- a/solution.py
+++ b/solution.py
@@ -20,7 +20,6 @@
 SECT = 9 * CAP + 2
 TASKS = 2048
 COUNT = TASKS + 64
-UNROLL = 4
 PAD = 1 << 16
 F32 = jnp.float32
 BF16 = jnp.bfloat16
@@ -219,12 +218,12 @@
     return used_local
 
 
-def run_tasks(listed, count, blocks, apart, own, sides, acc):
+def run_tasks(listed, count, unroll, blocks, apart, own, sides, acc):
     columns = point_columns()
 
     def step(i, carry):
-        for u in range(UNROLL):
-            entry = listed[UNROLL * i + u]
+        for u in range(unroll):
+            entry = listed[unroll * i + u]
             base = entry & 4095
             k = (entry >> 12) & 15
 
@@ -237,7 +236,7 @@
                 acc[k, a] = acc[k, a] + near[a]
         return carry
 
-    lax.fori_loop(0, (count + UNROLL - 1) // UNROLL, step, 0)
+    lax.fori_loop(0, (count + unroll - 1) // unroll, step, 0)
 
 
 def tasks_kernel(turn_no, rec_t, tasks, lst, smem, cnt, sem, local):
@@ -353,7 +352,7 @@
     acc[...] = jnp.zeros_like(acc)
     copy.wait()
     used = place_tasks(0, count, local, tasks, smem, cnt)
-    run_tasks(local, used, rec_x, NB, own, sides, acc)
+    run_tasks(local, used, 4, rec_x, NB, own, sides, acc)
     write_forces(acc, forces, so_far)
 
 
@@ -403,7 +402,7 @@
 def near_kernel(rec_z, tasks, own, so_far, mobility, forces, tops, sides, acc):
     acc[...] = jnp.zeros_like(acc)
     own_sides(own, sides)
-    run_tasks(tasks, tasks[COUNT], rec_z, CAP, own, sides, acc)
+    run_tasks(tasks, tasks[COUNT], 8, rec_z, CAP, own, sides, acc)
     write_forces(acc, forces, so_far)
     v = mobility[...] * forces[...]
     speed = jnp.sum(v * v, axis=0, keepdims=True)

time: 79.7 us -> 79.8 us (level)
  Pallas kernels: 17.6 us -> 15.8 us
  blocking collectives: 33 us -> 34.7 us
    pallas_call x1, Pallas kernels: 5.13 us -> 3.33 us  [add_near(): pl.pallas_call(near_kernel, out_shape=(shape(3, seg_count), shape(devices...]
    all_to_all x1, blocking collectives: 17.9 us -> 19.6 us  [body(): lax.all_to_all(tops.reshape(devices, 1, BLK), ('y', 'c', 'z', 'x'), 0, 0,...]
where the time goes in v7:
time: 79.8 us; the launch traced here: 79.5 us
  blocking collectives  34.7 us (43%)
  starting transfers between devices  16.9 us (21%)
  Pallas kernels  15.8 us (20%)
  waiting for transfers between devices  7.63 us (10%)
  loops' own time  3.07 us (4%)
    all_to_all x1, blocking collectives, body(): lax.all_to_all(tops.reshape(devices, 1, BLK), ('y', 'c', 'z', 'x'), 0, 0,...  19.6 us
    all_to_all x1, blocking collectives, body(): rec_t = lax.all_to_all(row.reshape(NZ, 8, BLK), 'z', 0, 0, tiled=True)  15.1 us
    ppermute x3, starting transfers between devices, beside(): lax.ppermute(moments, 'y', [(i, (i + k) % 4) for i in range(4)])  5.01 us
    all_to_all x1, starting transfers between devices, body(): lax.all_to_all(packed.reshape(NX, ROWS, BLK), 'x', 0, 0, tiled=True)  4.85 us
    all_to_all x1, waiting for transfers between devices, body(): lax.all_to_all(packed.reshape(NX, ROWS, BLK), 'x', 0, 0, tiled=True)  4.15 us
    ppermute x1, starting transfers between devices, body(): lax.ppermute(group, 'c', [(0, 1), (1, 0)])  3.57 us
    all_to_all x1, starting transfers between devices, body(): rec_z = lax.all_to_all(send.reshape(NZ, SECT, BLK), 'z', 0, 0, tiled=True)  3.5 us
    all_to_all x1, waiting for transfers between devices, body(): rec_z = lax.all_to_all(send.reshape(NZ, SECT, BLK), 'z', 0, 0, tiled=True)  3.48 us
  transfers between devices with their start and end apart: 6, of which 2 were waited for; matrix products, arithmetic and copies ran while one was open for 0% of the time, Pallas kernels for 9%

profile of v7, /device:TPU:1, one launch (start us, length us, event | category | flops | bytes accessed | tf_op | source)
XLA Modules:
  0.0 79.5 jit_solution(17668997417352920956)
XLA Ops:
  0.6 1.8 %pack.1 = (f32[608,128]{1,0:T(8,128)}, f32[152,128]{1,0:T(8,128)S(1)}, s32[16]{0:T(128)S(1)}) custom-call(f32[9,2048]{1,0:T(8,128)} %seg.1, s32[16]{0:T(128)} %cells.1, s32[2,32]{1,0:T(2,128)} %bitcast.38), custom_call_target="tpu_custom_call" | custom-call | tf_op jit(solution)/shard_map/pack/pallas_call | solution.py:431
  2.4 4.9 %all-to-all-start = ((f32[4,152,128]{2,1,0:T(8,128)}), f32[4,152,128]{2,1,0:T(8,128)S(1)}, u32[]{:S(2)}, u32[]{:S(2)}) async-start(f32[4,152,128]{2,1,0:T(8,128)} %bitcast.37), calls=%async_computation | async-start | bytes 622592 | tf_op jit(solution)/shard_map/all_to_all | solution.py:438
  7.3 1.6 %own.1 = f32[3,2048]{1,0:T(4,128)S(1)} custom-call(f32[152,128]{1,0:T(8,128)S(1)} %get-tuple-element.631.own), custom_call_target="tpu_custom_call" | custom-call | flops 1000000000 | bytes 1 | tf_op jit(solution)/shard_map/own/pallas_call | solution.py:441
  8.9 4.1 %all-to-all-done = f32[4,152,128]{2,1,0:T(8,128)S(1)} async-done(((f32[4,152,128]{2,1,0:T(8,128)}), f32[4,152,128]{2,1,0:T(8,128)S(1)}, u32[]{:S(2)}, u32[]{:S(2)}) %all-to-all-start) | async-done | bytes 311328 | tf_op jit(solution)/shard_map/all_to_all | solution.py:438
  13.1 0.1 row.1
  13.1 15.1 %all_to_all.20 = f32[8,8,128]{2,1,0:T(8,128)S(1)} all-to-all(f32[8,8,128]{2,1,0:T(8,128)S(1)} %bitcast.26), channel_id=1, replica_groups=mesh['y'=4,'c'=2,'z'=8,'x'=4] {'z'}, dimensions={0} | all-to-all | bytes 65536 | tf_op jit(solution)/shard_map/all_to_all | solution.py:461
  28.2 3.6 %collective-permute-start.10 = (f32[8,128]{1,0:T(8,128)S(1)}, f32[8,128]{1,0:T(8,128)S(1)}, u32[]{:S(2)}, u32[]{:S(2)}) collective-permute-start(f32[8,128]{1,0:T(8,128)S(1)} %reduce_sum.9), channel_id=1, source_target_pairs={{0,32},{32,0},{1,33},{33,1},{2,34},{34,2},{3,35},{35,3},{4,36},{36... | collective-permute-start | bytes 12296 | tf_op jit(solution)/shard_map/ppermute | solution.py:546
  31.8 2.5 %send.7 = (f32[1024,128]{1,0:T(8,128)}, s32[1]{0:T(128)}, s32[2176]{0:T(1024)}) custom-call(s32[1]{0:T(128)} %constant.297.clone.1.turn_no, f32[64,128]{1,0:T(8,128)S(1)} %bitcast.34, f32[608,128]{1,0:T(8,128)S(1)} %bitcast.32), custom_call_target="tpu_custom_call" | custom-call | tf_op jit(solution)/shard_map/send/pallas_call | solution.py:474
  34.3 3.5 %all-to-all-start.2 = ((f32[8,128,128]{2,1,0:T(8,128)}), f32[8,128,128]{2,1,0:T(8,128)S(1)}, u32[]{:S(2)}, u32[]{:S(2)}) async-start(f32[8,128,128]{2,1,0:T(8,128)} %bitcast.9), calls=%async_computation.2 | async-start | bytes 1048576 | tf_op jit(solution)/shard_map/all_to_all | solution.py:549
  37.8 0.0 copy-start.1
  37.9 0.0 copy-start.2
  37.9 0.7 copy-done.1
  38.5 0.0 copy-done.2
  38.6 13.8 %while.40 = (s32[1]{0:T(128)}, f32[3,2048]{1,0:T(4,128)S(1)}, s32[2176]{0:T(1024)}, f32[16,128]{1,0:T(8,128)S(1)}, f32[152,128]{1,0:T(8,128)S(1)}, /*index=5*/f3...) while((s32[1]{0:T(128)}, f32[3,2048]{1,0:T(4,128)S(1)}, ...), condition=%wide.region_4.5_spmd, body=%wide.region_1.4_spmd.sunk | while | flops 4000000000 | bytes 4360270 | solution.py:550
  39.2 1.0 %collective-permute-start.7 = (f32[16,128]{1,0:T(8,128)S(1)}, f32[16,128]{1,0:T(8,128)S(1)}, u32[]{:S(2)}, u32[]{:S(2)}) collective-permute-start(f32[16,128]{1,0:T(8,128)S(1)} %copy.28.m0), channel_id=1, source_target_pairs={{0,64},{64,128},{128,192},{192,0},{1,65},{65,129},{129,193},{193,1... | collective-permute-start | bytes 24584 | tf_op jit(solution)/shard_map/while/body/ppermute | solution.py:522
  40.3 2.6 %collective-permute-start.8 = (f32[16,128]{1,0:T(8,128)S(1)}, f32[16,128]{1,0:T(8,128)S(1)}, u32[]{:S(2)}, u32[]{:S(2)}) collective-permute-start(f32[16,128]{1,0:T(8,128)S(1)} %copy.28.m0), channel_id=1, source_target_pairs={{0,128},{64,192},{128,0},{192,64},{1,129},{65,193},{129,1},{193,65... | collective-permute-start | bytes 24584 | tf_op jit(solution)/shard_map/while/body/ppermute | solution.py:522
  42.9 1.4 %collective-permute-start.9 = (f32[16,128]{1,0:T(8,128)S(1)}, f32[16,128]{1,0:T(8,128)S(1)}, u32[]{:S(2)}, u32[]{:S(2)}) collective-permute-start(f32[16,128]{1,0:T(8,128)S(1)} %copy.28.m0), channel_id=1, source_target_pairs={{0,192},{64,0},{128,64},{192,128},{1,193},{65,1},{129,65},{193,129... | collective-permute-start | bytes 24584 | tf_op jit(solution)/shard_map/while/body/ppermute | solution.py:522
  44.2 2.6 %row_pairs.7 = (f32[3,2048]{1,0:T(4,128)S(1)}, s32[1]{0:T(128)}, s32[2176]{0:T(1024)}) custom-call(f32[152,128]{1,0:T(8,128)S(1)} %get-tuple-element.679.own, f32[64,128]{1,0:T(8,128)S(1)} %get-tuple-element.680.rec_t, f32[608,128]{1,0:T(8,128)S(1)} %get-tuple-element.681.rec_x, f32[3,2048]{1,0:T(4,128)S(1)} %get-tuple-element.652.so_far), custom_call_target="tpu_custom_call" | custom-call | flops 4000000000 | bytes 1 | tf_op jit(solution)/shard_map/while/body/row_pairs/pallas_call | solution.py:523
  47.5 3.1 %far.7 = f32[3,2048]{1,0:T(4,128)S(1)} custom-call(f32[152,128]{1,0:T(8,128)S(1)} %get-tuple-element.679.own, f32[16,128]{1,0:T(8,128)S(1)} %copy.28.m0, f32[16,128]{1,0:T(8,128)S(1)} %collective-permute-done.7.m1, f32[16,128]{1,0:T(8,128)S(1)} %collective-permute-done.8.m2, f32[16,128]{1,0:T(8,128)S(1)} %collective-permute-done.9.m3, ...), custom_call_target="tpu_custom_call" | custom-call | flops 1 | bytes 1 | tf_op jit(solution)/shard_map/while/body/far/pallas_call | solution.py:533
  50.6 0.6 while.41
  52.4 3.5 %all-to-all-done.2 = f32[8,128,128]{2,1,0:T(8,128)S(1)} async-done(((f32[8,128,128]{2,1,0:T(8,128)}), f32[8,128,128]{2,1,0:T(8,128)S(1)}, u32[]{:S(2)}, u32[]{:S(2)}) %all-to-all-start.2) | async-done | bytes 524320 | tf_op jit(solution)/shard_map/all_to_all | solution.py:549
  55.8 3.3 %near.7 = (f32[3,2048]{1,0:T(4,128)}, f32[256,128]{1,0:T(8,128)S(1)}) custom-call(f32[1024,128]{1,0:T(8,128)S(1)} %bitcast.24, s32[2176]{0:T(1024)} %get-tuple-element.726, f32[152,128]{1,0:T(8,128)S(1)} %get-tuple-element.728, f32[3,2048]{1,0:T(4,128)S(1)} %get-tuple-element.725, f32[1,2048]{1,0:T(1,128)S(1)} %get-tuple-element.733), custom_call_target="tpu_custom_call" | custom-call | tf_op jit(solution)/shard_map/near/pallas_call | solution.py:497
  59.2 19.6 %all_to_all.21 = f32[256,1,128]{2,1,0:T(1,128)S(1)} all-to-all(f32[256,1,128]{2,1,0:T(1,128)S(1)} %bitcast.27), channel_id=1, replica_groups=mesh['y'=4,'c'=2,'z'=8,'x'=4] {'y','c','z','x'}, dimensions={0} | all-to-all | bytes 262144 | tf_op jit(solution)/shard_map/all_to_all | solution.py:552
  78.8 0.7 step.1
  (9 shorter events, 0.0 us)
Async XLA Ops:
  2.4 10.6 %all-to-all-start = ((f32[4,152,128]{2,1,0:T(8,128)}), f32[4,152,128]{2,1,0:T(8,128)S(1)}, u32[]{:S(2)}, u32[]{:S(2)}) async-start(f32[4,152,128]{2,1,0:T(8,128)} %bitcast.37), calls=%async_computation | async-start | bytes 622592 | tf_op jit(solution)/shard_map/all_to_all | solution.py:438
  28.2 9.6 %collective-permute-start.10 = (f32[8,128]{1,0:T(8,128)S(1)}, f32[8,128]{1,0:T(8,128)S(1)}, u32[]{:S(2)}, u32[]{:S(2)}) collective-permute-start(f32[8,128]{1,0:T(8,128)S(1)} %reduce_sum.9), channel_id=1, source_target_pairs={{0,32},{32,0},{1,33},{33,1},{2,34},{34,2},{3,35},{35,3},{4,36},{36... | collective-permute-start | bytes 12296 | tf_op jit(solution)/shard_map/ppermute | solution.py:546
  34.3 21.5 %all-to-all-start.2 = ((f32[8,128,128]{2,1,0:T(8,128)}), f32[8,128,128]{2,1,0:T(8,128)S(1)}, u32[]{:S(2)}, u32[]{:S(2)}) async-start(f32[8,128,128]{2,1,0:T(8,128)} %bitcast.9), calls=%async_computation.2 | async-start | bytes 1048576 | tf_op jit(solution)/shard_map/all_to_all | solution.py:549
  37.8 0.7 copy-start.1
  37.9 0.7 copy-start.2
  39.2 8.2 %collective-permute-start.7 = (f32[16,128]{1,0:T(8,128)S(1)}, f32[16,128]{1,0:T(8,128)S(1)}, u32[]{:S(2)}, u32[]{:S(2)}) collective-permute-start(f32[16,128]{1,0:T(8,128)S(1)} %copy.28.m0), channel_id=1, source_target_pairs={{0,64},{64,128},{128,192},{192,0},{1,65},{65,129},{129,193},{193,1... | collective-permute-start | bytes 24584 | tf_op jit(solution)/shard_map/while/body/ppermute | solution.py:522
  40.3 7.2 %collective-permute-start.8 = (f32[16,128]{1,0:T(8,128)S(1)}, f32[16,128]{1,0:T(8,128)S(1)}, u32[]{:S(2)}, u32[]{:S(2)}) collective-permute-start(f32[16,128]{1,0:T(8,128)S(1)} %copy.28.m0), channel_id=1, source_target_pairs={{0,128},{64,192},{128,0},{192,64},{1,129},{65,193},{129,1},{193,65... | collective-permute-start | bytes 24584 | tf_op jit(solution)/shard_map/while/body/ppermute | solution.py:522
  42.9 4.6 %collective-permute-start.9 = (f32[16,128]{1,0:T(8,128)S(1)}, f32[16,128]{1,0:T(8,128)S(1)}, u32[]{:S(2)}, u32[]{:S(2)}) collective-permute-start(f32[16,128]{1,0:T(8,128)S(1)} %copy.28.m0), channel_id=1, source_target_pairs={{0,192},{64,0},{128,64},{192,128},{1,193},{65,1},{129,65},{193,129... | collective-permute-start | bytes 24584 | tf_op jit(solution)/shard_map/while/body/ppermute | solution.py:522
  59.2 19.6 %copy-start = (f32[3,2048]{1,0:T(4,128)S(1)}, f32[3,2048]{1,0:T(4,128)}, u32[]{:S(2)}) copy-start(f32[3,2048]{1,0:T(4,128)} %get-tuple-element.383.forces) | copy-start | bytes 73732

commit v8 on v7

--- a/solution.py
+++ b/solution.py
@@ -384,8 +384,8 @@
     own_sides(own, sides)
 
     def step(i, carry):
-        for u in range(2):
-            k = 2 * i + u
+        for u in range(4):
+            k = 4 * i + u
             here = [own[pl.ds(a * NB + k, 1), :] for a in range(3)]
             parts = [
                 pull(others[h], [there[h, a] for a in range(3)], sides[k], here, FAR_CORE, cells[k] - h * BLK)
@@ -395,7 +395,7 @@
                 acc[k, a] = parts[0][a] + parts[1][a]
         return carry
 
-    lax.fori_loop(0, NB // 2, step, 0)
+    lax.fori_loop(0, NB // 4, step, 0)
     write_forces(acc, forces, so_far)
 
 

time: 79.8 us -> 79.2 us (level)
    pallas_call x1, Pallas kernels: 2.58 us -> 3.38 us  [beside(): pl.pallas_call(row_pairs_kernel, out_shape=(shape(3, seg_count), shape(1,...]
  transfers between devices with their start and end apart: 6 -> 6, of which waited for: 2 -> 2; matrix products, arithmetic and copies ran while one was open for 0% -> 0% of each run, Pallas kernels for 9% -> 10%
where the time goes in v8:
time: 79.2 us; the launch traced here: 78.7 us
  blocking collectives  34.8 us (44%)
  starting transfers between devices  17.1 us (22%)
  Pallas kernels  15.4 us (19%)
  waiting for transfers between devices  6.88 us (9%)
  loops' own time  3.07 us (4%)
    all_to_all x1, blocking collectives, body(): lax.all_to_all(tops.reshape(devices, 1, BLK), ('y', 'c', 'z', 'x'), 0, 0,...  19.8 us
    all_to_all x1, blocking collectives, body(): rec_t = lax.all_to_all(row.reshape(NZ, 8, BLK), 'z', 0, 0, tiled=True)  15.1 us
    ppermute x3, starting transfers between devices, beside(): lax.ppermute(moments, 'y', [(i, (i + k) % 4) for i in range(4)])  5.21 us
    all_to_all x1, starting transfers between devices, body(): lax.all_to_all(packed.reshape(NX, ROWS, BLK), 'x', 0, 0, tiled=True)  4.85 us
    all_to_all x1, waiting for transfers between devices, body(): lax.all_to_all(packed.reshape(NX, ROWS, BLK), 'x', 0, 0, tiled=True)  4.15 us
    ppermute x1, starting transfers between devices, body(): lax.ppermute(group, 'c', [(0, 1), (1, 0)])  3.57 us
    all_to_all x1, starting transfers between devices, body(): rec_z = lax.all_to_all(send.reshape(NZ, SECT, BLK), 'z', 0, 0, tiled=True)  3.5 us
    pallas_call x1, Pallas kernels, beside(): pl.pallas_call(row_pairs_kernel, out_shape=(shape(3, seg_count), shape(1,...  3.38 us
  transfers between devices with their start and end apart: 6, of which 2 were waited for; matrix products, arithmetic and copies ran while one was open for 0% of the time, Pallas kernels for 10%

profile of v8, /device:TPU:1, one launch (start us, length us, event | category | flops | bytes accessed | tf_op | source)
XLA Modules:
  0.0 78.7 jit_solution(11155518846530943364)
XLA Ops:
  0.6 1.8 %pack.1 = (f32[608,128]{1,0:T(8,128)}, f32[152,128]{1,0:T(8,128)S(1)}, s32[16]{0:T(128)S(1)}) custom-call(f32[9,2048]{1,0:T(8,128)} %seg.1, s32[16]{0:T(128)} %cells.1, s32[2,32]{1,0:T(2,128)} %bitcast.38), custom_call_target="tpu_custom_call" | custom-call | tf_op jit(solution)/shard_map/pack/pallas_call | solution.py:431
  2.4 4.9 %all-to-all-start = ((f32[4,152,128]{2,1,0:T(8,128)}), f32[4,152,128]{2,1,0:T(8,128)S(1)}, u32[]{:S(2)}, u32[]{:S(2)}) async-start(f32[4,152,128]{2,1,0:T(8,128)} %bitcast.37), calls=%async_computation | async-start | bytes 622592 | tf_op jit(solution)/shard_map/all_to_all | solution.py:438
  7.3 1.6 %own.1 = f32[3,2048]{1,0:T(4,128)S(1)} custom-call(f32[152,128]{1,0:T(8,128)S(1)} %get-tuple-element.631.own), custom_call_target="tpu_custom_call" | custom-call | flops 1000000000 | bytes 1 | tf_op jit(solution)/shard_map/own/pallas_call | solution.py:441
  8.9 4.1 %all-to-all-done = f32[4,152,128]{2,1,0:T(8,128)S(1)} async-done(((f32[4,152,128]{2,1,0:T(8,128)}), f32[4,152,128]{2,1,0:T(8,128)S(1)}, u32[]{:S(2)}, u32[]{:S(2)}) %all-to-all-start) | async-done | bytes 311328 | tf_op jit(solution)/shard_map/all_to_all | solution.py:438
  13.1 0.1 row.1
  13.1 15.1 %all_to_all.20 = f32[8,8,128]{2,1,0:T(8,128)S(1)} all-to-all(f32[8,8,128]{2,1,0:T(8,128)S(1)} %bitcast.26), channel_id=1, replica_groups=mesh['y'=4,'c'=2,'z'=8,'x'=4] {'z'}, dimensions={0} | all-to-all | bytes 65536 | tf_op jit(solution)/shard_map/all_to_all | solution.py:461
  28.2 3.6 %collective-permute-start.10 = (f32[8,128]{1,0:T(8,128)S(1)}, f32[8,128]{1,0:T(8,128)S(1)}, u32[]{:S(2)}, u32[]{:S(2)}) collective-permute-start(f32[8,128]{1,0:T(8,128)S(1)} %reduce_sum.9), channel_id=1, source_target_pairs={{0,32},{32,0},{1,33},{33,1},{2,34},{34,2},{3,35},{35,3},{4,36},{36... | collective-permute-start | bytes 12296 | tf_op jit(solution)/shard_map/ppermute | solution.py:546
  31.8 2.2 %send.7 = (f32[1024,128]{1,0:T(8,128)}, s32[1]{0:T(128)}, s32[2176]{0:T(1024)}) custom-call(s32[1]{0:T(128)} %constant.297.clone.1.turn_no, f32[64,128]{1,0:T(8,128)S(1)} %bitcast.34, f32[608,128]{1,0:T(8,128)S(1)} %bitcast.32), custom_call_target="tpu_custom_call" | custom-call | tf_op jit(solution)/shard_map/send/pallas_call | solution.py:474
  34.0 3.5 %all-to-all-start.2 = ((f32[8,128,128]{2,1,0:T(8,128)}), f32[8,128,128]{2,1,0:T(8,128)S(1)}, u32[]{:S(2)}, u32[]{:S(2)}) async-start(f32[8,128,128]{2,1,0:T(8,128)} %bitcast.9), calls=%async_computation.2 | async-start | bytes 1048576 | tf_op jit(solution)/shard_map/all_to_all | solution.py:549
  37.5 0.0 copy-start.1
  37.6 0.0 copy-start.2
  37.6 0.7 copy-done.1
  38.2 0.0 copy-done.2
  38.3 14.5 %while.40 = (s32[1]{0:T(128)}, f32[3,2048]{1,0:T(4,128)S(1)}, s32[2176]{0:T(1024)}, f32[16,128]{1,0:T(8,128)S(1)}, f32[152,128]{1,0:T(8,128)S(1)}, /*index=5*/f3...) while((s32[1]{0:T(128)}, f32[3,2048]{1,0:T(4,128)S(1)}, ...), condition=%wide.region_4.5_spmd, body=%wide.region_1.4_spmd.sunk | while | flops 4000000000 | bytes 4360270 | solution.py:550
  38.9 1.7 %collective-permute-start.7 = (f32[16,128]{1,0:T(8,128)S(1)}, f32[16,128]{1,0:T(8,128)S(1)}, u32[]{:S(2)}, u32[]{:S(2)}) collective-permute-start(f32[16,128]{1,0:T(8,128)S(1)} %copy.28.m0), channel_id=1, source_target_pairs={{0,64},{64,128},{128,192},{192,0},{1,65},{65,129},{129,193},{193,1... | collective-permute-start | bytes 24584 | tf_op jit(solution)/shard_map/while/body/ppermute | solution.py:522
  40.6 2.5 %collective-permute-start.8 = (f32[16,128]{1,0:T(8,128)S(1)}, f32[16,128]{1,0:T(8,128)S(1)}, u32[]{:S(2)}, u32[]{:S(2)}) collective-permute-start(f32[16,128]{1,0:T(8,128)S(1)} %copy.28.m0), channel_id=1, source_target_pairs={{0,128},{64,192},{128,0},{192,64},{1,129},{65,193},{129,1},{193,65... | collective-permute-start | bytes 24584 | tf_op jit(solution)/shard_map/while/body/ppermute | solution.py:522
  43.1 1.0 %collective-permute-start.9 = (f32[16,128]{1,0:T(8,128)S(1)}, f32[16,128]{1,0:T(8,128)S(1)}, u32[]{:S(2)}, u32[]{:S(2)}) collective-permute-start(f32[16,128]{1,0:T(8,128)S(1)} %copy.28.m0), channel_id=1, source_target_pairs={{0,192},{64,0},{128,64},{192,128},{1,193},{65,1},{129,65},{193,129... | collective-permute-start | bytes 24584 | tf_op jit(solution)/shard_map/while/body/ppermute | solution.py:522
  44.1 3.4 %row_pairs.7 = (f32[3,2048]{1,0:T(4,128)S(1)}, s32[1]{0:T(128)}, s32[2176]{0:T(1024)}) custom-call(f32[152,128]{1,0:T(8,128)S(1)} %get-tuple-element.679.own, f32[64,128]{1,0:T(8,128)S(1)} %get-tuple-element.680.rec_t, f32[608,128]{1,0:T(8,128)S(1)} %get-tuple-element.681.rec_x, f32[3,2048]{1,0:T(4,128)S(1)} %get-tuple-element.652.so_far), custom_call_target="tpu_custom_call" | custom-call | flops 4000000000 | bytes 1 | tf_op jit(solution)/shard_map/while/body/row_pairs/pallas_call | solution.py:523
  48.2 2.8 %far.7 = f32[3,2048]{1,0:T(4,128)S(1)} custom-call(f32[152,128]{1,0:T(8,128)S(1)} %get-tuple-element.679.own, f32[16,128]{1,0:T(8,128)S(1)} %copy.28.m0, f32[16,128]{1,0:T(8,128)S(1)} %collective-permute-done.7.m1, f32[16,128]{1,0:T(8,128)S(1)} %collective-permute-done.8.m2, f32[16,128]{1,0:T(8,128)S(1)} %collective-permute-done.9.m3, ...), custom_call_target="tpu_custom_call" | custom-call | flops 1 | bytes 1 | tf_op jit(solution)/shard_map/while/body/far/pallas_call | solution.py:533
  51.0 0.6 while.41
  52.8 2.7 %all-to-all-done.2 = f32[8,128,128]{2,1,0:T(8,128)S(1)} async-done(((f32[8,128,128]{2,1,0:T(8,128)}), f32[8,128,128]{2,1,0:T(8,128)S(1)}, u32[]{:S(2)}, u32[]{:S(2)}) %all-to-all-start.2) | async-done | bytes 524320 | tf_op jit(solution)/shard_map/all_to_all | solution.py:549
  55.5 2.7 %near.7 = (f32[3,2048]{1,0:T(4,128)}, f32[256,128]{1,0:T(8,128)S(1)}) custom-call(f32[1024,128]{1,0:T(8,128)S(1)} %bitcast.24, s32[2176]{0:T(1024)} %get-tuple-element.726, f32[152,128]{1,0:T(8,128)S(1)} %get-tuple-element.728, f32[3,2048]{1,0:T(4,128)S(1)} %get-tuple-element.725, f32[1,2048]{1,0:T(1,128)S(1)} %get-tuple-element.733), custom_call_target="tpu_custom_call" | custom-call | tf_op jit(solution)/shard_map/near/pallas_call | solution.py:497
  58.2 19.8 %all_to_all.21 = f32[256,1,128]{2,1,0:T(1,128)S(1)} all-to-all(f32[256,1,128]{2,1,0:T(1,128)S(1)} %bitcast.27), channel_id=1, replica_groups=mesh['y'=4,'c'=2,'z'=8,'x'=4] {'y','c','z','x'}, dimensions={0} | all-to-all | bytes 262144 | tf_op jit(solution)/shard_map/all_to_all | solution.py:552
  78.0 0.7 step.1
  (9 shorter events, 0.0 us)
Async XLA Ops:
  2.4 10.6 %all-to-all-start = ((f32[4,152,128]{2,1,0:T(8,128)}), f32[4,152,128]{2,1,0:T(8,128)S(1)}, u32[]{:S(2)}, u32[]{:S(2)}) async-start(f32[4,152,128]{2,1,0:T(8,128)} %bitcast.37), calls=%async_computation | async-start | bytes 622592 | tf_op jit(solution)/shard_map/all_to_all | solution.py:438
  28.2 9.3 %collective-permute-start.10 = (f32[8,128]{1,0:T(8,128)S(1)}, f32[8,128]{1,0:T(8,128)S(1)}, u32[]{:S(2)}, u32[]{:S(2)}) collective-permute-start(f32[8,128]{1,0:T(8,128)S(1)} %reduce_sum.9), channel_id=1, source_target_pairs={{0,32},{32,0},{1,33},{33,1},{2,34},{34,2},{3,35},{35,3},{4,36},{36... | collective-permute-start | bytes 12296 | tf_op jit(solution)/shard_map/ppermute | solution.py:546
  34.0 21.5 %all-to-all-start.2 = ((f32[8,128,128]{2,1,0:T(8,128)}), f32[8,128,128]{2,1,0:T(8,128)S(1)}, u32[]{:S(2)}, u32[]{:S(2)}) async-start(f32[8,128,128]{2,1,0:T(8,128)} %bitcast.9), calls=%async_computation.2 | async-start | bytes 1048576 | tf_op jit(solution)/shard_map/all_to_all | solution.py:549
  37.5 0.7 copy-start.1
  37.6 0.7 copy-start.2
  38.9 9.2 %collective-permute-start.7 = (f32[16,128]{1,0:T(8,128)S(1)}, f32[16,128]{1,0:T(8,128)S(1)}, u32[]{:S(2)}, u32[]{:S(2)}) collective-permute-start(f32[16,128]{1,0:T(8,128)S(1)} %copy.28.m0), channel_id=1, source_target_pairs={{0,64},{64,128},{128,192},{192,0},{1,65},{65,129},{129,193},{193,1... | collective-permute-start | bytes 24584 | tf_op jit(solution)/shard_map/while/body/ppermute | solution.py:522
  40.6 7.6 %collective-permute-start.8 = (f32[16,128]{1,0:T(8,128)S(1)}, f32[16,128]{1,0:T(8,128)S(1)}, u32[]{:S(2)}, u32[]{:S(2)}) collective-permute-start(f32[16,128]{1,0:T(8,128)S(1)} %copy.28.m0), channel_id=1, source_target_pairs={{0,128},{64,192},{128,0},{192,64},{1,129},{65,193},{129,1},{193,65... | collective-permute-start | bytes 24584 | tf_op jit(solution)/shard_map/while/body/ppermute | solution.py:522
  43.1 5.1 %collective-permute-start.9 = (f32[16,128]{1,0:T(8,128)S(1)}, f32[16,128]{1,0:T(8,128)S(1)}, u32[]{:S(2)}, u32[]{:S(2)}) collective-permute-start(f32[16,128]{1,0:T(8,128)S(1)} %copy.28.m0), channel_id=1, source_target_pairs={{0,192},{64,0},{128,64},{192,128},{1,193},{65,1},{129,65},{193,129... | collective-permute-start | bytes 24584 | tf_op jit(solution)/shard_map/while/body/ppermute | solution.py:522
  58.2 19.8 %copy-start = (f32[3,2048]{1,0:T(4,128)S(1)}, f32[3,2048]{1,0:T(4,128)}, u32[]{:S(2)}) copy-start(f32[3,2048]{1,0:T(4,128)} %get-tuple-element.383.forces) | copy-start | bytes 73732

commit v9 on v8

--- a/solution.py
+++ b/solution.py
@@ -16,8 +16,8 @@
 NG = 8
 EXTRA = 9 * NB
 ROWS = EXTRA + 8
-CAP = 14
-SECT = 9 * CAP + 2
+CAP = 13
+SECT = 9 * CAP + 3
 TASKS = 2048
 COUNT = TASKS + 64
 PAD = 1 << 16

time: 79.2 us -> 79.4 us (level)
    pallas_call x1, Pallas kernels: 2.74 us -> 3.94 us  [add_near(): pl.pallas_call(near_kernel, out_shape=(shape(3, seg_count), shape(devices...]
  transfers between devices with their start and end apart: 6 -> 6, of which waited for: 2 -> 2; matrix products, arithmetic and copies ran while one was open for 0% -> 0% of each run, Pallas kernels for 10% -> 9%
where the time goes in v9:
time: 79.4 us; the launch traced here: 79 us
  blocking collectives  34.4 us (43%)
  starting transfers between devices  17 us (21%)
  Pallas kernels  16.1 us (20%)
  waiting for transfers between devices  6.63 us (8%)
  loops' own time  3.42 us (4%)
    all_to_all x1, blocking collectives, body(): lax.all_to_all(tops.reshape(devices, 1, BLK), ('y', 'c', 'z', 'x'), 0, 0,...  19.3 us
    all_to_all x1, blocking collectives, body(): rec_t = lax.all_to_all(row.reshape(NZ, 8, BLK), 'z', 0, 0, tiled=True)  15.1 us
    ppermute x3, starting transfers between devices, beside(): lax.ppermute(moments, 'y', [(i, (i + k) % 4) for i in range(4)])  5.13 us
    all_to_all x1, starting transfers between devices, body(): lax.all_to_all(packed.reshape(NX, ROWS, BLK), 'x', 0, 0, tiled=True)  4.85 us
    all_to_all x1, waiting for transfers between devices, body(): lax.all_to_all(packed.reshape(NX, ROWS, BLK), 'x', 0, 0, tiled=True)  4.15 us
    pallas_call x1, Pallas kernels, add_near(): pl.pallas_call(near_kernel, out_shape=(shape(3, seg_count), shape(devices...  3.94 us
    ppermute x1, starting transfers between devices, body(): lax.ppermute(group, 'c', [(0, 1), (1, 0)])  3.57 us
    all_to_all x1, starting transfers between devices, body(): rec_z = lax.all_to_all(send.reshape(NZ, SECT, BLK), 'z', 0, 0, tiled=True)  3.49 us
  transfers between devices with their start and end apart: 6, of which 2 were waited for; matrix products, arithmetic and copies ran while one was open for 0% of the time, Pallas kernels for 9%

profile of v9, /device:TPU:1, one launch (start us, length us, event | category | flops | bytes accessed | tf_op | source)
XLA Modules:
  0.0 79.0 jit_solution(6653977231325058723)
XLA Ops:
  0.6 1.8 %pack.1 = (f32[608,128]{1,0:T(8,128)}, f32[152,128]{1,0:T(8,128)S(1)}, s32[16]{0:T(128)S(1)}) custom-call(f32[9,2048]{1,0:T(8,128)} %seg.1, s32[16]{0:T(128)} %cells.1, s32[2,32]{1,0:T(2,128)} %bitcast.38), custom_call_target="tpu_custom_call" | custom-call | tf_op jit(solution)/shard_map/pack/pallas_call | solution.py:431
  2.4 4.9 %all-to-all-start = ((f32[4,152,128]{2,1,0:T(8,128)}), f32[4,152,128]{2,1,0:T(8,128)S(1)}, u32[]{:S(2)}, u32[]{:S(2)}) async-start(f32[4,152,128]{2,1,0:T(8,128)} %bitcast.37), calls=%async_computation | async-start | bytes 622592 | tf_op jit(solution)/shard_map/all_to_all | solution.py:438
  7.3 1.6 %own.1 = f32[3,2048]{1,0:T(4,128)S(1)} custom-call(f32[152,128]{1,0:T(8,128)S(1)} %get-tuple-element.631.own), custom_call_target="tpu_custom_call" | custom-call | flops 1000000000 | bytes 1 | tf_op jit(solution)/shard_map/own/pallas_call | solution.py:441
  8.9 4.1 %all-to-all-done = f32[4,152,128]{2,1,0:T(8,128)S(1)} async-done(((f32[4,152,128]{2,1,0:T(8,128)}), f32[4,152,128]{2,1,0:T(8,128)S(1)}, u32[]{:S(2)}, u32[]{:S(2)}) %all-to-all-start) | async-done | bytes 311328 | tf_op jit(solution)/shard_map/all_to_all | solution.py:438
  13.1 0.1 row.1
  13.1 15.1 %all_to_all.20 = f32[8,8,128]{2,1,0:T(8,128)S(1)} all-to-all(f32[8,8,128]{2,1,0:T(8,128)S(1)} %bitcast.26), channel_id=1, replica_groups=mesh['y'=4,'c'=2,'z'=8,'x'=4] {'z'}, dimensions={0} | all-to-all | bytes 65536 | tf_op jit(solution)/shard_map/all_to_all | solution.py:461
  28.2 3.6 %collective-permute-start.10 = (f32[8,128]{1,0:T(8,128)S(1)}, f32[8,128]{1,0:T(8,128)S(1)}, u32[]{:S(2)}, u32[]{:S(2)}) collective-permute-start(f32[8,128]{1,0:T(8,128)S(1)} %reduce_sum.9), channel_id=1, source_target_pairs={{0,32},{32,0},{1,33},{33,1},{2,34},{34,2},{3,35},{35,3},{4,36},{36... | collective-permute-start | bytes 12296 | tf_op jit(solution)/shard_map/ppermute | solution.py:546
  31.8 2.4 %send.7 = (f32[960,128]{1,0:T(8,128)}, s32[1]{0:T(128)}, s32[2176]{0:T(1024)}) custom-call(s32[1]{0:T(128)} %constant.297.clone.1.turn_no, f32[64,128]{1,0:T(8,128)S(1)} %bitcast.34, f32[608,128]{1,0:T(8,128)S(1)} %bitcast.32), custom_call_target="tpu_custom_call" | custom-call | tf_op jit(solution)/shard_map/send/pallas_call | solution.py:474
  34.2 3.5 %all-to-all-start.2 = ((f32[8,120,128]{2,1,0:T(8,128)}), f32[8,120,128]{2,1,0:T(8,128)S(1)}, u32[]{:S(2)}, u32[]{:S(2)}) async-start(f32[8,120,128]{2,1,0:T(8,128)} %bitcast.9), calls=%async_computation.2 | async-start | bytes 983040 | tf_op jit(solution)/shard_map/all_to_all | solution.py:549
  37.7 0.0 copy-start.1
  37.7 0.0 copy-start.2
  37.7 0.7 copy-done.1
  38.4 0.0 copy-done.2
  38.4 14.1 %while.40 = (s32[1]{0:T(128)}, f32[3,2048]{1,0:T(4,128)S(1)}, s32[2176]{0:T(1024)}, f32[16,128]{1,0:T(8,128)S(1)}, f32[152,128]{1,0:T(8,128)S(1)}, /*index=5*/f3...) while((s32[1]{0:T(128)}, f32[3,2048]{1,0:T(4,128)S(1)}, ...), condition=%wide.region_4.5_spmd, body=%wide.region_1.4_spmd.sunk | while | flops 4000000000 | bytes 4098126 | solution.py:550
  39.1 1.2 %collective-permute-start.7 = (f32[16,128]{1,0:T(8,128)S(1)}, f32[16,128]{1,0:T(8,128)S(1)}, u32[]{:S(2)}, u32[]{:S(2)}) collective-permute-start(f32[16,128]{1,0:T(8,128)S(1)} %copy.28.m0), channel_id=1, source_target_pairs={{0,64},{64,128},{128,192},{192,0},{1,65},{65,129},{129,193},{193,1... | collective-permute-start | bytes 24584 | tf_op jit(solution)/shard_map/while/body/ppermute | solution.py:522
  40.3 2.8 %collective-permute-start.8 = (f32[16,128]{1,0:T(8,128)S(1)}, f32[16,128]{1,0:T(8,128)S(1)}, u32[]{:S(2)}, u32[]{:S(2)}) collective-permute-start(f32[16,128]{1,0:T(8,128)S(1)} %copy.28.m0), channel_id=1, source_target_pairs={{0,128},{64,192},{128,0},{192,64},{1,129},{65,193},{129,1},{193,65... | collective-permute-start | bytes 24584 | tf_op jit(solution)/shard_map/while/body/ppermute | solution.py:522
  43.1 1.2 %collective-permute-start.9 = (f32[16,128]{1,0:T(8,128)S(1)}, f32[16,128]{1,0:T(8,128)S(1)}, u32[]{:S(2)}, u32[]{:S(2)}) collective-permute-start(f32[16,128]{1,0:T(8,128)S(1)} %copy.28.m0), channel_id=1, source_target_pairs={{0,192},{64,0},{128,64},{192,128},{1,193},{65,1},{129,65},{193,129... | collective-permute-start | bytes 24584 | tf_op jit(solution)/shard_map/while/body/ppermute | solution.py:522
  44.3 2.7 %row_pairs.7 = (f32[3,2048]{1,0:T(4,128)S(1)}, s32[1]{0:T(128)}, s32[2176]{0:T(1024)}) custom-call(f32[152,128]{1,0:T(8,128)S(1)} %get-tuple-element.679.own, f32[64,128]{1,0:T(8,128)S(1)} %get-tuple-element.680.rec_t, f32[608,128]{1,0:T(8,128)S(1)} %get-tuple-element.681.rec_x, f32[3,2048]{1,0:T(4,128)S(1)} %get-tuple-element.652.so_far), custom_call_target="tpu_custom_call" | custom-call | flops 4000000000 | bytes 1 | tf_op jit(solution)/shard_map/while/body/row_pairs/pallas_call | solution.py:523
  47.7 2.8 %far.7 = f32[3,2048]{1,0:T(4,128)S(1)} custom-call(f32[152,128]{1,0:T(8,128)S(1)} %get-tuple-element.679.own, f32[16,128]{1,0:T(8,128)S(1)} %copy.28.m0, f32[16,128]{1,0:T(8,128)S(1)} %collective-permute-done.7.m1, f32[16,128]{1,0:T(8,128)S(1)} %collective-permute-done.8.m2, f32[16,128]{1,0:T(8,128)S(1)} %collective-permute-done.9.m3, ...), custom_call_target="tpu_custom_call" | custom-call | flops 1 | bytes 1 | tf_op jit(solution)/shard_map/while/body/far/pallas_call | solution.py:533
  50.5 0.7 while.41
  52.5 2.5 %all-to-all-done.2 = f32[8,120,128]{2,1,0:T(8,128)S(1)} async-done(((f32[8,120,128]{2,1,0:T(8,128)}), f32[8,120,128]{2,1,0:T(8,128)S(1)}, u32[]{:S(2)}, u32[]{:S(2)}) %all-to-all-start.2) | async-done | bytes 491552 | tf_op jit(solution)/shard_map/all_to_all | solution.py:549
  55.0 3.9 %near.7 = (f32[3,2048]{1,0:T(4,128)}, f32[256,128]{1,0:T(8,128)S(1)}) custom-call(f32[960,128]{1,0:T(8,128)S(1)} %bitcast.24, s32[2176]{0:T(1024)} %get-tuple-element.726, f32[152,128]{1,0:T(8,128)S(1)} %get-tuple-element.728, f32[3,2048]{1,0:T(4,128)S(1)} %get-tuple-element.725, f32[1,2048]{1,0:T(1,128)S(1)} %get-tuple-element.733), custom_call_target="tpu_custom_call" | custom-call | tf_op jit(solution)/shard_map/near/pallas_call | solution.py:497
  58.9 19.3 %all_to_all.21 = f32[256,1,128]{2,1,0:T(1,128)S(1)} all-to-all(f32[256,1,128]{2,1,0:T(1,128)S(1)} %bitcast.27), channel_id=1, replica_groups=mesh['y'=4,'c'=2,'z'=8,'x'=4] {'y','c','z','x'}, dimensions={0} | all-to-all | bytes 262144 | tf_op jit(solution)/shard_map/all_to_all | solution.py:552
  78.3 0.7 step.1
  (9 shorter events, 0.0 us)
Async XLA Ops:
  2.4 10.6 %all-to-all-start = ((f32[4,152,128]{2,1,0:T(8,128)}), f32[4,152,128]{2,1,0:T(8,128)S(1)}, u32[]{:S(2)}, u32[]{:S(2)}) async-start(f32[4,152,128]{2,1,0:T(8,128)} %bitcast.37), calls=%async_computation | async-start | bytes 622592 | tf_op jit(solution)/shard_map/all_to_all | solution.py:438
  28.2 9.5 %collective-permute-start.10 = (f32[8,128]{1,0:T(8,128)S(1)}, f32[8,128]{1,0:T(8,128)S(1)}, u32[]{:S(2)}, u32[]{:S(2)}) collective-permute-start(f32[8,128]{1,0:T(8,128)S(1)} %reduce_sum.9), channel_id=1, source_target_pairs={{0,32},{32,0},{1,33},{33,1},{2,34},{34,2},{3,35},{35,3},{4,36},{36... | collective-permute-start | bytes 12296 | tf_op jit(solution)/shard_map/ppermute | solution.py:546
  34.2 20.8 %all-to-all-start.2 = ((f32[8,120,128]{2,1,0:T(8,128)}), f32[8,120,128]{2,1,0:T(8,128)S(1)}, u32[]{:S(2)}, u32[]{:S(2)}) async-start(f32[8,120,128]{2,1,0:T(8,128)} %bitcast.9), calls=%async_computation.2 | async-start | bytes 983040 | tf_op jit(solution)/shard_map/all_to_all | solution.py:549
  37.7 0.7 copy-start.1
  37.7 0.7 copy-start.2
  39.1 8.5 %collective-permute-start.7 = (f32[16,128]{1,0:T(8,128)S(1)}, f32[16,128]{1,0:T(8,128)S(1)}, u32[]{:S(2)}, u32[]{:S(2)}) collective-permute-start(f32[16,128]{1,0:T(8,128)S(1)} %copy.28.m0), channel_id=1, source_target_pairs={{0,64},{64,128},{128,192},{192,0},{1,65},{65,129},{129,193},{193,1... | collective-permute-start | bytes 24584 | tf_op jit(solution)/shard_map/while/body/ppermute | solution.py:522
  40.3 7.3 %collective-permute-start.8 = (f32[16,128]{1,0:T(8,128)S(1)}, f32[16,128]{1,0:T(8,128)S(1)}, u32[]{:S(2)}, u32[]{:S(2)}) collective-permute-start(f32[16,128]{1,0:T(8,128)S(1)} %copy.28.m0), channel_id=1, source_target_pairs={{0,128},{64,192},{128,0},{192,64},{1,129},{65,193},{129,1},{193,65... | collective-permute-start | bytes 24584 | tf_op jit(solution)/shard_map/while/body/ppermute | solution.py:522
  43.1 4.5 %collective-permute-start.9 = (f32[16,128]{1,0:T(8,128)S(1)}, f32[16,128]{1,0:T(8,128)S(1)}, u32[]{:S(2)}, u32[]{:S(2)}) collective-permute-start(f32[16,128]{1,0:T(8,128)S(1)} %copy.28.m0), channel_id=1, source_target_pairs={{0,192},{64,0},{128,64},{192,128},{1,193},{65,1},{129,65},{193,129... | collective-permute-start | bytes 24584 | tf_op jit(solution)/shard_map/while/body/ppermute | solution.py:522
  58.9 19.3 %copy-start = (f32[3,2048]{1,0:T(4,128)S(1)}, f32[3,2048]{1,0:T(4,128)}, u32[]{:S(2)}) copy-start(f32[3,2048]{1,0:T(4,128)} %get-tuple-element.383.forces) | copy-start | bytes 73732
